TPU v7x, 128 devices: a whole 4x4x4 slice. The times are simulated.
128 devices in a mesh: group: 2 (over z_hi), ctx: 8 (over z_lo, x), tp: 8 (over y, core).
Axes of the slice: x: 4, y: 4, z: 4 (z_hi: 2, z_lo: 2; z = z_hi * 2 + z_lo), core: 2. Of those that a mesh axis runs over, the one named last changes fastest.
Arguments:
- hidden_in: bfloat16 [2, 512, 16384], P('group', None, 'ctx'), may hold values from -6 to 6
- w_query: bfloat16 [16384, 8192], P('ctx', 'tp'), may hold values from -0.046875 to 0.046875
- w_keyval: bfloat16 [16384, 2048], P('ctx', 'tp'), may hold values from -0.046875 to 0.046875
- w_out: bfloat16 [8192, 16384], P('tp', 'ctx'), may hold values from -0.0625 to 0.0625
- kv_pages: bfloat16 [2, 512, 64, 2048], P('group', 'ctx', None, 'tp'), may hold values from -500 to 500
- page_slot: int32 [512], replicated, may hold values from 0 to 511, as said below
- lengths: int32 [512], P('ctx'), may hold values from 1 to 64, 16384 in all
Outputs:
- attn_out: bfloat16 [2, 512, 16384], P('group', 'tp', 'ctx')
- page_pools: bfloat16 [2, 512, 64, 2048], P('group', 'ctx', None, 'tp')
Inputs may be any that keep to these rules, and one draw needn't show every extreme that they name: page_slot is a permutation of the 512 pool slots; each aligned block of 64 pages sends exactly 8 pages into each aligned block of 64 slots. `lengths`: positions of a decode row at or beyond its length are not part of its context.
All inputs are finite; a program needn't handle non-finite values. No bound on the sum of `lengths` on one device may be relied on, other than what follows from the above.
Results may differ from a plain program's by a relative error of at most 0.019.
The roundings to bfloat16 on the way count: a program that leaves them out, or rounds other values in their place, can miss the bound.
Values may be sent and summed in bfloat16 or wider, within the bound.
No kernel may reach another device: no remote copies, remote signals or barrier semaphores. Data moves between devices by JAX's collectives and lax.ppermute only.
A program may use at most 128 MiB of HBM per device.

v0:
```python
import jax
import jax.numpy as jnp
from jax import lax
from jax.sharding import PartitionSpec as P

HD = 128


def joined(value, axis, combine):
    everything = jax.tree.map(lambda part: lax.all_gather(part, axis), value)
    initial = jax.tree.map(lambda part: part[0], everything)

    def turn(k, so_far):
        return combine(so_far, jax.tree.map(lambda part: part[k], everything))

    return lax.fori_loop(1, lax.axis_size(axis), turn, initial)


def attend_block(carried, queries, key_rows, value_rows, score_scale):
    running_max, running_sum, running_acc = carried
    scores = (
        jnp.einsum("rkgd,skd->rkgs", queries, key_rows, preferred_element_type=jnp.float32)
        * score_scale
    )
    new_max = jnp.maximum(running_max, jnp.max(scores, axis=3))
    faded = jnp.exp(running_max - new_max)
    weights = jnp.exp(scores - new_max[..., None])
    new_sum = running_sum * faded + jnp.sum(weights, axis=3)
    new_acc = running_acc * faded[..., None] + jnp.einsum(
        "rkgs,skd->rkgd",
        weights.astype(jnp.bfloat16),
        value_rows,
        preferred_element_type=jnp.float32,
    )
    return (new_max, new_sum, new_acc)


def combine_states(state_one, state_two):
    joint_max = jnp.maximum(state_one[0], state_two[0])
    fade_one = jnp.exp(state_one[0] - joint_max)
    fade_two = jnp.exp(state_two[0] - joint_max)
    joint_sum = state_one[1] * fade_one + state_two[1] * fade_two
    joint_acc = state_one[2] * fade_one[..., None] + state_two[2] * fade_two[..., None]
    return (joint_max, joint_sum, joint_acc)


def attend_pages(carried, queries, pages, score_scale, block_keys):
    kv_heads = queries.shape[1]
    positions = pages.shape[0] * pages.shape[1]
    head_size = pages.shape[2] // (2 * kv_heads)
    grouped = pages.reshape(positions // block_keys, block_keys, kv_heads, 2, head_size)

    def one_block(inner_state, key_block):
        return (
            attend_block(inner_state, queries, key_block[:, :, 0], key_block[:, :, 1], score_scale),
            None,
        )

    result, unused = lax.scan(one_block, carried, grouped)
    return result


def recent_state(queries, new_keys, new_values, first_row, score_scale):
    scores = (
        jnp.einsum("rkgd,jkd->rkgj", queries, new_keys, preferred_element_type=jnp.float32)
        * score_scale
    )
    query_pos = first_row + jnp.arange(queries.shape[0], dtype=jnp.int32)
    key_pos = jnp.arange(new_keys.shape[0], dtype=jnp.int32)
    allowed = key_pos[None, :] <= query_pos[:, None]
    scores = jnp.where(allowed[:, None, None, :], scores, -jnp.inf)
    row_max = jnp.max(scores, axis=3)
    weights = jnp.exp(scores - row_max[..., None])
    mixture = jnp.einsum(
        "rkgj,jkd->rkgd",
        weights.astype(jnp.bfloat16),
        new_values,
        preferred_element_type=jnp.float32,
    )
    return (row_max, jnp.sum(weights, axis=3), mixture)


def decode_state(queries, own_key, own_value, resident, relaid, lengths, score_scale):
    live_mask = jnp.arange(resident.shape[1], dtype=jnp.int32)[None, :] < lengths[:, None]
    resident_scores = (
        jnp.einsum(
            "rkgd,rskd->rkgs", queries, resident[:, :, :, 0], preferred_element_type=jnp.float32
        )
        * score_scale
    )
    resident_scores = jnp.where(live_mask[:, None, None, :], resident_scores, -jnp.inf)
    relaid_scores = (
        jnp.einsum(
            "rkgd,rskd->rkgs", queries, relaid[:, :, :, 0], preferred_element_type=jnp.float32
        )
        * score_scale
    )
    own_scores = (
        jnp.einsum("rkgd,rkd->rkg", queries, own_key, preferred_element_type=jnp.float32)
        * score_scale
    )
    largest = jnp.maximum(
        jnp.maximum(jnp.max(resident_scores, axis=3), jnp.max(relaid_scores, axis=3)), own_scores
    )
    resident_weights = jnp.exp(resident_scores - largest[..., None])
    relaid_weights = jnp.exp(relaid_scores - largest[..., None])
    own_weights = jnp.exp(own_scores - largest)
    totals = jnp.sum(resident_weights, axis=3) + jnp.sum(relaid_weights, axis=3) + own_weights
    mixture = jnp.einsum(
        "rkgs,rskd->rkgd",
        resident_weights.astype(jnp.bfloat16),
        resident[:, :, :, 1],
        preferred_element_type=jnp.float32,
    )
    mixture = mixture + jnp.einsum(
        "rkgs,rskd->rkgd",
        relaid_weights.astype(jnp.bfloat16),
        relaid[:, :, :, 1],
        preferred_element_type=jnp.float32,
    )
    mixture = mixture + jnp.einsum(
        "rkg,rkd->rkgd",
        own_weights.astype(jnp.bfloat16),
        own_value,
        preferred_element_type=jnp.float32,
    )
    return mixture / totals[..., None]


def shards(hidden_in, w_query, w_keyval, w_out, kv_pages, page_slot, lengths):
    ctx_count = lax.axis_size("ctx")
    ctx_index = lax.axis_index("ctx")
    is_prefill = lax.axis_index("group") == 0
    tokens = hidden_in[0]
    rows_all = tokens.shape[0]
    row_dev = rows_all // ctx_count
    query_width = w_query.shape[1]
    kv_heads = w_keyval.shape[1] // (2 * HD)
    q_share = query_width // HD // kv_heads
    score_scale = HD ** (-0.5)
    own_pages = kv_pages[0]
    pages_dev = own_pages.shape[0]
    page_len = own_pages.shape[1]
    pair_width = own_pages.shape[2]
    first_row = ctx_index * row_dev
    qkv_all = lax.psum(
        jnp.concatenate(
            [
                jnp.dot(tokens, w_query, preferred_element_type=jnp.float32),
                jnp.dot(tokens, w_keyval, preferred_element_type=jnp.float32),
            ],
            axis=1,
        ),
        "ctx",
    ).astype(jnp.bfloat16)
    qkv_mine = lax.dynamic_slice_in_dim(qkv_all, first_row, row_dev, 0)

    def split_rows(qkv_rows):
        row_total = qkv_rows.shape[0]
        queries = qkv_rows[:, :query_width].reshape(row_total, kv_heads, q_share, HD)
        kv_pairs = qkv_rows[:, query_width:].reshape(row_total, kv_heads, 2, HD)
        return (queries, kv_pairs[:, :, 0], kv_pairs[:, :, 1])

    all_queries, new_keys, new_values = split_rows(qkv_all)
    my_queries, my_keys, my_values = split_rows(qkv_mine)
    self_state = recent_state(my_queries, new_keys, new_values, first_row, score_scale)
    stat_shape = all_queries.shape[:3]

    def context_scan(unused):
        start_state = (
            jnp.full(stat_shape, -jnp.inf, jnp.float32),
            jnp.zeros(stat_shape, jnp.float32),
            jnp.zeros(all_queries.shape, jnp.float32),
        )
        return attend_pages(start_state, all_queries, own_pages, score_scale, 1024)

    def context_skip(unused):
        zero_stats = jnp.zeros(stat_shape, jnp.float32)
        return (zero_stats, zero_stats, jnp.zeros(all_queries.shape, jnp.float32))

    partial_state = lax.cond(is_prefill, context_scan, context_skip, 0)
    merged = joined(partial_state, "ctx", combine_states)
    mine_state = tuple(
        (lax.dynamic_slice_in_dim(member, first_row, row_dev, 0) for member in merged)
    )
    final_state = combine_states(mine_state, self_state)
    slot_table = page_slot.reshape(ctx_count, pages_dev)
    per_peer = pages_dev // ctx_count
    my_slots = lax.dynamic_index_in_dim(slot_table, ctx_index, 0, keepdims=False)
    send_order = jnp.argsort(my_slots // pages_dev, stable=True)
    outgoing = jnp.take(own_pages, send_order, axis=0).reshape(
        ctx_count, per_peer, page_len, pair_width
    )
    filled = jnp.where(is_prefill, outgoing, jnp.zeros_like(outgoing))
    buffer = jnp.concatenate([jnp.zeros_like(outgoing), filled], axis=0)
    incoming = lax.all_to_all(buffer, ("group", "ctx"), split_axis=0, concat_axis=0, tiled=True)[
        :ctx_count
    ]
    peer_rank = jnp.argsort(
        (slot_table // pages_dev != ctx_index).astype(jnp.int32), axis=1, stable=True
    )[:, :per_peer]
    arrival_slots = jnp.take_along_axis(slot_table, peer_rank, axis=1) % pages_dev
    relaid_pool = (
        jnp.zeros_like(own_pages)
        .at[arrival_slots.reshape(-1)]
        .set(incoming.reshape(ctx_count * per_peer, page_len, pair_width))
    )
    pool_block = jnp.where(is_prefill, own_pages, relaid_pool)
    res_len = pages_dev * page_len // row_dev
    resident = own_pages.reshape(row_dev, res_len, kv_heads, 2, HD)
    relaid = relaid_pool.reshape(row_dev, res_len, kv_heads, 2, HD)

    def finish_prefill(unused):
        return (
            (final_state[2] / final_state[1][..., None])
            .astype(jnp.bfloat16)
            .reshape(row_dev, query_width)
        )

    def finish_decode(unused):
        mixture = decode_state(
            my_queries, my_keys, my_values, resident, relaid, lengths, score_scale
        )
        return mixture.astype(jnp.bfloat16).reshape(row_dev, query_width)

    head_block = lax.cond(is_prefill, finish_prefill, finish_decode, 0)
    gathered = lax.all_gather(head_block, "ctx", axis=0, tiled=True)
    summed = lax.psum_scatter(
        jnp.dot(gathered, w_out, preferred_element_type=jnp.float32).astype(jnp.bfloat16),
        "tp",
        scatter_dimension=0,
        tiled=True,
    )
    return (summed[None], pool_block[None])


def solution(mesh):
    placed = (
        P("group", None, "ctx"),
        P("ctx", "tp"),
        P("ctx", "tp"),
        P("tp", "ctx"),
        P("group", "ctx", None, "tp"),
        P(),
        P("ctx"),
    )
    return jax.shard_map(
        shards,
        mesh=mesh,
        in_specs=placed,
        out_specs=(P("group", "tp", "ctx"), P("group", "ctx", None, "tp")),
        check_vma=False,
    )
```

profile of v0, /device:TPU:1, one launch (start us, length us, event | category | flops | bytes accessed | tf_op | source)
XLA Modules:
  0.0 596.2 jit_solution(14386583693871428924)
XLA Ops:
  7.2 1.5 copy-done
  8.8 4.6 fusion.46
  14.1 1.7 pad_maximum_fusion
  15.8 68.2 %all-reduce.2 = bf16[512,1280]{1,0:T(8,128)(2,1)S(1)} all-reduce(f32[512,1280]{1,0:T(8,128)} %pad_maximum_fusion), channel_id=1, replica_groups=mesh['group'=2,'ctx'=8,'tp'=8] {'ctx'}, use_global_device_ids=true, to_apply=%region_0.0 | all-reduce | flops 655360 | bytes 3932160 | tf_op jit(solution)/shard_map/psum | solution.py:146
  84.1 132.5 %conditional.2 = (f32[512,1,8]{0,2,1:T(8,128)}, f32[512,1,8]{0,2,1:T(8,128)}, f32[512,1,8,128]{0,3,2,1:T(8,128)}) conditional(s32[]{:T(128)} %convert_element_type.42, () %tuple.60, (bf16[1,64,64,256]{3,2,1,0:T(8,128)(2,1)}, bf16[512,1280]{1,0:T(8,128)(2,1)S(1)}) %tuple.61), branch_computations={%region_4.5_spmd, %region_5.10_spmd} | conditional | flops 2182635520 | bytes 69468352 | solution.py:181
  84.9 1.0 slice.90
  86.0 1.6 copy.62
  87.6 4.0 reshape_squeeze.4
  91.6 124.9 %while.33 = (s32[]{:T(128)}, f32[512,1,8]{0,2,1:T(8,128)}, f32[512,1,8]{0,2,1:T(8,128)}, f32[512,1,8,128]{0,3,2,1:T(8,128)}, bf16[4,1024,1,2,128]{4,3,1,0,2:T(2,...) while((s32[]{:T(128)}, f32[512,1,8]{0,2,1:T(8,128)}, ...), condition=%wide.region_9.9_spmd.clone, body=%wide.region_6.8_spmd.clone.sunk | while | flops 2182635520 | bytes 58458208 | solution.py:59
  91.6 1.4 constant_dynamic-slice_fusion.3
  93.1 8.1 %bitcast_reduce_fusion.2 = (f32[512,8]{0,1:T(8,128)S(1)}, f32[1024,512,8]{1,0,2:T(8,128)}) fusion(bf16[512,1,8,128]{3,0,2,1:T(8,128)(2,1)S(1)} %get-tuple-element.645, bf16[1024,1,2,128]{3,0,2,1:T(8,128)(2,1)S(1)} %bitcast.245), kind=kOutput, calls=%fused_computation.59.clone.1 | convolution fusion | flops 1082126336 | bytes 18104320 | tf_op jit(solution)/shard_map/cond/branch_1_fun/while/body/eval_jaxpr/rkgd,skd->rkgs/dot_general | solution.py:22
  101.2 10.4 %bitcast_add_fusion.5 = f32[512,1,8,128]{0,3,2,1:T(8,128)} fusion(f32[512,1,8,128]{0,3,2,1:T(8,128)} %get-tuple-element.635, f32[1024,512,8]{1,0,2:T(8,128)} %get-tuple-element.622, f32[512,8]{0,1:T(8,128)S(1)} %bitcast.248, f32[512,8]{0,1:T(8,128)S(1)} %get-tuple-element.623, pred[]{:T(512)S(6)} %compare.23, bf16[1024,1,2,128]{3,0,2,1:T(8,128)(2,1)S(1)} %bitcast.246), kind=kOutput, calls=%fused_computation.67.clone.1 | convolution fusion | flops 1087897600 | bytes 21266432 | tf_op jit(solution)/shard_map/cond/branch_1_fun/while/body/eval_jaxpr/rkgs,skd->rkgd/dot_general | solution.py:29
  111.6 8.5 %fusion.87 = f32[512,8]{0,1:T(8,128)S(1)} fusion(f32[1024,512,8]{1,0,2:T(8,128)} %get-tuple-element.622, f32[512,8]{0,1:T(8,128)S(1)} %bitcast.249), kind=kLoop, calls=%fused_computation.62.clone.1 | loop fusion | flops 12578816 | bytes 16809984 | tf_op jit(solution)/shard_map/cond/branch_1_fun/while/body/eval_jaxpr/reduce_sum | solution.py:28
  121.3 1.4 constant_dynamic-slice_fusion.3
  122.8 8.1 %bitcast_reduce_fusion.2 = (f32[512,8]{0,1:T(8,128)S(1)}, f32[1024,512,8]{1,0,2:T(8,128)}) fusion(bf16[512,1,8,128]{3,0,2,1:T(8,128)(2,1)S(1)} %get-tuple-element.645, bf16[1024,1,2,128]{3,0,2,1:T(8,128)(2,1)S(1)} %bitcast.245), kind=kOutput, calls=%fused_computation.59.clone.1 | convolution fusion | flops 1082126336 | bytes 18104320 | tf_op jit(solution)/shard_map/cond/branch_1_fun/while/body/eval_jaxpr/rkgd,skd->rkgs/dot_general | solution.py:22
  131.6 11.0 %bitcast_add_fusion.5 = f32[512,1,8,128]{0,3,2,1:T(8,128)} fusion(f32[512,1,8,128]{0,3,2,1:T(8,128)} %get-tuple-element.635, f32[1024,512,8]{1,0,2:T(8,128)} %get-tuple-element.622, f32[512,8]{0,1:T(8,128)S(1)} %bitcast.248, f32[512,8]{0,1:T(8,128)S(1)} %get-tuple-element.623, pred[]{:T(512)S(6)} %compare.23, bf16[1024,1,2,128]{3,0,2,1:T(8,128)(2,1)S(1)} %bitcast.246), kind=kOutput, calls=%fused_computation.67.clone.1 | convolution fusion | flops 1087897600 | bytes 21266432 | tf_op jit(solution)/shard_map/cond/branch_1_fun/while/body/eval_jaxpr/rkgs,skd->rkgd/dot_general | solution.py:29
  142.6 8.5 %fusion.87 = f32[512,8]{0,1:T(8,128)S(1)} fusion(f32[1024,512,8]{1,0,2:T(8,128)} %get-tuple-element.622, f32[512,8]{0,1:T(8,128)S(1)} %bitcast.249), kind=kLoop, calls=%fused_computation.62.clone.1 | loop fusion | flops 12578816 | bytes 16809984 | tf_op jit(solution)/shard_map/cond/branch_1_fun/while/body/eval_jaxpr/reduce_sum | solution.py:28
  151.1 1.4 bitcast_add_fusion.4
  153.0 1.4 constant_dynamic-slice_fusion.3
  154.5 8.1 %bitcast_reduce_fusion.2 = (f32[512,8]{0,1:T(8,128)S(1)}, f32[1024,512,8]{1,0,2:T(8,128)}) fusion(bf16[512,1,8,128]{3,0,2,1:T(8,128)(2,1)S(1)} %get-tuple-element.645, bf16[1024,1,2,128]{3,0,2,1:T(8,128)(2,1)S(1)} %bitcast.245), kind=kOutput, calls=%fused_computation.59.clone.1 | convolution fusion | flops 1082126336 | bytes 18104320 | tf_op jit(solution)/shard_map/cond/branch_1_fun/while/body/eval_jaxpr/rkgd,skd->rkgs/dot_general | solution.py:22
  163.3 11.0 %bitcast_add_fusion.5 = f32[512,1,8,128]{0,3,2,1:T(8,128)} fusion(f32[512,1,8,128]{0,3,2,1:T(8,128)} %get-tuple-element.635, f32[1024,512,8]{1,0,2:T(8,128)} %get-tuple-element.622, f32[512,8]{0,1:T(8,128)S(1)} %bitcast.248, f32[512,8]{0,1:T(8,128)S(1)} %get-tuple-element.623, pred[]{:T(512)S(6)} %compare.23, bf16[1024,1,2,128]{3,0,2,1:T(8,128)(2,1)S(1)} %bitcast.246), kind=kOutput, calls=%fused_computation.67.clone.1 | convolution fusion | flops 1087897600 | bytes 21266432 | tf_op jit(solution)/shard_map/cond/branch_1_fun/while/body/eval_jaxpr/rkgs,skd->rkgd/dot_general | solution.py:29
  174.3 8.5 %fusion.87 = f32[512,8]{0,1:T(8,128)S(1)} fusion(f32[1024,512,8]{1,0,2:T(8,128)} %get-tuple-element.622, f32[512,8]{0,1:T(8,128)S(1)} %bitcast.249), kind=kLoop, calls=%fused_computation.62.clone.1 | loop fusion | flops 12578816 | bytes 16809984 | tf_op jit(solution)/shard_map/cond/branch_1_fun/while/body/eval_jaxpr/reduce_sum | solution.py:28
  182.8 1.4 bitcast_add_fusion.4
  184.8 1.4 constant_dynamic-slice_fusion.3
  186.3 8.1 %bitcast_reduce_fusion.2 = (f32[512,8]{0,1:T(8,128)S(1)}, f32[1024,512,8]{1,0,2:T(8,128)}) fusion(bf16[512,1,8,128]{3,0,2,1:T(8,128)(2,1)S(1)} %get-tuple-element.645, bf16[1024,1,2,128]{3,0,2,1:T(8,128)(2,1)S(1)} %bitcast.245), kind=kOutput, calls=%fused_computation.59.clone.1 | convolution fusion | flops 1082126336 | bytes 18104320 | tf_op jit(solution)/shard_map/cond/branch_1_fun/while/body/eval_jaxpr/rkgd,skd->rkgs/dot_general | solution.py:22
  195.1 11.0 %bitcast_add_fusion.5 = f32[512,1,8,128]{0,3,2,1:T(8,128)} fusion(f32[512,1,8,128]{0,3,2,1:T(8,128)} %get-tuple-element.635, f32[1024,512,8]{1,0,2:T(8,128)} %get-tuple-element.622, f32[512,8]{0,1:T(8,128)S(1)} %bitcast.248, f32[512,8]{0,1:T(8,128)S(1)} %get-tuple-element.623, pred[]{:T(512)S(6)} %compare.23, bf16[1024,1,2,128]{3,0,2,1:T(8,128)(2,1)S(1)} %bitcast.246), kind=kOutput, calls=%fused_computation.67.clone.1 | convolution fusion | flops 1087897600 | bytes 21266432 | tf_op jit(solution)/shard_map/cond/branch_1_fun/while/body/eval_jaxpr/rkgs,skd->rkgd/dot_general | solution.py:29
  206.1 8.5 %fusion.87 = f32[512,8]{0,1:T(8,128)S(1)} fusion(f32[1024,512,8]{1,0,2:T(8,128)} %get-tuple-element.622, f32[512,8]{0,1:T(8,128)S(1)} %bitcast.249), kind=kLoop, calls=%fused_computation.62.clone.1 | loop fusion | flops 12578816 | bytes 16809984 | tf_op jit(solution)/shard_map/cond/branch_1_fun/while/body/eval_jaxpr/reduce_sum | solution.py:28
  214.6 1.4 bitcast_add_fusion.4
  216.5 3.0 copy.69
  220.3 2.0 sort.35
  222.4 3.6 gather_fusion
  226.0 1.9 select_select_fusion
  227.9 2.5 concatenate.7
  230.4 4.5 all-to-all-start
  235.1 108.2 %all-gather = f32[4096,1,8]{0,2,1:T(8,128)S(1)} all-gather(f32[512,1,8]{0,2,1:T(8,128)} %get-tuple-element.375), channel_id=2, replica_groups=mesh['group'=2,'ctx'=8,'tp'=8] {'ctx'}, dimensions={0}, use_global_device_ids=true | all-gather | bytes 147456 | tf_op jit(solution)/shard_map/all_gather | solution.py:10
  343.3 25.9 %all-gather.1 = f32[4096,1,8]{0,2,1:T(8,128)S(1)} all-gather(f32[512,1,8]{0,2,1:T(8,128)} %get-tuple-element.376), channel_id=3, replica_groups=mesh['group'=2,'ctx'=8,'tp'=8] {'ctx'}, dimensions={0}, use_global_device_ids=true | all-gather | bytes 147456 | tf_op jit(solution)/shard_map/all_gather | solution.py:10
  369.3 1.0 sort.34
  373.7 3.2 slice.91
  377.1 6.6 %scatter_fusion = bf16[64,64,256]{2,1,0:T(8,128)(2,1)S(1)} fusion(bf16[64,64,256]{2,1,0:T(8,128)(2,1)S(1)} %broadcast_in_dim.73, s32[64]{0:T(128)S(1)} %fusion.59, bf16[64,64,256]{2,1,0:T(8,128)(2,1)} %bitcast.251), kind=kCustom, calls=%fused_computation.2 | custom fusion | bytes 6291712 | tf_op jit(solution)/shard_map/scatter | solution.py:206
  383.8 1.3 copy-done.2
  385.1 62.8 %all-gather.8.cloned.1.call-done = f32[4096,1,8,128]{3,2,1,0:T(8,128)} async-done(((f32[512,1,8,128]{3,2,1,0:T(8,128)}), f32[4096,1,8,128]{3,2,1,0:T(8,128)}) %all-gather.8.cloned.1.call-update) | async-done | bytes 16777232 | tf_op jit(solution)/shard_map/all_gather | solution.py:10
  447.9 1.7 slice.94
  449.6 39.3 %while.34 = (s32[]{:T(128)}, f32[512,1,8]{0,2,1:T(8,128)S(1)}, f32[512,1,8]{0,2,1:T(8,128)S(1)}, f32[512,1,8,128]{3,2,1,0:T(8,128)S(1)}, f32[8,512,1,8]{1,3,2,0:...) while((s32[]{:T(128)}, f32[512,1,8]{0,2,1:T(8,128)S(1)}, ...), condition=%wide.region_11.12_spmd, body=%wide.region_10.11_spmd.sunk | while | flops 1601541 | bytes 6602907 | solution.py:16
  449.7 0.8 fusion.82
  450.4 0.8 fusion.83
  451.5 3.8 fusion.84
  456.0 0.8 fusion.83
  457.1 3.8 fusion.84
  461.7 0.8 fusion.83
  462.7 3.8 fusion.84
  467.3 0.8 fusion.83
  468.3 3.8 fusion.84
  472.9 0.8 fusion.83
  473.9 3.8 fusion.84
  478.5 0.8 fusion.83
  479.5 3.8 fusion.84
  484.1 0.8 fusion.83
  485.1 3.8 fusion.84
  489.0 2.2 conditional.3
  489.3 1.4 reduce_sum.38
  491.9 56.6 %all-gather.6.cloned.1.call-done = bf16[512,1024]{1,0:T(8,128)(2,1)} async-done(((bf16[64,1024]{1,0:T(8,128)(2,1)}), bf16[512,1024]{1,0:T(8,128)(2,1)}) %all-gather.6.cloned.1.call-update) | async-done | bytes 1048592 | tf_op jit(solution)/shard_map/all_gather | solution.py:227
  548.5 6.2 %convolution_convert_fusion = bf16[512,2048]{1,0:T(8,128)(2,1)} fusion(bf16[512,1024]{1,0:T(8,128)(2,1)} %all-gather.6.cloned.1.call-done, bf16[1024,2048]{1,0:T(8,128)(2,1)} %param.18), kind=kOutput, calls=%fused_computation.81 | convolution fusion | flops 2148532224 | bytes 7340032 | tf_op jit(solution)/shard_map/dot_general | solution.py:229
  554.8 3.3 select_bitcast_fusion
  558.1 31.6 %reduce-scatter.2.cloned.1.call-done = bf16[64,2048]{1,0:T(8,128)(2,1)} async-done(((bf16[512,2048]{1,0:T(8,128)(2,1)}), bf16[64,2048]{1,0:T(8,128)(2,1)}) %reduce-scatter.2.cloned.1.call-update) | async-done | bytes 262160 | tf_op jit(solution)/shard_map/reduce_scatter | solution.py:228
  (114 shorter events, 19.2 us)
Async XLA Ops:
  7.2 1.6 copy-start
  7.2 440.7 %all-gather.8.cloned.1.call-start = ((), (), s32[]{:S(2)}) async-start(), calls=%async_computation.4 | async-start | bytes 18874368 | tf_op jit(solution)/shard_map/all_gather | solution.py:10
  8.8 4.6 copy-start.12
  219.5 0.7 copy-start.10
  230.4 143.2 %all-to-all-start = ((bf16[16,8,64,256]{3,2,1,0:T(8,128)(2,1)}), bf16[16,8,64,256]{3,2,1,0:T(8,128)(2,1)}, u32[]{:S(2)}, u32[]{:S(2)}) async-start(bf16[16,8,64,256]{3,2,1,0:T(8,128)(2,1)} %concatenate.7), calls=%async_computation | async-start | bytes 8388608 | tf_op jit(solution)/shard_map/all_to_all | solution.py:196
  234.9 313.6 %all-gather.6.cloned.1.call-start = ((), (), s32[]{:S(2)}) async-start(), calls=%async_computation.2 | async-start | bytes 1179648 | tf_op jit(solution)/shard_map/all_gather | solution.py:227
  343.3 27.1 %copy-start.6 = (f32[4096,1,8]{0,2,1:T(8,128)}, f32[4096,1,8]{0,2,1:T(8,128)S(1)}, u32[]{:S(2)}) copy-start(f32[4096,1,8]{0,2,1:T(8,128)S(1)} %all-gather) | copy-start | bytes 393220
  369.2 2.0 copy-start.9
  373.3 3.5 copy-start.4
  383.7 1.3 copy-start.2
  449.6 39.4 %copy-start.7 = (bf16[64,1024]{1,0:T(8,128)(2,1)S(1)}, bf16[64,1024]{1,0:T(8,128)(2,1)}, u32[]{:S(2)}) copy-start(bf16[64,1024]{1,0:T(8,128)(2,1)} %constant_dynamic-slice_fusion.1) | copy-start | bytes 393220
  449.6 39.4 %copy-start.11 = (s32[64]{0:T(128)S(1)}, s32[64]{0:T(128)}, u32[]{:S(2)}) copy-start(s32[64]{0:T(128)} %param.21) | copy-start | bytes 772
  491.2 0.7 copy-start.8
  491.9 97.8 %reduce-scatter.2.cloned.1.call-start = ((), (), s32[]{:S(2)}) async-start(), calls=%async_computation.3 | async-start | bytes 2359296 | tf_op jit(solution)/shard_map/reduce_scatter | solution.py:228
  554.8 34.9 %copy-start.1 = (bf16[1,512,2048]{2,1,0:T(8,128)(2,1)S(1)}, bf16[1,512,2048]{2,1,0:T(8,128)(2,1)}, u32[]{:S(2)}) copy-start(bf16[1,512,2048]{2,1,0:T(8,128)(2,1)} %param.15) | copy-start | bytes 6291460
Sparse Core Ops, SparseCore 0:
  219.6 228.1 all-gather.7
  492.0 56.5 all-gather.5
  554.9 34.7 reduce-scatter.1
where the time goes:
time: 602 us; the launch traced here: 596 us
  blocking collectives  202 us (34%)
  waiting for transfers between devices  151 us (25%)
  other arithmetic  90.1 us (15%)
  matrix products  87.9 us (15%)
  local copies, waits for them, and re-layouts  45.4 us (8%)
  between operations  14 us (2%)
    all_gather x2, blocking collectives, joined(): everything = jax.tree.map(lambda part: lax.all_gather(part, axis), value)  134 us
    psum x1, blocking collectives, shards(): lax.psum(jnp.concatenate([jnp.dot(tokens, w_query, preferred_element_type...  68.2 us
    all_gather x1, waiting for transfers between devices, joined(): everything = jax.tree.map(lambda part: lax.all_gather(part, axis), value)  62.8 us
    all_gather x1, waiting for transfers between devices, shards(): gathered = lax.all_gather(head_block, 'ctx', axis=0, tiled=True)  56.6 us
    dot_general x4, matrix products, attend_block(): jnp.einsum('rkgs,skd->rkgd', weights.astype(jnp.bfloat16), value_rows, pr...  43.4 us
    reduce_sum x4, other arithmetic, attend_block(): new_sum = running_sum * faded + jnp.sum(weights, axis=3)  34 us
    dot_general x4, matrix products, attend_block(): jnp.einsum('rkgd,skd->rkgs', queries, key_rows, preferred_element_type=jn...  32.2 us
    reduce_scatter x1, waiting for transfers between devices, shards(): lax.psum_scatter(jnp.dot(gathered, w_out, preferred_element_type=jnp.floa...  31.6 us
  transfers between devices with their start and end apart: 4, of which 3 were waited for; matrix products, arithmetic and copies ran while one was open for 5% of the time, Pallas kernels for 0%

commit v1 on v0

v1 whole, which is shorter than its diff:
```python
import functools
import math

import jax
import jax.numpy as jnp
from jax import lax
from jax.experimental import pallas as pl
from jax.experimental.pallas import tpu as pltpu
from jax.sharding import PartitionSpec as P

HD = 128
HEADS = 8
CTX = 8
ROW = 64
STEPS = ((0, 0), (0, 1), (0, 3), (1, 0), (1, 1), (1, 3), (0, 2), (1, 2))
COEF = HD ** -0.5 * math.log2(math.e)
BF = jnp.bfloat16
F32 = jnp.float32
QKV_SEND = F32
SMEM = pl.BlockSpec(memory_space=pltpu.SMEM)
VMEM = pl.BlockSpec(memory_space=pltpu.VMEM)
ANY = pl.BlockSpec(memory_space=pl.ANY)
PREFILL, ME, TO, FROM, SENDS, PLACE = 0, 1, 8, 16, 24, 32


def peer(place, step, sign):
    flip, turn = step
    return (place // 4 ^ flip) * 4 + (place + sign * turn) % 4


def table():
    ctx = lax.axis_index("ctx")
    tp = lax.axis_index("tp")
    flips = jnp.array([s[0] for s in STEPS], jnp.int32)
    turns = jnp.array([s[1] for s in STEPS], jnp.int32)
    to = (ctx // 4 ^ flips) * 4 + (ctx + turns) % 4
    origin = (ctx // 4 ^ flips) * 4 + (ctx + 4 - turns) % 4
    head = jnp.stack(
        [(lax.axis_index("group") == 0).astype(jnp.int32), ctx, tp] + [jnp.int32(0)] * 5
    )
    sends = (origin % 2 != tp % 2).astype(jnp.int32)
    place = (origin // 2 + 4 - tp // 2) % 4
    return jnp.concatenate([head, to, origin, sends, place]).astype(jnp.int32)


def params(limit=48 << 20, **more):
    return pltpu.CompilerParams(vmem_limit_bytes=limit, **more)


def nbytes(*arrays):
    return sum(math.prod(a.shape) * a.dtype.itemsize for a in arrays)


def project_kernel(meta, x, wq, wkv, *rest):
    outs, acc = rest[:CTX], rest[CTX]
    k = pl.program_id(0)
    wide = wq.shape[1]
    part_q = jnp.dot(x[...], wq[...], preferred_element_type=F32)
    part_kv = jnp.dot(x[...], wkv[...], preferred_element_type=F32)

    @pl.when(k == 0)
    def _():
        acc[:, :wide] = part_q
        acc[:, wide:] = part_kv

    @pl.when(k > 0)
    def _():
        acc[:, :wide] += part_q
        acc[:, wide:] += part_kv

    @pl.when(k == pl.num_programs(0) - 1)
    def _():
        for s in range(CTX):
            first = pl.multiple_of(meta[TO + s] * ROW, ROW)
            outs[s][...] = acc[pl.ds(first, ROW), :].astype(outs[s].dtype)


def project(meta, tokens, w_query, w_keyval):
    rows, depth = tokens.shape
    wide = w_query.shape[1]
    both = wide + w_keyval.shape[1]
    blocks = 4
    deep = depth // blocks
    return pl.pallas_call(
        project_kernel,
        grid=(blocks,),
        in_specs=[
            SMEM,
            pl.BlockSpec((rows, deep), lambda k: (0, k)),
            pl.BlockSpec((deep, wide), lambda k: (k, 0)),
            pl.BlockSpec((deep, both - wide), lambda k: (k, 0)),
        ],
        out_specs=[pl.BlockSpec((ROW, both), lambda k: (0, 0))] * CTX,
        out_shape=[jax.ShapeDtypeStruct((ROW, both), F32 if s == 0 else QKV_SEND) for s in range(CTX)],
        scratch_shapes=[pltpu.VMEM((rows, both), F32)],
        compiler_params=params(),
        cost_estimate=pl.CostEstimate(
            flops=2 * rows * depth * both, bytes_accessed=nbytes(tokens, w_query, w_keyval), transcendentals=0
        ),
        name="project",
    )(meta, tokens, w_query, w_keyval)


def add_kernel(*refs):
    parts, q, kv = refs[:CTX], refs[CTX], refs[CTX + 1]
    total = parts[0][...]
    for part in parts[1:]:
        total = total + part[...].astype(F32)
    total = total.astype(BF)
    q[...] = total[:, : HEADS * HD]
    kv[...] = total[:, HEADS * HD :]


def add_parts(parts):
    return pl.pallas_call(
        add_kernel,
        in_specs=[VMEM] * CTX,
        out_specs=[VMEM] * 2,
        out_shape=[
            jax.ShapeDtypeStruct((ROW, HEADS * HD), BF),
            jax.ShapeDtypeStruct((ROW, 2 * HD), BF),
        ],
        compiler_params=params(),
        cost_estimate=pl.CostEstimate(flops=8 * 64 * 1280, bytes_accessed=nbytes(*parts), transcendentals=0),
        name="add_parts",
    )(*parts)


def sort_kernel(meta, slots, pages, *rest):
    outs, arrivals, counts, order, sem = rest[:CTX], rest[CTX], rest[CTX + 1], rest[CTX + 2], rest[CTX + 3]
    me = meta[ME]
    per = 8

    def clear(i, _):
        counts[i] = 0
        return 0

    @pl.when(meta[PREFILL] == 1)
    def _():
        lax.fori_loop(0, CTX, clear, 0)

        def place(i, _):
            target = lax.shift_right_logical(slots[me * 64 + i], 6)
            n = counts[target]
            order[target * per + n] = i
            counts[target] = n + 1
            return 0

        lax.fori_loop(0, 64, place, 0)
        for s in range(CTX):
            to = meta[TO + s]
            for n in range(per):
                pltpu.make_async_copy(pages.at[order[to * per + n]], outs[s].at[n], sem).start()
        for s in range(CTX):
            pltpu.make_async_copy(pages.at[pl.ds(0, per)], outs[s], sem).wait()

    @pl.when(meta[PREFILL] == 0)
    def _():
        lax.fori_loop(0, CTX, clear, 0)
        for s in range(CTX):
            origin = meta[FROM + s]

            def place(i, n):
                slot = slots[origin * 64 + i]
                mine = lax.shift_right_logical(slot, 6) == me

                @pl.when(mine)
                def _():
                    arrivals[s * per + n] = lax.bitwise_and(slot, 63)

                return n + mine.astype(jnp.int32)

            lax.fori_loop(0, 64, place, 0)


def sort_pages(meta, page_slot, pages):
    chunk = jax.ShapeDtypeStruct((8,) + pages.shape[1:], pages.dtype)
    return pl.pallas_call(
        sort_kernel,
        in_specs=[SMEM, SMEM, ANY],
        out_specs=[ANY] * CTX + [SMEM],
        out_shape=[chunk] * CTX + [jax.ShapeDtypeStruct((64,), jnp.int32)],
        scratch_shapes=[pltpu.SMEM((CTX,), jnp.int32), pltpu.SMEM((64,), jnp.int32), pltpu.SemaphoreType.DMA],
        compiler_params=params(4 << 20),
        cost_estimate=pl.CostEstimate(flops=0, bytes_accessed=2 * nbytes(pages), transcendentals=0),
        name="sort_pages",
    )(meta, page_slot, pages)


def weigh(scores, values, m, l, acc):
    new = jnp.maximum(m[...], jnp.max(scores, axis=1, keepdims=True))
    fade = jnp.exp2((m[...] - new) * COEF)
    weights = jnp.exp2((scores - new[:, :1]) * COEF)
    l[...] = l[...] * fade + jnp.sum(weights, axis=1, keepdims=True)
    acc[...] = acc[...] * fade + jnp.dot(weights.astype(BF), values, preferred_element_type=F32)
    m[...] = new


def attend_kernel(step, meta, q, kv, own, out, q2, m, l, acc):
    j = pl.program_id(0)
    contract = (((1,), (1,)), ((), ()))

    @pl.when(meta[PREFILL] == 1)
    def _():
        @pl.when(j == 0)
        def _():
            for h in range(HEADS):
                q2[pl.ds(h * ROW, ROW), :] = q[:, h * HD : (h + 1) * HD]
            m[...] = jnp.full_like(m, -1e30)
            l[...] = jnp.zeros_like(l)
            acc[...] = jnp.zeros_like(acc)

        scores = lax.dot_general(q2[...], kv[:, :HD], contract, preferred_element_type=F32)
        weigh(scores, kv[:, HD:], m, l, acc)

        @pl.when(j == pl.num_programs(0) - 1)
        def _():
            ahead = (meta[FROM + step] - meta[ME]) * ROW
            scores = lax.dot_general(q2[...], own[:, :HD], contract, preferred_element_type=F32)
            token = lax.bitwise_and(lax.broadcasted_iota(jnp.int32, scores.shape, 0), ROW - 1)
            key = lax.broadcasted_iota(jnp.int32, scores.shape, 1)
            scores = jnp.where(key <= token + ahead, scores, -1e30)
            weigh(scores, own[:, HD:], m, l, acc)
            mixed = acc[...] / l[...]
            level = m[...] * COEF + jnp.log2(l[...])
            high = level.astype(BF).astype(F32)
            rest = level - high
            mid = rest.astype(BF).astype(F32)
            low = rest - mid
            lane = lax.broadcasted_iota(jnp.int32, (ROW, HD), 1)
            stats = jnp.zeros((ROW, HD), F32)
            for h in range(HEADS):
                rows = slice(h * ROW, (h + 1) * ROW)
                out[:, h * HD : (h + 1) * HD] = mixed[rows].astype(out.dtype)
                stats = jnp.where(lane == 3 * h, high[rows], stats)
                stats = jnp.where(lane == 3 * h + 1, mid[rows], stats)
                stats = jnp.where(lane == 3 * h + 2, low[rows], stats)
            out[:, HEADS * HD :] = stats.astype(out.dtype)


def attend(step, meta, q, pages, own, block=1024):
    keys = pages.shape[0]
    big = HEADS * ROW
    return pl.pallas_call(
        functools.partial(attend_kernel, step),
        grid=(keys // block,),
        in_specs=[
            SMEM,
            pl.BlockSpec((ROW, HEADS * HD), lambda j: (0, 0)),
            pl.BlockSpec((block, 2 * HD), lambda j: (j, 0)),
            pl.BlockSpec((ROW, 2 * HD), lambda j: (0, 0)),
        ],
        out_specs=pl.BlockSpec((ROW, (HEADS + 1) * HD), lambda j: (0, 0)),
        out_shape=jax.ShapeDtypeStruct((ROW, (HEADS + 1) * HD), F32 if step == 0 else BF),
        scratch_shapes=[
            pltpu.VMEM((big, HD), BF),
            pltpu.VMEM((big, HD), F32),
            pltpu.VMEM((big, HD), F32),
            pltpu.VMEM((big, HD), F32),
        ],
        compiler_params=params(),
        cost_estimate=pl.CostEstimate(
            flops=4 * big * keys * HD, bytes_accessed=nbytes(pages), transcendentals=big * keys
        ),
        name=f"attend_{step}",
    )(meta, q, pages, own)


def finish_kernel(meta, lengths, arrivals, q, own, *rest):
    states, pages, chunks = rest[:CTX], rest[CTX], rest[CTX + 1 : 2 * CTX + 1]
    heads, pool = rest[2 * CTX + 1 : 2 * CTX + 3]
    held, relaid, q3, o3, sems = rest[2 * CTX + 3 :]
    contract = (((1,), (1,)), ((), ()))
    per = 8

    @pl.when(meta[PREFILL] == 1)
    def _():
        copy = pltpu.make_async_copy(pages, pool, sems.at[0])
        copy.start()
        for h in range(HEADS):
            cols = slice(h * HD, (h + 1) * HD)
            levels = []
            for state in states:
                three = state[:, HEADS * HD :].astype(F32)[:, 3 * h : 3 * h + 3]
                levels.append(three[:, 0:1] + three[:, 1:2] + three[:, 2:3])
            top = functools.reduce(jnp.maximum, levels)
            parts = [jnp.exp2(level - top) for level in levels]
            mixed = sum(state[:, cols].astype(F32) * part for state, part in zip(states, parts))
            heads[:, cols] = (mixed / sum(parts)).astype(BF)
        copy.wait()

    @pl.when(meta[PREFILL] == 0)
    def _():
        load = pltpu.make_async_copy(pages, held, sems.at[0])
        load.start()
        for s in range(CTX):
            for n in range(per):
                slot = arrivals[s * per + n]
                pltpu.make_async_copy(chunks[s].at[n], relaid.at[slot], sems.at[1]).start()
                pltpu.make_async_copy(chunks[s].at[n], pool.at[slot], sems.at[2]).start()
        for h in range(HEADS):
            q3[:, h, :] = q[:, h * HD : (h + 1) * HD].astype(F32)
        load.wait()
        pltpu.make_async_copy(pages, relaid, sems.at[1]).wait()
        at_once = 8
        lane = lax.broadcasted_iota(jnp.int32, (HEADS, 2 * ROW), 1)

        def some(i, _):
            first = i * at_once
            own_rows = own[pl.ds(pl.multiple_of(first, at_once), at_once), :].astype(F32)
            scores, own_scores, values = [], [], []
            for r in range(at_once):
                both = jnp.concatenate([held[first + r], relaid[first + r]], axis=0)
                queries = q3[first + r]
                s = lax.dot_general(queries.astype(BF), both[:, :HD], contract, preferred_element_type=F32)
                seen = (lane < lengths[first + r]) | (lane >= ROW)
                scores.append(jnp.where(seen, s, -1e30))
                own_scores.append(jnp.sum(queries * own_rows[r : r + 1, :HD], axis=1, keepdims=True))
                values.append(both[:, HD:])
            scores = jnp.concatenate(scores, axis=0)
            own_scores = jnp.concatenate(own_scores, axis=0)
            top = jnp.maximum(jnp.max(scores, axis=1, keepdims=True), own_scores)
            weights = jnp.exp2((scores - top) * COEF)
            own_weights = jnp.exp2((own_scores - top) * COEF)
            total = jnp.sum(weights, axis=1, keepdims=True) + own_weights
            weights = weights.astype(BF)
            own_weights = own_weights.astype(BF).astype(F32)
            for r in range(at_once):
                rows = slice(r * HEADS, (r + 1) * HEADS)
                mixed = jnp.dot(weights[rows], values[r], preferred_element_type=F32)
                mixed = mixed + own_weights[rows] * own_rows[r : r + 1, HD:]
                o3[first + r] = mixed / total[rows]
            return 0

        lax.fori_loop(0, ROW // at_once, some, 0)
        for h in range(HEADS):
            heads[:, h * HD : (h + 1) * HD] = o3[:, h, :].astype(BF)
        pltpu.make_async_copy(pages, pool, sems.at[2]).wait()


def finish(meta, lengths, arrivals, q, own, states, pages, chunks):
    return pl.pallas_call(
        finish_kernel,
        in_specs=[SMEM] * 3 + [VMEM] * (2 + CTX) + [ANY] * (1 + CTX),
        out_specs=[VMEM, ANY],
        out_shape=[
            jax.ShapeDtypeStruct((ROW, HEADS * HD), BF),
            jax.ShapeDtypeStruct(pages.shape, BF),
        ],
        scratch_shapes=[
            pltpu.VMEM(pages.shape, BF),
            pltpu.VMEM(pages.shape, BF),
            pltpu.VMEM((ROW, HEADS, HD), F32),
            pltpu.VMEM((ROW, HEADS, HD), F32),
            pltpu.SemaphoreType.DMA((3,)),
        ],
        compiler_params=params(),
        cost_estimate=pl.CostEstimate(flops=1 << 24, bytes_accessed=3 * nbytes(pages), transcendentals=1 << 16),
        name="finish",
    )(meta, lengths, arrivals, q, own, *states, pages, *chunks)


def gather_rows(meta, chunks, rows, wanted):
    for s in range(CTX):
        @pl.when(meta[SENDS + s] == wanted)
        def _():
            rows[pl.ds(pl.multiple_of(meta[PLACE + s] * ROW, ROW), ROW), :] = chunks[s][...]


def other_half_kernel(meta, *rest):
    chunks, w, out, rows = rest[:CTX], rest[CTX], rest[CTX + 1], rest[CTX + 2]

    @pl.when(pl.program_id(0) == 0)
    def _():
        gather_rows(meta, chunks, rows, 1)

    out[...] = jnp.dot(rows[...], w[...], preferred_element_type=F32).astype(BF)


def own_half_kernel(meta, *rest):
    chunks, w, came, rows = rest[:CTX], rest[CTX], rest[CTX + 1], rest[-1]
    outs = rest[CTX + 2 : CTX + 6]

    @pl.when(pl.program_id(0) == 0)
    def _():
        gather_rows(meta, chunks, rows, 0)

    total = jnp.dot(rows[...], w[...], preferred_element_type=F32) + came[...].astype(F32)
    for p in range(4):
        outs[p][...] = total[p * ROW : (p + 1) * ROW].astype(outs[p].dtype)


def out_specs_of(chunks, w_out, block):
    wide = w_out.shape[0]
    return [SMEM] + [pl.BlockSpec((ROW, wide), lambda n: (0, 0))] * CTX + [
        pl.BlockSpec((wide, block), lambda n: (0, n))
    ]


def other_half(meta, chunks, w_out, block=512):
    depth, wide = w_out.shape
    return pl.pallas_call(
        other_half_kernel,
        grid=(wide // block,),
        in_specs=out_specs_of(chunks, w_out, block),
        out_specs=pl.BlockSpec((4 * ROW, block), lambda n: (0, n)),
        out_shape=jax.ShapeDtypeStruct((4 * ROW, wide), BF),
        scratch_shapes=[pltpu.VMEM((4 * ROW, depth), BF)],
        compiler_params=params(),
        cost_estimate=pl.CostEstimate(
            flops=8 * ROW * depth * wide, bytes_accessed=nbytes(w_out), transcendentals=0
        ),
        name="other_half",
    )(meta, *chunks, w_out)


def own_half(meta, chunks, w_out, came, block=512):
    depth, wide = w_out.shape
    return pl.pallas_call(
        own_half_kernel,
        grid=(wide // block,),
        in_specs=out_specs_of(chunks, w_out, block) + [pl.BlockSpec((4 * ROW, block), lambda n: (0, n))],
        out_specs=[pl.BlockSpec((ROW, block), lambda n: (0, n))] * 4,
        out_shape=[jax.ShapeDtypeStruct((ROW, wide), F32 if p == 0 else BF) for p in range(4)],
        scratch_shapes=[pltpu.VMEM((4 * ROW, depth), BF)],
        compiler_params=params(),
        cost_estimate=pl.CostEstimate(
            flops=8 * ROW * depth * wide, bytes_accessed=nbytes(w_out), transcendentals=0
        ),
        name="own_half",
    )(meta, *chunks, w_out, came)


def last_kernel(a, b, c, d, out):
    out[...] = (a[...] + b[...].astype(F32) + c[...].astype(F32) + d[...].astype(F32)).astype(BF)


def last_sum(parts):
    return pl.pallas_call(
        last_kernel,
        in_specs=[VMEM] * 4,
        out_specs=VMEM,
        out_shape=jax.ShapeDtypeStruct(parts[0].shape, BF),
        compiler_params=params(),
        cost_estimate=pl.CostEstimate(flops=1 << 19, bytes_accessed=nbytes(*parts), transcendentals=0),
        name="last_sum",
    )(*parts)


def shards(hidden_in, w_query, w_keyval, w_out, kv_pages, page_slot, lengths):
    meta = table()
    pages = kv_pages[0]
    flat_pages = pages.reshape(-1, pages.shape[2])

    def ring(value, s, sign=1):
        return lax.ppermute(value, "ctx", [(c, peer(c, STEPS[s], sign)) for c in range(CTX)])

    parts = project(meta, hidden_in[0], w_query, w_keyval)
    parts = [parts[0]] + [ring(parts[s], s) for s in range(1, CTX)]
    *sorted_pages, arrivals = sort_pages(meta, page_slot, pages)
    chunks = [
        lax.ppermute(
            sorted_pages[s], ("group", "ctx"), [(c, CTX + peer(c, STEPS[s], 1)) for c in range(CTX)]
        )
        for s in range(CTX)
    ]
    q, own = add_parts(parts)
    states = [attend(0, meta, q, flat_pages, own)]
    for s in range(1, CTX):
        came = ring(q, s)
        states.append(ring(attend(s, meta, came, flat_pages, own), s, -1))
    heads, pool = finish(meta, lengths, arrivals, q, own, states, pages, chunks)
    gathered = [heads] + [ring(heads, s) for s in range(1, CTX)]
    sent = other_half(meta, gathered, w_out)
    came = lax.ppermute(sent, "tp", [(t, t ^ 1) for t in range(8)])
    mine = own_half(meta, gathered, w_out, came)
    totals = [mine[0]] + [
        lax.ppermute(mine[p], "tp", [(t, (t + 2 * p) % 8) for t in range(8)]) for p in range(1, 4)
    ]
    return (last_sum(totals)[None], pool[None])


def solution(mesh):
    placed = (
        P("group", None, "ctx"),
        P("ctx", "tp"),
        P("ctx", "tp"),
        P("tp", "ctx"),
        P("group", "ctx", None, "tp"),
        P(),
        P("ctx"),
    )
    return jax.shard_map(
        shards,
        mesh=mesh,
        in_specs=placed,
        out_specs=(P("group", "tp", "ctx"), P("group", "ctx", None, "tp")),
        check_vma=False,
    )
```

time: 602 us -> 197 us (0.33)
  blocking collectives: 202 us -> 0 us
  waiting for transfers between devices: 151 us -> 36.1 us
  other arithmetic: 90.1 us -> 0.73 us
  matrix products: 87.9 us -> 0 us
  Pallas kernels: 0 us -> 78.3 us
  starting transfers between devices: 4.66 us -> 77.8 us
  local copies, waits for them, and re-layouts: 45.4 us -> 2.92 us
  between operations: 14 us -> 1.07 us
    all_gather x2 -> x0, blocking collectives: 134 us -> none  [joined(): everything = jax.tree.map(lambda part: lax.all_gather(part, axis), value)]
    all_gather x2 -> x0, waiting for transfers between devices: 119 us -> none  [the longest x1 62.8 us: joined(): everything = jax.tree.map(lambda part: lax.all_gather(part, axis), value)]
    dot_general x13 -> x0, matrix products: 87.9 us -> none  [the longest x4 43.4 us: attend_block(): jnp.einsum('rkgs,skd->rkgd', weights.astype(jnp.bfloat16), value_rows, pr...]
    pallas_call x0 -> x15, Pallas kernels: none -> 78.3 us  [the longest x8 53.9 us: attend(): pl.pallas_call(functools.partial(attend_kernel, step), grid=(keys // bloc...]
    ppermute x0 -> x40, starting transfers between devices: none -> 77.8 us  [the longest x28 41.1 us: ring(): lax.ppermute(value, 'ctx', [(c, peer(c, STEPS[s], sign)) for c in range(C...]
    psum x1 -> x0, blocking collectives: 68.2 us -> none  [shards(): lax.psum(jnp.concatenate([jnp.dot(tokens, w_query, preferred_element_type...]
    ppermute x0 -> x40, waiting for transfers between devices: none -> 36.1 us  [the longest x28 19.9 us: ring(): lax.ppermute(value, 'ctx', [(c, peer(c, STEPS[s], sign)) for c in range(C...]
    reduce_sum x5 -> x0, other arithmetic: 35.4 us -> none  [the longest x4 34 us: attend_block(): new_sum = running_sum * faded + jnp.sum(weights, axis=3)]
  transfers between devices with their start and end apart: 4 -> 40, of which waited for: 3 -> 11; matrix products, arithmetic and copies ran while one was open for 5% -> 0% of each run, Pallas kernels for 0% -> 30%
where the time goes in v1:
time: 197 us
  Pallas kernels  78.3 us (40%)
  starting transfers between devices  77.8 us (39%)
  waiting for transfers between devices  36.1 us (18%)
  local copies, waits for them, and re-layouts  2.92 us (1%)
    pallas_call x8, Pallas kernels, attend(): pl.pallas_call(functools.partial(attend_kernel, step), grid=(keys // bloc...  53.9 us
    ppermute x28, starting transfers between devices, ring(): lax.ppermute(value, 'ctx', [(c, peer(c, STEPS[s], sign)) for c in range(C...  41.1 us
    ppermute x8, starting transfers between devices, shards(): lax.ppermute(sorted_pages[s], ('group', 'ctx'), [(c, CTX + peer(c, STEPS[...  24.6 us
    ppermute x28, waiting for transfers between devices, ring(): lax.ppermute(value, 'ctx', [(c, peer(c, STEPS[s], sign)) for c in range(C...  19.9 us
    ppermute x3, waiting for transfers between devices, shards(): lax.ppermute(mine[p], 'tp', [(t, (t + 2 * p) % 8) for t in range(8)])  10.6 us
    ppermute x1, starting transfers between devices, shards(): came = lax.ppermute(sent, 'tp', [(t, t ^ 1) for t in range(8)])  7.13 us
    pallas_call x1, Pallas kernels, project(): pl.pallas_call(project_kernel, grid=(blocks,), in_specs=[SMEM, pl.BlockSp...  6.14 us
    pallas_call x1, Pallas kernels, sort_pages(): pl.pallas_call(sort_kernel, in_specs=[SMEM, SMEM, ANY], out_specs=[ANY] *...  5.16 us
  transfers between devices with their start and end apart: 40, of which 11 were waited for; matrix products, arithmetic and copies ran while one was open for 0% of the time, Pallas kernels for 30%

profile of v1, /device:TPU:1, one launch (start us, length us, event | category | flops | bytes accessed | tf_op | source)
XLA Modules:
  0.0 196.9 jit_solution(18140215750793909811)
XLA Ops:
  0.7 0.7 and_select_fusion
  1.4 0.1 concatenate.3.meta
  1.5 1.6 copy-done.3
  3.1 1.2 copy-done.4
  4.3 6.1 %project.1 = (f32[64,1280]{1,0:T(8,128)S(1)}, f32[64,1280]{1,0:T(8,128)S(1)}, f32[64,1280]{1,0:T(8,128)S(1)}, f32[64,1280]{1,0:T(8,128)S(1)}, f32[64,1280]{1,0:T...) custom-call(s32[40]{0:T(128)S(1)} %concatenate.3.meta, ...), custom_call_target="tpu_custom_call" | custom-call | flops 2684354560 | bytes 7340032 | tf_op jit(solution)/shard_map/project/pallas_call | solution.py:84
  10.5 2.1 %collective-permute-start = (f32[64,1280]{1,0:T(8,128)S(1)}, f32[64,1280]{1,0:T(8,128)S(1)}, u32[]{:S(2)}, u32[]{:S(2)}) collective-permute-start(f32[64,1280]{1,0:T(8,128)S(1)} %get-tuple-element.29), channel_id=1, source_target_pairs={{0,8},{8,16},{16,24},{24,0},{32,40},{40,48},{48,56},{56,32},{1,9},... | collective-permute-start | bytes 983048 | tf_op jit(solution)/shard_map/ppermute | solution.py:456
  12.6 1.4 collective-permute-start.1
  13.9 1.7 collective-permute-start.2
  15.7 3.6 %collective-permute-start.4 = (f32[64,1280]{1,0:T(8,128)S(1)}, f32[64,1280]{1,0:T(8,128)S(1)}, u32[]{:S(2)}, u32[]{:S(2)}) collective-permute-start(f32[64,1280]{1,0:T(8,128)S(1)} %get-tuple-element.33), channel_id=1, source_target_pairs={{0,56},{8,32},{16,40},{24,48},{32,24},{40,0},{48,8},{56,16},{1,57}... | collective-permute-start | bytes 983048 | tf_op jit(solution)/shard_map/ppermute | solution.py:456
  19.3 1.6 collective-permute-done.refs_1_
  20.9 1.8 collective-permute-start.5
  22.7 2.8 %collective-permute-start.6 = (f32[64,1280]{1,0:T(8,128)S(1)}, f32[64,1280]{1,0:T(8,128)S(1)}, u32[]{:S(2)}, u32[]{:S(2)}) collective-permute-start(f32[64,1280]{1,0:T(8,128)S(1)} %get-tuple-element.35), channel_id=1, source_target_pairs={{0,48},{8,56},{16,32},{24,40},{32,16},{40,24},{48,0},{56,8},{1,49}... | collective-permute-start | bytes 983048 | tf_op jit(solution)/shard_map/ppermute | solution.py:456
  25.5 5.2 %sort_pages.1 = (bf16[8,64,256]{2,1,0:T(8,128)(2,1)S(1)}, bf16[8,64,256]{2,1,0:T(8,128)(2,1)S(1)}, bf16[8,64,256]{2,1,0:T(8,128)(2,1)S(1)}, bf16[8,64,256]{2,1,0...) custom-call(s32[40]{0:T(128)S(1)} %concatenate.3.meta, ...), custom_call_target="tpu_custom_call" | custom-call | bytes 4194304 | tf_op jit(solution)/shard_map/sort_pages/pallas_call | solution.py:178
  30.6 4.7 %collective-permute-done.2.refs_3_ = f32[64,1280]{1,0:T(8,128)S(1)} collective-permute-done((f32[64,1280]{1,0:T(8,128)S(1)}, f32[64,1280]{1,0:T(8,128)S(1)}, u32[]{:S(2)}, u32[]{:S(2)}) %collective-permute-start.2) | collective-permute-done | bytes 327712 | tf_op jit(solution)/shard_map/ppermute | solution.py:456
  35.3 5.2 %collective-permute-start.21 = (bf16[8,64,256]{2,1,0:T(8,128)(2,1)S(1)}, bf16[8,64,256]{2,1,0:T(8,128)(2,1)S(1)}, u32[]{:S(2)}, u32[]{:S(2)}) collective-permute-start(bf16[8,64,256]{2,1,0:T(8,128)(2,1)S(1)} %get-tuple-element.38), channel_id=1, source_target_pairs={{0,64},{8,72},{16,80},{24,88},{32,96},{40,104},{48,112},{56,120},{... | collective-permute-start | bytes 786440 | tf_op jit(solution)/shard_map/ppermute | solution.py:462
  40.6 1.3 collective-permute-start.22
  41.9 7.8 %collective-permute-done.6.refs_7_ = f32[64,1280]{1,0:T(8,128)S(1)} collective-permute-done((f32[64,1280]{1,0:T(8,128)S(1)}, f32[64,1280]{1,0:T(8,128)S(1)}, u32[]{:S(2)}, u32[]{:S(2)}) %collective-permute-start.6) | collective-permute-done | bytes 327712 | tf_op jit(solution)/shard_map/ppermute | solution.py:456
  49.7 0.1 add_parts.1
  49.9 0.1 collective-permute-start.19
  50.0 2.6 %collective-permute-start.17 = (bf16[64,1024]{1,0:T(8,128)(2,1)S(1)}, bf16[64,1024]{1,0:T(8,128)(2,1)S(1)}, u32[]{:S(2)}, u32[]{:S(2)}) collective-permute-start(bf16[64,1024]{1,0:T(8,128)(2,1)S(1)} %get-tuple-element.36.q), channel_id=1, source_target_pairs={{0,16},{8,24},{16,0},{24,8},{32,48},{40,56},{48,32},{56,40},{1,17}... | collective-permute-start | bytes 393224 | tf_op jit(solution)/shard_map/ppermute | solution.py:456
  52.6 6.1 %collective-permute-start.23 = (bf16[8,64,256]{2,1,0:T(8,128)(2,1)S(1)}, bf16[8,64,256]{2,1,0:T(8,128)(2,1)S(1)}, u32[]{:S(2)}, u32[]{:S(2)}) collective-permute-start(bf16[8,64,256]{2,1,0:T(8,128)(2,1)S(1)} %get-tuple-element.40), channel_id=1, source_target_pairs={{0,88},{8,64},{16,72},{24,80},{32,120},{40,96},{48,104},{56,112},{... | collective-permute-start | bytes 786440 | tf_op jit(solution)/shard_map/ppermute | solution.py:462
  58.6 0.6 collective-permute-done.19.q
  59.2 6.7 %attend_7.1 = bf16[64,1152]{1,0:T(8,128)(2,1)S(1)} custom-call(s32[40]{0:T(128)S(1)} %concatenate.3.meta, bf16[64,1024]{1,0:T(8,128)(2,1)S(1)} %collective-permute-done.19.q, bf16[4096,256]{1,0:T(8,128)(2,1)S(1)} %bitcast.9, bf16[64,256]{1,0:T(8,128)(2,1)S(1)} %get-tuple-element.37.own), custom_call_target="tpu_custom_call" | custom-call | flops 1073741824 | bytes 2097152 | tf_op jit(solution)/shard_map/attend_7/pallas_call | solution.py:244
  66.0 3.3 %collective-permute-done.21.rest_9_ = bf16[8,64,256]{2,1,0:T(8,128)(2,1)S(1)} collective-permute-done((bf16[8,64,256]{2,1,0:T(8,128)(2,1)S(1)}, bf16[8,64,256]{2,1,0:T(8,128)(2,1)S(1)}, u32[]{:S(2)}, u32[]{:S(2)}) %collective-permute-start.21) | collective-permute-done | bytes 262176 | tf_op jit(solution)/shard_map/ppermute | solution.py:462
  69.2 6.8 %collective-permute-start.24 = (bf16[8,64,256]{2,1,0:T(8,128)(2,1)S(1)}, bf16[8,64,256]{2,1,0:T(8,128)(2,1)S(1)}, u32[]{:S(2)}, u32[]{:S(2)}) collective-permute-start(bf16[8,64,256]{2,1,0:T(8,128)(2,1)S(1)} %get-tuple-element.41), channel_id=1, source_target_pairs={{0,96},{8,104},{16,112},{24,120},{32,64},{40,72},{48,80},{56,88},{... | collective-permute-start | bytes 786440 | tf_op jit(solution)/shard_map/ppermute | solution.py:462
  76.0 1.3 collective-permute-start.25
  77.3 2.4 %collective-permute-start.9 = (bf16[64,1024]{1,0:T(8,128)(2,1)S(1)}, bf16[64,1024]{1,0:T(8,128)(2,1)S(1)}, u32[]{:S(2)}, u32[]{:S(2)}) collective-permute-start(bf16[64,1024]{1,0:T(8,128)(2,1)S(1)} %get-tuple-element.36.q), channel_id=1, source_target_pairs={{0,24},{8,0},{16,8},{24,16},{32,56},{40,32},{48,40},{56,48},{1,25}... | collective-permute-start | bytes 393224 | tf_op jit(solution)/shard_map/ppermute | solution.py:456
  79.8 6.7 %attend_6.1 = bf16[64,1152]{1,0:T(8,128)(2,1)S(1)} custom-call(s32[40]{0:T(128)S(1)} %concatenate.3.meta, bf16[64,1024]{1,0:T(8,128)(2,1)S(1)} %collective-permute-done.17.q, bf16[4096,256]{1,0:T(8,128)(2,1)S(1)} %bitcast.10, bf16[64,256]{1,0:T(8,128)(2,1)S(1)} %get-tuple-element.37.own), custom_call_target="tpu_custom_call" | custom-call | flops 1073741824 | bytes 2097152 | tf_op jit(solution)/shard_map/attend_6/pallas_call | solution.py:244
  86.5 0.1 collective-permute-start.7
  86.6 6.8 %attend_5.1 = bf16[64,1152]{1,0:T(8,128)(2,1)S(1)} custom-call(s32[40]{0:T(128)S(1)} %concatenate.3.meta, bf16[64,1024]{1,0:T(8,128)(2,1)S(1)} %collective-permute-done.15.q, bf16[4096,256]{1,0:T(8,128)(2,1)S(1)} %bitcast.11, bf16[64,256]{1,0:T(8,128)(2,1)S(1)} %get-tuple-element.37.own), custom_call_target="tpu_custom_call" | custom-call | flops 1073741824 | bytes 2097152 | tf_op jit(solution)/shard_map/attend_5/pallas_call | solution.py:244
  93.4 0.3 collective-permute-start.13
  93.7 0.2 collective-permute-start.11
  93.9 6.7 %attend_2.1 = bf16[64,1152]{1,0:T(8,128)(2,1)S(1)} custom-call(s32[40]{0:T(128)S(1)} %concatenate.3.meta, bf16[64,1024]{1,0:T(8,128)(2,1)S(1)} %collective-permute-done.9.q, bf16[4096,256]{1,0:T(8,128)(2,1)S(1)} %bitcast.12, bf16[64,256]{1,0:T(8,128)(2,1)S(1)} %get-tuple-element.37.own), custom_call_target="tpu_custom_call" | custom-call | flops 1073741824 | bytes 2097152 | tf_op jit(solution)/shard_map/attend_2/pallas_call | solution.py:244
  100.7 1.3 collective-permute-start.26
  102.0 1.3 collective-permute-start.27
  103.3 1.3 collective-permute-start.28
  104.6 6.8 %attend_1.1 = bf16[64,1152]{1,0:T(8,128)(2,1)S(1)} custom-call(s32[40]{0:T(128)S(1)} %concatenate.3.meta, bf16[64,1024]{1,0:T(8,128)(2,1)S(1)} %collective-permute-done.7.q, bf16[4096,256]{1,0:T(8,128)(2,1)S(1)} %bitcast.13, bf16[64,256]{1,0:T(8,128)(2,1)S(1)} %get-tuple-element.37.own), custom_call_target="tpu_custom_call" | custom-call | flops 1073741824 | bytes 2097152 | tf_op jit(solution)/shard_map/attend_1/pallas_call | solution.py:244
  111.4 3.7 %collective-permute-start.8 = (bf16[64,1152]{1,0:T(8,128)(2,1)S(1)}, bf16[64,1152]{1,0:T(8,128)(2,1)S(1)}, u32[]{:S(2)}, u32[]{:S(2)}) collective-permute-start(bf16[64,1152]{1,0:T(8,128)(2,1)S(1)} %attend_1.1), channel_id=1, source_target_pairs={{0,24},{8,0},{16,8},{24,16},{32,56},{40,32},{48,40},{56,48},{1,25}... | collective-permute-start | bytes 442376 | tf_op jit(solution)/shard_map/ppermute | solution.py:456
  115.1 6.7 %attend_4.1 = bf16[64,1152]{1,0:T(8,128)(2,1)S(1)} custom-call(s32[40]{0:T(128)S(1)} %concatenate.3.meta, bf16[64,1024]{1,0:T(8,128)(2,1)S(1)} %collective-permute-done.13.q, bf16[4096,256]{1,0:T(8,128)(2,1)S(1)} %bitcast.14, bf16[64,256]{1,0:T(8,128)(2,1)S(1)} %get-tuple-element.37.own), custom_call_target="tpu_custom_call" | custom-call | flops 1073741824 | bytes 2097152 | tf_op jit(solution)/shard_map/attend_4/pallas_call | solution.py:244
  121.8 6.8 %attend_3.1 = bf16[64,1152]{1,0:T(8,128)(2,1)S(1)} custom-call(s32[40]{0:T(128)S(1)} %concatenate.3.meta, bf16[64,1024]{1,0:T(8,128)(2,1)S(1)} %collective-permute-done.11.q, bf16[4096,256]{1,0:T(8,128)(2,1)S(1)} %bitcast.15, bf16[64,256]{1,0:T(8,128)(2,1)S(1)} %get-tuple-element.37.own), custom_call_target="tpu_custom_call" | custom-call | flops 1073741824 | bytes 2097152 | tf_op jit(solution)/shard_map/attend_3/pallas_call | solution.py:244
  128.6 0.4 collective-permute-start.12
  129.0 3.5 %collective-permute-start.14 = (bf16[64,1152]{1,0:T(8,128)(2,1)S(1)}, bf16[64,1152]{1,0:T(8,128)(2,1)S(1)}, u32[]{:S(2)}, u32[]{:S(2)}) collective-permute-start(bf16[64,1152]{1,0:T(8,128)(2,1)S(1)} %attend_4.1), channel_id=1, source_target_pairs={{0,56},{8,32},{16,40},{24,48},{32,24},{40,0},{48,8},{56,16},{1,57}... | collective-permute-start | bytes 442376 | tf_op jit(solution)/shard_map/ppermute | solution.py:456
  132.5 1.3 collective-permute-start.18
  133.8 1.9 collective-permute-start.20
  135.7 6.7 %attend_0.1.rest_0_ = f32[64,1152]{1,0:T(8,128)S(1)} custom-call(s32[40]{0:T(128)S(1)} %concatenate.3.meta, bf16[64,1024]{1,0:T(8,128)(2,1)S(1)} %get-tuple-element.36.q, bf16[4096,256]{1,0:T(8,128)(2,1)S(1)} %bitcast.16, bf16[64,256]{1,0:T(8,128)(2,1)S(1)} %get-tuple-element.37.own), custom_call_target="tpu_custom_call" | custom-call | flops 1073741824 | bytes 2097152 | tf_op jit(solution)/shard_map/attend_0/pallas_call | solution.py:244
  142.4 4.0 %finish.1 = (bf16[64,1024]{1,0:T(8,128)(2,1)S(1)}, bf16[64,64,256]{2,1,0:T(8,128)(2,1)}) custom-call(s32[40]{0:T(128)S(1)} %concatenate.3.meta, s32[64]{0:T(128)S(1)} %copy-done.2, s32[64]{0:T(128)S(1)} %get-tuple-element.27.arrivals, bf16[64,1024]{1,0:T(8,128)(2,1)S(1)} %get-tuple-element.36.q, bf16[64,256]{1,0:T(8,128)(2,1)S(1)} %get-tuple-element.37.own, ...), custom_call_target="tpu_custom_call" | custom-call | flops 16777216 | bytes 6291456 | tf_op jit(solution)/shard_map/finish/pallas_call | solution.py:342
  146.4 2.1 %collective-permute-start.35 = (bf16[64,1024]{1,0:T(8,128)(2,1)S(1)}, bf16[64,1024]{1,0:T(8,128)(2,1)S(1)}, u32[]{:S(2)}, u32[]{:S(2)}) collective-permute-start(bf16[64,1024]{1,0:T(8,128)(2,1)S(1)} %get-tuple-element.46.rest_0_), channel_id=1, source_target_pairs={{0,48},{8,56},{16,32},{24,40},{32,16},{40,24},{48,0},{56,8},{1,49}... | collective-permute-start | bytes 393224 | tf_op jit(solution)/shard_map/ppermute | solution.py:456
  148.5 1.8 collective-permute-start.34
  150.3 3.5 %collective-permute-start.33 = (bf16[64,1024]{1,0:T(8,128)(2,1)S(1)}, bf16[64,1024]{1,0:T(8,128)(2,1)S(1)}, u32[]{:S(2)}, u32[]{:S(2)}) collective-permute-start(bf16[64,1024]{1,0:T(8,128)(2,1)S(1)} %get-tuple-element.46.rest_0_), channel_id=1, source_target_pairs={{0,56},{8,32},{16,40},{24,48},{32,24},{40,0},{48,8},{56,16},{1,57}... | collective-permute-start | bytes 393224 | tf_op jit(solution)/shard_map/ppermute | solution.py:456
  153.8 0.3 collective-permute-start.31
  154.1 3.5 %collective-permute-start.30 = (bf16[64,1024]{1,0:T(8,128)(2,1)S(1)}, bf16[64,1024]{1,0:T(8,128)(2,1)S(1)}, u32[]{:S(2)}, u32[]{:S(2)}) collective-permute-start(bf16[64,1024]{1,0:T(8,128)(2,1)S(1)} %get-tuple-element.46.rest_0_), channel_id=1, source_target_pairs={{0,24},{8,0},{16,8},{24,16},{32,56},{40,32},{48,40},{56,48},{1,25}... | collective-permute-start | bytes 393224 | tf_op jit(solution)/shard_map/ppermute | solution.py:456
  157.7 4.1 %collective-permute-done.32.rest_4_ = bf16[64,1024]{1,0:T(8,128)(2,1)S(1)} collective-permute-done((bf16[64,1024]{1,0:T(8,128)(2,1)S(1)}, bf16[64,1024]{1,0:T(8,128)(2,1)S(1)}, u32[]{:S(2)}, u32[]{:S(2)}) %collective-permute-start.32) | collective-permute-done | bytes 131104 | tf_op jit(solution)/shard_map/ppermute | solution.py:456
  161.8 0.3 collective-permute-done.30.rest_2_
  162.1 0.7 collective-permute-done.29.rest_1_
  162.8 4.0 %other_half.1 = bf16[256,2048]{1,0:T(8,128)(2,1)S(1)} custom-call(s32[40]{0:T(128)S(1)} %concatenate.3.meta, bf16[64,1024]{1,0:T(8,128)(2,1)S(1)} %get-tuple-element.46.rest_0_, bf16[64,1024]{1,0:T(8,128)(2,1)S(1)} %collective-permute-done.29.rest_1_, bf16[64,1024]{1,0:T(8,128)(2,1)S(1)} %collective-permute-done.30.rest_2_, ...), custom_call_target="tpu_custom_call" | custom-call | flops 1073741824 | bytes 4194304 | tf_op jit(solution)/shard_map/other_half/pallas_call | solution.py:402
  166.9 7.1 %collective-permute-start.36 = (bf16[256,2048]{1,0:T(8,128)(2,1)S(1)}, bf16[256,2048]{1,0:T(8,128)(2,1)S(1)}, u32[]{:S(2)}, u32[]{:S(2)}) collective-permute-start(bf16[256,2048]{1,0:T(8,128)(2,1)S(1)} %other_half.1), channel_id=1, source_target_pairs={{0,1},{1,0},{2,3},{3,2},{4,5},{5,4},{6,7},{7,6},{8,9},{9,8},{10,11... | collective-permute-start | bytes 3145736 | tf_op jit(solution)/shard_map/ppermute | solution.py:475
  174.0 2.3 %collective-permute-done.36.rest_9_ = bf16[256,2048]{1,0:T(8,128)(2,1)S(1)} collective-permute-done((bf16[256,2048]{1,0:T(8,128)(2,1)S(1)}, bf16[256,2048]{1,0:T(8,128)(2,1)S(1)}, u32[]{:S(2)}, u32[]{:S(2)}) %collective-permute-start.36) | collective-permute-done | bytes 1048608 | tf_op jit(solution)/shard_map/ppermute | solution.py:475
  176.3 4.1 %own_half.1 = (f32[64,2048]{1,0:T(8,128)S(1)}, bf16[64,2048]{1,0:T(8,128)(2,1)S(1)}, bf16[64,2048]{1,0:T(8,128)(2,1)S(1)}, bf16[64,2048]{1,0:T(8,128)(2,1)S(1)}) custom-call(s32[40]{0:T(128)S(1)} %concatenate.3.meta, bf16[64,1024]{1,0:T(8,128)(2,1)S(1)} %get-tuple-element.46.rest_0_, bf16[64,1024]{1,0:T(8,128)(2,1)S(1)} %collective-permute-done.29.rest_1_, ...), custom_call_target="tpu_custom_call" | custom-call | flops 1073741824 | bytes 4194304 | tf_op jit(solution)/shard_map/own_half/pallas_call | solution.py:419
  180.4 1.4 collective-permute-start.37
  181.8 2.6 %collective-permute-start.38 = (bf16[64,2048]{1,0:T(8,128)(2,1)S(1)}, bf16[64,2048]{1,0:T(8,128)(2,1)S(1)}, u32[]{:S(2)}, u32[]{:S(2)}) collective-permute-start(bf16[64,2048]{1,0:T(8,128)(2,1)S(1)} %get-tuple-element.49), channel_id=1, source_target_pairs={{0,4},{1,5},{2,6},{3,7},{4,0},{5,1},{6,2},{7,3},{8,12},{9,13},{10,... | collective-permute-start | bytes 786440 | tf_op jit(solution)/shard_map/ppermute | solution.py:478
  184.4 1.1 collective-permute-start.39
  185.5 3.9 %collective-permute-done.37.b = bf16[64,2048]{1,0:T(8,128)(2,1)S(1)} collective-permute-done((bf16[64,2048]{1,0:T(8,128)(2,1)S(1)}, bf16[64,2048]{1,0:T(8,128)(2,1)S(1)}, u32[]{:S(2)}, u32[]{:S(2)}) %collective-permute-start.37) | collective-permute-done | bytes 262176 | tf_op jit(solution)/shard_map/ppermute | solution.py:478
  189.3 6.7 %collective-permute-done.38.c = bf16[64,2048]{1,0:T(8,128)(2,1)S(1)} collective-permute-done((bf16[64,2048]{1,0:T(8,128)(2,1)S(1)}, bf16[64,2048]{1,0:T(8,128)(2,1)S(1)}, u32[]{:S(2)}, u32[]{:S(2)}) %collective-permute-start.38) | collective-permute-done | bytes 262176 | tf_op jit(solution)/shard_map/ppermute | solution.py:478
  196.1 0.8 last_sum.1
  (45 shorter events, 0.1 us)
Async XLA Ops:
  1.5 1.6 copy-start.3
  3.1 1.2 copy-start.4
  4.3 21.2 %copy-start = (bf16[1,64,64,256]{3,2,1,0:T(8,128)(2,1)S(1)}, bf16[1,64,64,256]{3,2,1,0:T(8,128)(2,1)}, u32[]{:S(2)}) copy-start(bf16[1,64,64,256]{3,2,1,0:T(8,128)(2,1)} %param.13) | copy-start | bytes 6291460
  4.3 21.2 %copy-start.1 = (s32[512]{0:T(512)S(1)}, s32[512]{0:T(512)}, u32[]{:S(2)}) copy-start(s32[512]{0:T(512)} %slots.1) | copy-start | bytes 6148
  10.5 10.4 %collective-permute-start = (f32[64,1280]{1,0:T(8,128)S(1)}, f32[64,1280]{1,0:T(8,128)S(1)}, u32[]{:S(2)}, u32[]{:S(2)}) collective-permute-start(f32[64,1280]{1,0:T(8,128)S(1)} %get-tuple-element.29), channel_id=1, source_target_pairs={{0,8},{8,16},{16,24},{24,0},{32,40},{40,48},{48,56},{56,32},{1,9},... | collective-permute-start | bytes 983048 | tf_op jit(solution)/shard_map/ppermute | solution.py:456
  12.6 10.1 %collective-permute-start.1 = (f32[64,1280]{1,0:T(8,128)S(1)}, f32[64,1280]{1,0:T(8,128)S(1)}, u32[]{:S(2)}, u32[]{:S(2)}) collective-permute-start(f32[64,1280]{1,0:T(8,128)S(1)} %get-tuple-element.30), channel_id=1, source_target_pairs={{0,24},{8,0},{16,8},{24,16},{32,56},{40,32},{48,40},{56,48},{1,25}... | collective-permute-start | bytes 983048 | tf_op jit(solution)/shard_map/ppermute | solution.py:456
  13.9 21.4 %collective-permute-start.2 = (f32[64,1280]{1,0:T(8,128)S(1)}, f32[64,1280]{1,0:T(8,128)S(1)}, u32[]{:S(2)}, u32[]{:S(2)}) collective-permute-start(f32[64,1280]{1,0:T(8,128)S(1)} %get-tuple-element.31), channel_id=1, source_target_pairs={{0,32},{8,40},{16,48},{24,56},{32,0},{40,8},{48,16},{56,24},{1,33}... | collective-permute-start | bytes 983048 | tf_op jit(solution)/shard_map/ppermute | solution.py:456
  15.7 24.9 %collective-permute-start.3 = (f32[64,1280]{1,0:T(8,128)S(1)}, f32[64,1280]{1,0:T(8,128)S(1)}, u32[]{:S(2)}, u32[]{:S(2)}) collective-permute-start(f32[64,1280]{1,0:T(8,128)S(1)} %get-tuple-element.32), channel_id=1, source_target_pairs={{0,40},{8,48},{16,56},{24,32},{32,8},{40,16},{48,24},{56,0},{1,41}... | collective-permute-start | bytes 983048 | tf_op jit(solution)/shard_map/ppermute | solution.py:456
  15.7 26.2 %collective-permute-start.4 = (f32[64,1280]{1,0:T(8,128)S(1)}, f32[64,1280]{1,0:T(8,128)S(1)}, u32[]{:S(2)}, u32[]{:S(2)}) collective-permute-start(f32[64,1280]{1,0:T(8,128)S(1)} %get-tuple-element.33), channel_id=1, source_target_pairs={{0,56},{8,32},{16,40},{24,48},{32,24},{40,0},{48,8},{56,16},{1,57}... | collective-permute-start | bytes 983048 | tf_op jit(solution)/shard_map/ppermute | solution.py:456
  20.9 21.0 %collective-permute-start.5 = (f32[64,1280]{1,0:T(8,128)S(1)}, f32[64,1280]{1,0:T(8,128)S(1)}, u32[]{:S(2)}, u32[]{:S(2)}) collective-permute-start(f32[64,1280]{1,0:T(8,128)S(1)} %get-tuple-element.34), channel_id=1, source_target_pairs={{0,16},{8,24},{16,0},{24,8},{32,48},{40,56},{48,32},{56,40},{1,17}... | collective-permute-start | bytes 983048 | tf_op jit(solution)/shard_map/ppermute | solution.py:456
  22.7 27.0 %collective-permute-start.6 = (f32[64,1280]{1,0:T(8,128)S(1)}, f32[64,1280]{1,0:T(8,128)S(1)}, u32[]{:S(2)}, u32[]{:S(2)}) collective-permute-start(f32[64,1280]{1,0:T(8,128)S(1)} %get-tuple-element.35), channel_id=1, source_target_pairs={{0,48},{8,56},{16,32},{24,40},{32,16},{40,24},{48,0},{56,8},{1,49}... | collective-permute-start | bytes 983048 | tf_op jit(solution)/shard_map/ppermute | solution.py:456
  35.3 33.9 %collective-permute-start.21 = (bf16[8,64,256]{2,1,0:T(8,128)(2,1)S(1)}, bf16[8,64,256]{2,1,0:T(8,128)(2,1)S(1)}, u32[]{:S(2)}, u32[]{:S(2)}) collective-permute-start(bf16[8,64,256]{2,1,0:T(8,128)(2,1)S(1)} %get-tuple-element.38), channel_id=1, source_target_pairs={{0,64},{8,72},{16,80},{24,88},{32,96},{40,104},{48,112},{56,120},{... | collective-permute-start | bytes 786440 | tf_op jit(solution)/shard_map/ppermute | solution.py:462
  40.6 35.4 %collective-permute-start.22 = (bf16[8,64,256]{2,1,0:T(8,128)(2,1)S(1)}, bf16[8,64,256]{2,1,0:T(8,128)(2,1)S(1)}, u32[]{:S(2)}, u32[]{:S(2)}) collective-permute-start(bf16[8,64,256]{2,1,0:T(8,128)(2,1)S(1)} %get-tuple-element.39), channel_id=1, source_target_pairs={{0,72},{8,80},{16,88},{24,64},{32,104},{40,112},{48,120},{56,96},{... | collective-permute-start | bytes 786440 | tf_op jit(solution)/shard_map/ppermute | solution.py:462
  49.9 9.4 %collective-permute-start.19 = (bf16[64,1024]{1,0:T(8,128)(2,1)S(1)}, bf16[64,1024]{1,0:T(8,128)(2,1)S(1)}, u32[]{:S(2)}, u32[]{:S(2)}) collective-permute-start(bf16[64,1024]{1,0:T(8,128)(2,1)S(1)} %get-tuple-element.36.q), channel_id=1, source_target_pairs={{0,48},{8,56},{16,32},{24,40},{32,16},{40,24},{48,0},{56,8},{1,49}... | collective-permute-start | bytes 393224 | tf_op jit(solution)/shard_map/ppermute | solution.py:456
  50.0 27.4 %collective-permute-start.17 = (bf16[64,1024]{1,0:T(8,128)(2,1)S(1)}, bf16[64,1024]{1,0:T(8,128)(2,1)S(1)}, u32[]{:S(2)}, u32[]{:S(2)}) collective-permute-start(bf16[64,1024]{1,0:T(8,128)(2,1)S(1)} %get-tuple-element.36.q), channel_id=1, source_target_pairs={{0,16},{8,24},{16,0},{24,8},{32,48},{40,56},{48,32},{56,40},{1,17}... | collective-permute-start | bytes 393224 | tf_op jit(solution)/shard_map/ppermute | solution.py:456
  52.6 40.8 %collective-permute-start.23 = (bf16[8,64,256]{2,1,0:T(8,128)(2,1)S(1)}, bf16[8,64,256]{2,1,0:T(8,128)(2,1)S(1)}, u32[]{:S(2)}, u32[]{:S(2)}) collective-permute-start(bf16[8,64,256]{2,1,0:T(8,128)(2,1)S(1)} %get-tuple-element.40), channel_id=1, source_target_pairs={{0,88},{8,64},{16,72},{24,80},{32,120},{40,96},{48,104},{56,112},{... | collective-permute-start | bytes 786440 | tf_op jit(solution)/shard_map/ppermute | solution.py:462
  59.2 27.3 %collective-permute-start.15 = (bf16[64,1024]{1,0:T(8,128)(2,1)S(1)}, bf16[64,1024]{1,0:T(8,128)(2,1)S(1)}, u32[]{:S(2)}, u32[]{:S(2)}) collective-permute-start(bf16[64,1024]{1,0:T(8,128)(2,1)S(1)} %get-tuple-element.36.q), channel_id=1, source_target_pairs={{0,56},{8,32},{16,40},{24,48},{32,24},{40,0},{48,8},{56,16},{1,57}... | collective-permute-start | bytes 393224 | tf_op jit(solution)/shard_map/ppermute | solution.py:456
  69.2 31.4 %collective-permute-start.24 = (bf16[8,64,256]{2,1,0:T(8,128)(2,1)S(1)}, bf16[8,64,256]{2,1,0:T(8,128)(2,1)S(1)}, u32[]{:S(2)}, u32[]{:S(2)}) collective-permute-start(bf16[8,64,256]{2,1,0:T(8,128)(2,1)S(1)} %get-tuple-element.41), channel_id=1, source_target_pairs={{0,96},{8,104},{16,112},{24,120},{32,64},{40,72},{48,80},{56,88},{... | collective-permute-start | bytes 786440 | tf_op jit(solution)/shard_map/ppermute | solution.py:462
  76.0 26.0 %collective-permute-start.25 = (bf16[8,64,256]{2,1,0:T(8,128)(2,1)S(1)}, bf16[8,64,256]{2,1,0:T(8,128)(2,1)S(1)}, u32[]{:S(2)}, u32[]{:S(2)}) collective-permute-start(bf16[8,64,256]{2,1,0:T(8,128)(2,1)S(1)} %get-tuple-element.42), channel_id=1, source_target_pairs={{0,104},{8,112},{16,120},{24,96},{32,72},{40,80},{48,88},{56,64},{... | collective-permute-start | bytes 786440 | tf_op jit(solution)/shard_map/ppermute | solution.py:462
  77.3 16.3 %collective-permute-start.9 = (bf16[64,1024]{1,0:T(8,128)(2,1)S(1)}, bf16[64,1024]{1,0:T(8,128)(2,1)S(1)}, u32[]{:S(2)}, u32[]{:S(2)}) collective-permute-start(bf16[64,1024]{1,0:T(8,128)(2,1)S(1)} %get-tuple-element.36.q), channel_id=1, source_target_pairs={{0,24},{8,0},{16,8},{24,16},{32,56},{40,32},{48,40},{56,48},{1,25}... | collective-permute-start | bytes 393224 | tf_op jit(solution)/shard_map/ppermute | solution.py:456
  86.5 16.8 %collective-permute-start.7 = (bf16[64,1024]{1,0:T(8,128)(2,1)S(1)}, bf16[64,1024]{1,0:T(8,128)(2,1)S(1)}, u32[]{:S(2)}, u32[]{:S(2)}) collective-permute-start(bf16[64,1024]{1,0:T(8,128)(2,1)S(1)} %get-tuple-element.36.q), channel_id=1, source_target_pairs={{0,8},{8,16},{16,24},{24,0},{32,40},{40,48},{48,56},{56,32},{1,9},... | collective-permute-start | bytes 393224 | tf_op jit(solution)/shard_map/ppermute | solution.py:456
  93.4 18.0 %collective-permute-start.13 = (bf16[64,1024]{1,0:T(8,128)(2,1)S(1)}, bf16[64,1024]{1,0:T(8,128)(2,1)S(1)}, u32[]{:S(2)}, u32[]{:S(2)}) collective-permute-start(bf16[64,1024]{1,0:T(8,128)(2,1)S(1)} %get-tuple-element.36.q), channel_id=1, source_target_pairs={{0,40},{8,48},{16,56},{24,32},{32,8},{40,16},{48,24},{56,0},{1,41}... | collective-permute-start | bytes 393224 | tf_op jit(solution)/shard_map/ppermute | solution.py:456
  93.7 21.4 %collective-permute-start.11 = (bf16[64,1024]{1,0:T(8,128)(2,1)S(1)}, bf16[64,1024]{1,0:T(8,128)(2,1)S(1)}, u32[]{:S(2)}, u32[]{:S(2)}) collective-permute-start(bf16[64,1024]{1,0:T(8,128)(2,1)S(1)} %get-tuple-element.36.q), channel_id=1, source_target_pairs={{0,32},{8,40},{16,48},{24,56},{32,0},{40,8},{48,16},{56,24},{1,33}... | collective-permute-start | bytes 393224 | tf_op jit(solution)/shard_map/ppermute | solution.py:456
  100.7 27.9 %collective-permute-start.26 = (bf16[8,64,256]{2,1,0:T(8,128)(2,1)S(1)}, bf16[8,64,256]{2,1,0:T(8,128)(2,1)S(1)}, u32[]{:S(2)}, u32[]{:S(2)}) collective-permute-start(bf16[8,64,256]{2,1,0:T(8,128)(2,1)S(1)} %get-tuple-element.43), channel_id=1, source_target_pairs={{0,120},{8,96},{16,104},{24,112},{32,88},{40,64},{48,72},{56,80},{... | collective-permute-start | bytes 786440 | tf_op jit(solution)/shard_map/ppermute | solution.py:462
  102.0 27.0 %collective-permute-start.27 = (bf16[8,64,256]{2,1,0:T(8,128)(2,1)S(1)}, bf16[8,64,256]{2,1,0:T(8,128)(2,1)S(1)}, u32[]{:S(2)}, u32[]{:S(2)}) collective-permute-start(bf16[8,64,256]{2,1,0:T(8,128)(2,1)S(1)} %get-tuple-element.44), channel_id=1, source_target_pairs={{0,80},{8,88},{16,64},{24,72},{32,112},{40,120},{48,96},{56,104},{... | collective-permute-start | bytes 786440 | tf_op jit(solution)/shard_map/ppermute | solution.py:462
  103.3 29.2 %collective-permute-start.28 = (bf16[8,64,256]{2,1,0:T(8,128)(2,1)S(1)}, bf16[8,64,256]{2,1,0:T(8,128)(2,1)S(1)}, u32[]{:S(2)}, u32[]{:S(2)}) collective-permute-start(bf16[8,64,256]{2,1,0:T(8,128)(2,1)S(1)} %get-tuple-element.45), channel_id=1, source_target_pairs={{0,112},{8,120},{16,96},{24,104},{32,80},{40,88},{48,64},{56,72},{... | collective-permute-start | bytes 786440 | tf_op jit(solution)/shard_map/ppermute | solution.py:462
  111.4 21.1 %collective-permute-start.8 = (bf16[64,1152]{1,0:T(8,128)(2,1)S(1)}, bf16[64,1152]{1,0:T(8,128)(2,1)S(1)}, u32[]{:S(2)}, u32[]{:S(2)}) collective-permute-start(bf16[64,1152]{1,0:T(8,128)(2,1)S(1)} %attend_1.1), channel_id=1, source_target_pairs={{0,24},{8,0},{16,8},{24,16},{32,56},{40,32},{48,40},{56,48},{1,25}... | collective-permute-start | bytes 442376 | tf_op jit(solution)/shard_map/ppermute | solution.py:456
  115.1 18.7 %collective-permute-start.10 = (bf16[64,1152]{1,0:T(8,128)(2,1)S(1)}, bf16[64,1152]{1,0:T(8,128)(2,1)S(1)}, u32[]{:S(2)}, u32[]{:S(2)}) collective-permute-start(bf16[64,1152]{1,0:T(8,128)(2,1)S(1)} %attend_2.1), channel_id=1, source_target_pairs={{0,8},{8,16},{16,24},{24,0},{32,40},{40,48},{48,56},{56,32},{1,9},... | collective-permute-start | bytes 442376 | tf_op jit(solution)/shard_map/ppermute | solution.py:456
  128.6 13.9 %copy-start.2 = (s32[64]{0:T(128)S(1)}, s32[64]{0:T(128)}, u32[]{:S(2)}) copy-start(s32[64]{0:T(128)} %lengths.1) | copy-start | bytes 772
  128.6 13.8 %collective-permute-start.12 = (bf16[64,1152]{1,0:T(8,128)(2,1)S(1)}, bf16[64,1152]{1,0:T(8,128)(2,1)S(1)}, u32[]{:S(2)}, u32[]{:S(2)}) collective-permute-start(bf16[64,1152]{1,0:T(8,128)(2,1)S(1)} %attend_3.1), channel_id=1, source_target_pairs={{0,32},{8,40},{16,48},{24,56},{32,0},{40,8},{48,16},{56,24},{1,33}... | collective-permute-start | bytes 442376 | tf_op jit(solution)/shard_map/ppermute | solution.py:456
  129.0 13.4 %collective-permute-start.14 = (bf16[64,1152]{1,0:T(8,128)(2,1)S(1)}, bf16[64,1152]{1,0:T(8,128)(2,1)S(1)}, u32[]{:S(2)}, u32[]{:S(2)}) collective-permute-start(bf16[64,1152]{1,0:T(8,128)(2,1)S(1)} %attend_4.1), channel_id=1, source_target_pairs={{0,56},{8,32},{16,40},{24,48},{32,24},{40,0},{48,8},{56,16},{1,57}... | collective-permute-start | bytes 442376 | tf_op jit(solution)/shard_map/ppermute | solution.py:456
  132.5 9.9 %collective-permute-start.16 = (bf16[64,1152]{1,0:T(8,128)(2,1)S(1)}, bf16[64,1152]{1,0:T(8,128)(2,1)S(1)}, u32[]{:S(2)}, u32[]{:S(2)}) collective-permute-start(bf16[64,1152]{1,0:T(8,128)(2,1)S(1)} %attend_5.1), channel_id=1, source_target_pairs={{0,40},{8,48},{16,56},{24,32},{32,8},{40,16},{48,24},{56,0},{1,41}... | collective-permute-start | bytes 442376 | tf_op jit(solution)/shard_map/ppermute | solution.py:456
  132.5 9.9 %collective-permute-start.18 = (bf16[64,1152]{1,0:T(8,128)(2,1)S(1)}, bf16[64,1152]{1,0:T(8,128)(2,1)S(1)}, u32[]{:S(2)}, u32[]{:S(2)}) collective-permute-start(bf16[64,1152]{1,0:T(8,128)(2,1)S(1)} %attend_6.1), channel_id=1, source_target_pairs={{0,16},{8,24},{16,0},{24,8},{32,48},{40,56},{48,32},{56,40},{1,17}... | collective-permute-start | bytes 442376 | tf_op jit(solution)/shard_map/ppermute | solution.py:456
  133.8 8.6 %collective-permute-start.20 = (bf16[64,1152]{1,0:T(8,128)(2,1)S(1)}, bf16[64,1152]{1,0:T(8,128)(2,1)S(1)}, u32[]{:S(2)}, u32[]{:S(2)}) collective-permute-start(bf16[64,1152]{1,0:T(8,128)(2,1)S(1)} %attend_7.1), channel_id=1, source_target_pairs={{0,48},{8,56},{16,32},{24,40},{32,16},{40,24},{48,0},{56,8},{1,49}... | collective-permute-start | bytes 442376 | tf_op jit(solution)/shard_map/ppermute | solution.py:456
  146.4 7.7 %collective-permute-start.35 = (bf16[64,1024]{1,0:T(8,128)(2,1)S(1)}, bf16[64,1024]{1,0:T(8,128)(2,1)S(1)}, u32[]{:S(2)}, u32[]{:S(2)}) collective-permute-start(bf16[64,1024]{1,0:T(8,128)(2,1)S(1)} %get-tuple-element.46.rest_0_), channel_id=1, source_target_pairs={{0,48},{8,56},{16,32},{24,40},{32,16},{40,24},{48,0},{56,8},{1,49}... | collective-permute-start | bytes 393224 | tf_op jit(solution)/shard_map/ppermute | solution.py:456
  148.5 9.2 %collective-permute-start.34 = (bf16[64,1024]{1,0:T(8,128)(2,1)S(1)}, bf16[64,1024]{1,0:T(8,128)(2,1)S(1)}, u32[]{:S(2)}, u32[]{:S(2)}) collective-permute-start(bf16[64,1024]{1,0:T(8,128)(2,1)S(1)} %get-tuple-element.46.rest_0_), channel_id=1, source_target_pairs={{0,16},{8,24},{16,0},{24,8},{32,48},{40,56},{48,32},{56,40},{1,17}... | collective-permute-start | bytes 393224 | tf_op jit(solution)/shard_map/ppermute | solution.py:456
  150.3 7.4 %collective-permute-start.33 = (bf16[64,1024]{1,0:T(8,128)(2,1)S(1)}, bf16[64,1024]{1,0:T(8,128)(2,1)S(1)}, u32[]{:S(2)}, u32[]{:S(2)}) collective-permute-start(bf16[64,1024]{1,0:T(8,128)(2,1)S(1)} %get-tuple-element.46.rest_0_), channel_id=1, source_target_pairs={{0,56},{8,32},{16,40},{24,48},{32,24},{40,0},{48,8},{56,16},{1,57}... | collective-permute-start | bytes 393224 | tf_op jit(solution)/shard_map/ppermute | solution.py:456
  153.8 8.0 %collective-permute-start.32 = (bf16[64,1024]{1,0:T(8,128)(2,1)S(1)}, bf16[64,1024]{1,0:T(8,128)(2,1)S(1)}, u32[]{:S(2)}, u32[]{:S(2)}) collective-permute-start(bf16[64,1024]{1,0:T(8,128)(2,1)S(1)} %get-tuple-element.46.rest_0_), channel_id=1, source_target_pairs={{0,40},{8,48},{16,56},{24,32},{32,8},{40,16},{48,24},{56,0},{1,41}... | collective-permute-start | bytes 393224 | tf_op jit(solution)/shard_map/ppermute | solution.py:456
  153.8 8.0 %collective-permute-start.31 = (bf16[64,1024]{1,0:T(8,128)(2,1)S(1)}, bf16[64,1024]{1,0:T(8,128)(2,1)S(1)}, u32[]{:S(2)}, u32[]{:S(2)}) collective-permute-start(bf16[64,1024]{1,0:T(8,128)(2,1)S(1)} %get-tuple-element.46.rest_0_), channel_id=1, source_target_pairs={{0,32},{8,40},{16,48},{24,56},{32,0},{40,8},{48,16},{56,24},{1,33}... | collective-permute-start | bytes 393224 | tf_op jit(solution)/shard_map/ppermute | solution.py:456
  154.1 7.9 %collective-permute-start.30 = (bf16[64,1024]{1,0:T(8,128)(2,1)S(1)}, bf16[64,1024]{1,0:T(8,128)(2,1)S(1)}, u32[]{:S(2)}, u32[]{:S(2)}) collective-permute-start(bf16[64,1024]{1,0:T(8,128)(2,1)S(1)} %get-tuple-element.46.rest_0_), channel_id=1, source_target_pairs={{0,24},{8,0},{16,8},{24,16},{32,56},{40,32},{48,40},{56,48},{1,25}... | collective-permute-start | bytes 393224 | tf_op jit(solution)/shard_map/ppermute | solution.py:456
  157.7 5.2 %collective-permute-start.29 = (bf16[64,1024]{1,0:T(8,128)(2,1)S(1)}, bf16[64,1024]{1,0:T(8,128)(2,1)S(1)}, u32[]{:S(2)}, u32[]{:S(2)}) collective-permute-start(bf16[64,1024]{1,0:T(8,128)(2,1)S(1)} %get-tuple-element.46.rest_0_), channel_id=1, source_target_pairs={{0,8},{8,16},{16,24},{24,0},{32,40},{40,48},{48,56},{56,32},{1,9},... | collective-permute-start | bytes 393224 | tf_op jit(solution)/shard_map/ppermute | solution.py:456
  166.9 9.4 %collective-permute-start.36 = (bf16[256,2048]{1,0:T(8,128)(2,1)S(1)}, bf16[256,2048]{1,0:T(8,128)(2,1)S(1)}, u32[]{:S(2)}, u32[]{:S(2)}) collective-permute-start(bf16[256,2048]{1,0:T(8,128)(2,1)S(1)} %other_half.1), channel_id=1, source_target_pairs={{0,1},{1,0},{2,3},{3,2},{4,5},{5,4},{6,7},{7,6},{8,9},{9,8},{10,11... | collective-permute-start | bytes 3145736 | tf_op jit(solution)/shard_map/ppermute | solution.py:475
  180.4 8.9 %collective-permute-start.37 = (bf16[64,2048]{1,0:T(8,128)(2,1)S(1)}, bf16[64,2048]{1,0:T(8,128)(2,1)S(1)}, u32[]{:S(2)}, u32[]{:S(2)}) collective-permute-start(bf16[64,2048]{1,0:T(8,128)(2,1)S(1)} %get-tuple-element.48), channel_id=1, source_target_pairs={{0,2},{1,3},{2,4},{3,5},{4,6},{5,7},{6,0},{7,1},{8,10},{9,11},{10,... | collective-permute-start | bytes 786440 | tf_op jit(solution)/shard_map/ppermute | solution.py:478
  181.8 14.3 %collective-permute-start.38 = (bf16[64,2048]{1,0:T(8,128)(2,1)S(1)}, bf16[64,2048]{1,0:T(8,128)(2,1)S(1)}, u32[]{:S(2)}, u32[]{:S(2)}) collective-permute-start(bf16[64,2048]{1,0:T(8,128)(2,1)S(1)} %get-tuple-element.49), channel_id=1, source_target_pairs={{0,4},{1,5},{2,6},{3,7},{4,0},{5,1},{6,2},{7,3},{8,12},{9,13},{10,... | collective-permute-start | bytes 786440 | tf_op jit(solution)/shard_map/ppermute | solution.py:478
  184.4 11.7 %collective-permute-start.39 = (bf16[64,2048]{1,0:T(8,128)(2,1)S(1)}, bf16[64,2048]{1,0:T(8,128)(2,1)S(1)}, u32[]{:S(2)}, u32[]{:S(2)}) collective-permute-start(bf16[64,2048]{1,0:T(8,128)(2,1)S(1)} %get-tuple-element.50), channel_id=1, source_target_pairs={{0,6},{1,7},{2,0},{3,1},{4,2},{5,3},{6,4},{7,5},{8,14},{9,15},{10,... | collective-permute-start | bytes 786440 | tf_op jit(solution)/shard_map/ppermute | solution.py:478

commit v2 on v1

v2 whole, which is shorter than its diff:
```python
import functools
import math

import jax
import jax.numpy as jnp
from jax import lax
from jax.experimental import pallas as pl
from jax.experimental.pallas import tpu as pltpu
from jax.sharding import PartitionSpec as P

HD = 128
HEADS = 8
STATE = (HEADS + 1) * HD
CTX = 8
ROW = 64
STEPS = ((0, 0), (1, 0), (0, 1), (0, 3), (1, 1), (1, 3), (0, 2), (1, 2))
COEF = HD ** -0.5 * math.log2(math.e)
BF = jnp.bfloat16
F32 = jnp.float32
F16 = jnp.float16
LIFT = 64.0
SMEM = pl.BlockSpec(memory_space=pltpu.SMEM)
VMEM = pl.BlockSpec(memory_space=pltpu.VMEM)
ANY = pl.BlockSpec(memory_space=pl.ANY)
PREFILL, ME, TP = 0, 1, 2


def peer(place, step, sign):
    flip, turn = step
    return (place // 4 ^ flip) * 4 + (place + sign * turn) % 4


def place_here():
    return jnp.stack([1 - lax.axis_index("group"), lax.axis_index("ctx"), lax.axis_index("tp")]).astype(jnp.int32)


def params(limit=24 << 20, **more):
    return pltpu.CompilerParams(vmem_limit_bytes=limit, **more)


def nbytes(*arrays):
    return sum(math.prod(a.shape) * a.dtype.itemsize for a in arrays)


def pages_for(slots, holder, target, found):
    origin = lax.bitwise_xor(holder, 4)

    def look(i, n):
        slot = slots[origin * 64 + i]
        there = lax.shift_right_logical(slot, 6) == target

        @pl.when(there)
        def _():
            found(n, i, lax.bitwise_and(slot, 63))

        return n + there.astype(jnp.int32)

    lax.fori_loop(0, 64, look, jnp.int32(0), unroll=4)


def places(meta, slots, spots):
    me = meta[ME]
    for step in range(CTX):
        def coming(n, page, slot):
            spots[step * 8 + n] = slot

        def leaving(n, page, slot):
            spots[64 + step * 8 + n] = page

        pages_for(slots, peer(me, STEPS[step], 1), me, coming)
        pages_for(slots, me, peer(me, STEPS[step], -1), leaving)


def weigh(scores, values, state):
    m, l, acc = state
    new = jnp.maximum(m, jnp.max(scores, axis=1, keepdims=True))
    fade = jnp.exp2((m - new) * COEF)
    weights = jnp.exp2((scores - new) * COEF)
    lanes = [weights[:, x : x + HD] for x in range(0, weights.shape[1], HD)]
    l = l * fade + functools.reduce(jnp.add, lanes)
    acc = acc * fade + jnp.dot(weights.astype(BF), values, preferred_element_type=F32)
    return (new, l, acc)


def attend_rows(meta, owner, block, q, kv, mine, out, q2, pair):
    contract = (((1,), (1,)), ((), ()))
    big = HEADS * ROW
    if q is not None:
        for h in range(HEADS):
            q2[h * ROW : (h + 1) * ROW, :] = q[:, h * HD : (h + 1) * HD]
    pair[:ROW, :] = mine[:, HEADS * HD :]
    pair[ROW:, :] = jnp.zeros((HD - ROW, 2 * HD), BF)
    ahead = (owner - meta[ME]) * ROW
    scores = lax.dot_general(q2[...], pair[:, :HD], contract, preferred_element_type=F32)
    token = lax.bitwise_and(lax.broadcasted_iota(jnp.int32, scores.shape, 0), ROW - 1)
    key = lax.broadcasted_iota(jnp.int32, scores.shape, 1)
    scores = jnp.where((key <= token + ahead) & (key < ROW), scores, -1e30)
    state = (
        jnp.full((big, 1), -1e30, F32),
        jnp.zeros((big, HD), F32),
        jnp.zeros((big, HD), F32),
    )
    state = weigh(scores, pair[:, HD:], state)
    for first in range(0, kv.shape[0], block):
        some = slice(first, first + block)
        scores = lax.dot_general(q2[...], kv[some, :HD], contract, preferred_element_type=F32)
        state = weigh(scores, kv[some, HD:], state)
    m, l, acc = state
    l = jnp.sum(l, axis=1, keepdims=True)
    mixed = acc * (1.0 / l)
    level = m * COEF + jnp.log2(l)
    high = level.astype(BF).astype(F32)
    rest = level - high
    mid = rest.astype(BF).astype(F32)
    low = rest - mid
    lane = lax.broadcasted_iota(jnp.int32, (ROW, HD), 1)
    stats = jnp.zeros((ROW, HD), F32)
    for h in range(HEADS):
        rows = slice(h * ROW, (h + 1) * ROW)
        out[:, h * HD : (h + 1) * HD] = mixed[rows].astype(out.dtype)
        stats = jnp.where(lane == h, high[rows], stats)
        stats = jnp.where(lane == 8 + h, mid[rows], stats)
        stats = jnp.where(lane == 16 + h, low[rows], stats)
    out[:, HEADS * HD :] = stats.astype(out.dtype)


def plan_kernel(meta, slots, spots):
    @pl.when(meta[PREFILL] == 0)
    def _():
        places(meta, slots, spots)


def plan(meta, slots):
    return pl.pallas_call(
        plan_kernel,
        in_specs=[SMEM] * 2,
        out_specs=SMEM,
        out_shape=jax.ShapeDtypeStruct((128,), jnp.int32),
        compiler_params=params(),
        cost_estimate=pl.CostEstimate(flops=0, bytes_accessed=0, transcendentals=0),
        name="plan",
    )(meta, slots)


def own_kernel(block, meta, mine, kv, after, out, q2, pair):
    @pl.when(meta[PREFILL] == 1)
    def _():
        attend_rows(meta, meta[ME], block, mine, kv, mine, out, q2, pair)


def attend_own(meta, mine, pages, after, block=2048):
    big = HEADS * ROW
    return pl.pallas_call(
        functools.partial(own_kernel, block),
        in_specs=[SMEM] + [VMEM] * 2 + [ANY],
        out_specs=VMEM,
        out_shape=jax.ShapeDtypeStruct((ROW, STATE), F32),
        scratch_shapes=[pltpu.VMEM((big, HD), BF), pltpu.VMEM((HD, 2 * HD), BF)],
        compiler_params=params(),
        cost_estimate=pl.CostEstimate(flops=1 << 32, bytes_accessed=0, transcendentals=0),
        name="attend_own",
    )(meta, mine, pages, after)


def attend_kernel(steps, block, meta, spots, crossed, kv, mine, *rest):
    queries, outs, (state, q2, pair, sem) = rest[: len(steps)], rest[-len(steps) - 4 : -4], rest[-4:]
    i = pl.program_id(0)

    @pl.when(meta[PREFILL] == 1)
    def _():
        attend_step(meta, steps, block, queries, kv, mine, outs, state, q2, pair)

    @pl.when((meta[PREFILL] == 0) & (i == 0))
    def _():
        fill_pages(steps, spots, crossed, outs, sem)


def attend_step(meta, steps, block, queries, kv, mine, outs, state, q2, pair):
    i = pl.program_id(0)
    owner = jnp.int32(0)
    for n, step in enumerate(steps):
        owner = jnp.where(i == n, peer(meta[ME], STEPS[step], -1), owner)
        @pl.when(i == n)
        def _():
            for h in range(HEADS):
                q2[h * ROW : (h + 1) * ROW, :] = queries[n][:, h * HD : (h + 1) * HD]
    attend_rows(meta, owner, block, None, kv, mine, state, q2, pair)
    for n in range(len(steps)):
        @pl.when(i == n)
        def _():
            outs[n][:, :STATE] = state[...]


def attend_scratch():
    return [
        pltpu.VMEM((ROW, STATE), BF),
        pltpu.VMEM((HEADS * ROW, HD), BF),
        pltpu.VMEM((HD, 2 * HD), BF),
    ]


def attend(steps, meta, spots, crossed, pages, mine, queries, after, block=2048):
    return pl.pallas_call(
        functools.partial(attend_kernel, steps, block),
        grid=(len(steps),),
        in_specs=[SMEM] * 2 + [ANY] + [VMEM] * (2 + len(queries)) + [ANY] * len(after),
        out_specs=[VMEM] * len(steps),
        out_shape=[jax.ShapeDtypeStruct((ROW, 16 * HD), BF)] * len(steps),
        scratch_shapes=attend_scratch() + [pltpu.SemaphoreType.DMA((len(steps), 8))],
        compiler_params=params(),
        cost_estimate=pl.CostEstimate(flops=len(steps) << 32, bytes_accessed=0, transcendentals=0),
        name=f"attend_{steps[0]}",
    )(meta, spots, crossed, pages, mine, *queries, *after)


def start_kernel(steps, block, meta, kv, mine, *rest):
    queries, outs, (pool, state, q2, pair, sem) = rest[: len(steps)], rest[-len(steps) - 5 : -5], rest[-5:]
    i = pl.program_id(0)

    @pl.when(meta[PREFILL] == 1)
    def _():
        keep = pltpu.make_async_copy(kv, pool, sem)

        @pl.when(i == 0)
        def _():
            keep.start()

        attend_step(meta, steps, block, queries, kv, mine, outs, state, q2, pair)

        @pl.when(i == len(steps) - 1)
        def _():
            keep.wait()


def attend_first(steps, meta, pages, mine, queries, block=2048):
    return pl.pallas_call(
        functools.partial(start_kernel, steps, block),
        grid=(len(steps),),
        in_specs=[SMEM] + [VMEM] * (2 + len(queries)),
        out_specs=[VMEM] * len(steps) + [ANY],
        out_shape=[jax.ShapeDtypeStruct((ROW, 16 * HD), BF)] * len(steps)
        + [jax.ShapeDtypeStruct(pages.shape, BF)],
        scratch_shapes=attend_scratch() + [pltpu.SemaphoreType.DMA],
        compiler_params=params(),
        cost_estimate=pl.CostEstimate(flops=0, bytes_accessed=0, transcendentals=0),
        name=f"attend_{steps[0]}",
    )(meta, pages, mine, *queries)


def fill_pages(steps, spots, crossed, outs, sem):
    copies = [
        pltpu.make_async_copy(
            crossed.at[spots[64 + step * 8 + p]], outs[n].at[:, p * 2 * HD : (p + 1) * 2 * HD], sem.at[n, p]
        )
        for n, step in enumerate(steps)
        for p in range(8)
    ]
    for copy in copies:
        copy.start()
    for copy in copies:
        copy.wait()


def fill_kernel(steps, meta, spots, crossed, *rest):
    outs, sem = rest[len(steps) : -1], rest[-1]

    @pl.when(meta[PREFILL] == 0)
    def _():
        fill_pages(steps, spots, crossed, outs, sem)


def fill(steps, meta, spots, crossed, values):
    return pl.pallas_call(
        functools.partial(fill_kernel, steps),
        in_specs=[SMEM] * 2 + [ANY] + [VMEM] * len(steps),
        out_specs=[VMEM] * len(steps),
        out_shape=[jax.ShapeDtypeStruct(value.shape, BF) for value in values],
        scratch_shapes=[pltpu.SemaphoreType.DMA((len(steps), 8))],
        input_output_aliases={3 + n: n for n in range(len(steps))},
        compiler_params=params(),
        cost_estimate=pl.CostEstimate(flops=0, bytes_accessed=0, transcendentals=0),
        name=f"fill_{steps[0]}",
    )(meta, spots, crossed, *values)


def finish_kernel(meta, spots, lengths, mine, *rest):
    came, (pages, crossed, _, heads, pool, held, relaid, q3, o3, sems) = rest[:CTX], rest[CTX:]
    contract = (((1,), (1,)), ((), ()))

    @pl.when(meta[PREFILL] == 1)
    def _():
        levels = []
        for j in range(CTX):
            stats = came[j][:, HEADS * HD : STATE].astype(F32)
            levels.append(stats + pltpu.roll(stats, HD - 8, 1) + pltpu.roll(stats, HD - 16, 1))
        top = functools.reduce(jnp.maximum, levels)
        parts = [jnp.exp2(level - top) for level in levels]
        share = 1.0 / functools.reduce(jnp.add, parts)
        parts = [part * share for part in parts]
        for h in range(HEADS):
            cols = slice(h * HD, (h + 1) * HD)
            mixed = [came[j][:, cols].astype(F32) * parts[j][:, h : h + 1] for j in range(CTX)]
            heads[:, cols] = functools.reduce(jnp.add, mixed).astype(BF)

    @pl.when(meta[PREFILL] == 0)
    def _():
        load = pltpu.make_async_copy(pages, held, sems.at[0])
        load.start()
        for n in range(8):
            page = crossed.at[spots[64 + n]]
            pltpu.make_async_copy(page, relaid.at[spots[n]], sems.at[1]).start()
        for step in range(1, CTX):
            for n in range(8):
                relaid[spots[step * 8 + n]] = came[step][:, n * 2 * HD : (n + 1) * 2 * HD]
        for h in range(HEADS):
            q3[:, h, :] = mine[:, h * HD : (h + 1) * HD].astype(F32)
        load.wait()
        pltpu.make_async_copy(pages.at[pl.ds(0, 8)], relaid.at[pl.ds(0, 8)], sems.at[1]).wait()
        keep = pltpu.make_async_copy(relaid, pool, sems.at[2])
        keep.start()
        at_once = 8
        lane = lax.broadcasted_iota(jnp.int32, (HEADS, 2 * ROW), 1)

        def some(i, _):
            first = i * at_once
            own = mine[pl.ds(pl.multiple_of(first, at_once), at_once), HEADS * HD :].astype(F32)
            scores, own_scores, values = [], [], []
            for r in range(at_once):
                both = jnp.concatenate([held[first + r], relaid[first + r]], axis=0)
                queries = q3[first + r]
                s = lax.dot_general(queries.astype(BF), both[:, :HD], contract, preferred_element_type=F32)
                seen = (lane < lengths[first + r]) | (lane >= ROW)
                scores.append(jnp.where(seen, s, -1e30))
                own_scores.append(jnp.sum(queries * own[r : r + 1, :HD], axis=1, keepdims=True))
                values.append(both[:, HD:])
            scores = jnp.concatenate(scores, axis=0)
            own_scores = jnp.concatenate(own_scores, axis=0)
            top = jnp.maximum(jnp.max(scores, axis=1, keepdims=True), own_scores)
            weights = jnp.exp2((scores - top) * COEF)
            own_weights = jnp.exp2((own_scores - top) * COEF)
            total = jnp.sum(weights, axis=1, keepdims=True) + own_weights
            weights = weights.astype(BF)
            own_weights = own_weights.astype(BF).astype(F32)
            for r in range(at_once):
                rows = slice(r * HEADS, (r + 1) * HEADS)
                mixed = jnp.dot(weights[rows], values[r], preferred_element_type=F32)
                mixed = mixed + own_weights[rows] * own[r : r + 1, HD:]
                o3[first + r] = mixed / total[rows]
            return 0

        lax.fori_loop(0, ROW // at_once, some, 0)
        for h in range(HEADS):
            heads[:, h * HD : (h + 1) * HD] = o3[:, h, :].astype(BF)
        keep.wait()


def finish(meta, spots, lengths, mine, came, pages, crossed, pool):
    return pl.pallas_call(
        finish_kernel,
        in_specs=[SMEM] * 3 + [VMEM] * (1 + CTX) + [ANY] * 3,
        out_specs=[VMEM, ANY],
        out_shape=[
            jax.ShapeDtypeStruct((ROW, HEADS * HD), BF),
            jax.ShapeDtypeStruct(pool.shape, BF),
        ],
        scratch_shapes=[
            pltpu.VMEM(pool.shape, BF),
            pltpu.VMEM(pool.shape, BF),
            pltpu.VMEM((ROW, HEADS, HD), F32),
            pltpu.VMEM((ROW, HEADS, HD), F32),
            pltpu.SemaphoreType.DMA((3,)),
        ],
        input_output_aliases={6 + CTX: 1},
        compiler_params=params(),
        cost_estimate=pl.CostEstimate(flops=1 << 24, bytes_accessed=3 * nbytes(pool), transcendentals=1 << 16),
        name="finish",
    )(meta, spots, lengths, mine, *came, pages, crossed, pool)


def gather_rows(meta, chunks, rows, wanted):
    for s in range(CTX):
        origin = peer(meta[ME], STEPS[s], -1)
        sends = lax.bitwise_xor(origin, meta[TP]) & 1
        turn = (origin // 2 + 4 - meta[TP] // 2) % 4

        @pl.when(sends == wanted)
        def _():
            rows[pl.ds(pl.multiple_of(turn * ROW, ROW), ROW), :] = chunks[s][...]


def other_half_kernel(block, meta, *rest):
    chunks, w, out, rows = rest[:CTX], *rest[CTX:]
    gather_rows(meta, chunks, rows, 1)
    for n in range(0, w.shape[1], block):
        out[:, n : n + block] = jnp.dot(rows[...], w[:, n : n + block], preferred_element_type=F32)


def own_half_kernel(block, meta, *rest):
    chunks, w, out, rows = rest[:CTX], *rest[CTX:]
    gather_rows(meta, chunks, rows, 0)
    for n in range(0, w.shape[1], block):
        out[:, n : n + block] = jnp.dot(rows[...], w[:, n : n + block], preferred_element_type=F32)


def pair_kernel(own, came, *outs):
    for p in range(4):
        rows = slice(p * ROW, (p + 1) * ROW)
        outs[p][...] = (own[rows] + came[rows]).astype(outs[p].dtype)


def pair_sum(own, came):
    wide = own.shape[1]
    return pl.pallas_call(
        pair_kernel,
        in_specs=[VMEM] * 2,
        out_specs=[VMEM] * 4,
        out_shape=[jax.ShapeDtypeStruct((ROW, wide), F32 if p == 0 else BF) for p in range(4)],
        compiler_params=params(),
        cost_estimate=pl.CostEstimate(flops=1 << 19, bytes_accessed=nbytes(own, came), transcendentals=0),
        name="pair_sum",
    )(own, came)


def half(kernel, name, meta, chunks, w_out, block=512):
    depth, wide = w_out.shape
    return pl.pallas_call(
        functools.partial(kernel, block),
        in_specs=[SMEM] + [VMEM] * (CTX + 1),
        out_specs=VMEM,
        out_shape=jax.ShapeDtypeStruct((4 * ROW, wide), F32),
        scratch_shapes=[pltpu.VMEM((4 * ROW, depth), BF)],
        compiler_params=params(),
        cost_estimate=pl.CostEstimate(
            flops=8 * ROW * depth * wide, bytes_accessed=nbytes(w_out), transcendentals=0
        ),
        name=name,
    )(meta, *chunks, w_out)


def last_kernel(a, b, c, d, out):
    out[...] = (a[...] + b[...].astype(F32) + c[...].astype(F32) + d[...].astype(F32)).astype(BF)


def last_sum(parts):
    return pl.pallas_call(
        last_kernel,
        in_specs=[VMEM] * 4,
        out_specs=VMEM,
        out_shape=jax.ShapeDtypeStruct(parts[0].shape, BF),
        compiler_params=params(),
        cost_estimate=pl.CostEstimate(flops=1 << 19, bytes_accessed=nbytes(*parts), transcendentals=0),
        name="last_sum",
    )(*parts)


def shards(hidden_in, w_query, w_keyval, w_out, kv_pages, page_slot, lengths):
    meta = place_here()
    pages = kv_pages[0]
    flat_pages = pages.reshape(-1, pages.shape[2])

    def both_rings(value, s):
        return lax.ppermute(value, "ctx", [(c, peer(c, STEPS[s], 1)) for c in range(CTX)])

    def back(value, s):
        return lax.ppermute(value, "ctx", [(c, peer(c, STEPS[s], -1)) for c in range(CTX)])

    def across(value):
        pairs = [(c, CTX + (c ^ 4)) for c in range(CTX)]
        return lax.ppermute(value, ("group", "ctx"), pairs + [(b, a) for a, b in pairs])

    def swap(value):
        return lax.all_to_all(value, "ctx", 0, 0, tiled=True)

    crossed = across(pages)
    part = jnp.concatenate(
        [
            (jnp.dot(hidden_in[0], w, preferred_element_type=F32) * LIFT).astype(F16)
            for w in (w_query, w_keyval)
        ],
        axis=1,
    )
    came = swap(part.reshape(CTX, ROW, -1))
    mine = (jnp.sum(came.astype(F32), axis=0) * (1.0 / LIFT)).astype(BF)
    queries = mine[:, : HEADS * HD]
    spots = plan(meta, page_slot)
    groups = ((7, 6), (5, 4), (3, 2), (1,))
    asked = {s: both_rings(queries, s) for steps in groups for s in steps}
    *outs, pool = attend_first(groups[0], meta, flat_pages, mine, [asked[s] for s in groups[0]])
    outs = fill(groups[0], meta, spots, crossed, outs)
    came = {}
    before = []
    for n, steps in enumerate(groups):
        if n > 0:
            ask = [asked[s] for s in steps]
            outs = attend(steps, meta, spots, crossed, flat_pages, mine, ask, [outs[0]] + before)
            before = [came[s] for s in groups[n - 1]]
        for s, value in zip(steps, outs):
            came[s] = back(value, s)
    state = attend_own(meta, mine, flat_pages, outs[0])
    states = [state] + [came[s] for s in range(1, CTX)]
    heads, pool = finish(meta, spots, lengths, mine, states, pages, crossed, pool.reshape(pages.shape))
    gathered = [heads] + [both_rings(heads, s) for s in range(1, CTX)]
    sent = half(other_half_kernel, "other_half", meta, gathered, w_out)
    came = lax.ppermute(sent, "tp", [(t, t ^ 1) for t in range(8)])
    mine = pair_sum(half(own_half_kernel, "own_half", meta, gathered, w_out), came)
    totals = [mine[0]] + [
        lax.ppermute(mine[p], "tp", [(t, (t + 2 * p) % 8) for t in range(8)]) for p in range(1, 4)
    ]
    return (last_sum(totals)[None], pool[None])


def solution(mesh):
    placed = (
        P("group", None, "ctx"),
        P("ctx", "tp"),
        P("ctx", "tp"),
        P("tp", "ctx"),
        P("group", "ctx", None, "tp"),
        P(),
        P("ctx"),
    )
    return jax.shard_map(
        shards,
        mesh=mesh,
        in_specs=placed,
        out_specs=(P("group", "tp", "ctx"), P("group", "ctx", None, "tp")),
        check_vma=False,
    )
```

time: 197 us -> 141 us (0.72)
  Pallas kernels: 78.3 us -> 40.5 us
  starting transfers between devices: 77.8 us -> 51.5 us
  blocking collectives: 0 us -> 21.1 us
  waiting for transfers between devices: 36.1 us -> 17.8 us
  matrix products: 0 us -> 6.45 us
    pallas_call x14 -> x11, Pallas kernels: 77.5 us -> 39.6 us  [the longest x3 20.2 us: attend(): pl.pallas_call(functools.partial(attend_kernel, steps, block), grid=(len(...]
    ppermute x36 -> x22, starting transfers between devices: 65.6 us -> 35.1 us  [the longest x14 20.8 us: both_rings(): lax.ppermute(value, 'ctx', [(c, peer(c, STEPS[s], 1)) for c in range(CTX)])]
    all_to_all x0 -> x1, blocking collectives: none -> 21.1 us  [swap(): return lax.all_to_all(value, 'ctx', 0, 0, tiled=True)]
    ppermute x36 -> x22, waiting for transfers between devices: 23.2 us -> 5.49 us  [the longest x14 5.47 us: both_rings(): lax.ppermute(value, 'ctx', [(c, peer(c, STEPS[s], 1)) for c in range(CTX)])]
    dot_general x0 -> x2, matrix products: none -> 6.45 us  [shards(): jnp.dot(hidden_in[0], w, preferred_element_type=F32) * LIFT]
    ppermute x1, starting transfers between devices: 7.13 us -> 11.4 us  [shards(): came = lax.ppermute(sent, 'tp', [(t, t ^ 1) for t in range(8)])]
  transfers between devices with their start and end apart: 40 -> 26, of which waited for: 11 -> 6; matrix products, arithmetic and copies ran while one was open for 0% -> 5% of each run, Pallas kernels for 30% -> 26%
where the time goes in v2:
time: 141 us
  starting transfers between devices  51.5 us (37%)
  Pallas kernels  40.5 us (29%)
  blocking collectives  21.1 us (15%)
  waiting for transfers between devices  17.8 us (13%)
  matrix products  6.45 us (5%)
  local copies, waits for them, and re-layouts  1.63 us (1%)
    all_to_all x1, blocking collectives, swap(): return lax.all_to_all(value, 'ctx', 0, 0, tiled=True)  21.1 us
    ppermute x14, starting transfers between devices, both_rings(): lax.ppermute(value, 'ctx', [(c, peer(c, STEPS[s], 1)) for c in range(CTX)])  20.8 us
    pallas_call x3, Pallas kernels, attend(): pl.pallas_call(functools.partial(attend_kernel, steps, block), grid=(len(...  20.2 us
    ppermute x1, starting transfers between devices, shards(): came = lax.ppermute(sent, 'tp', [(t, t ^ 1) for t in range(8)])  11.4 us
    ppermute x3, waiting for transfers between devices, shards(): lax.ppermute(mine[p], 'tp', [(t, (t + 2 * p) % 8) for t in range(8)])  10.6 us
    ppermute x7, starting transfers between devices, back(): lax.ppermute(value, 'ctx', [(c, peer(c, STEPS[s], -1)) for c in range(CTX)])  9.7 us
    pallas_call x1, Pallas kernels, attend_first(): pl.pallas_call(functools.partial(start_kernel, steps, block), grid=(len(s...  7.75 us
    dot_general x2, matrix products, shards(): jnp.dot(hidden_in[0], w, preferred_element_type=F32) * LIFT  6.45 us
  transfers between devices with their start and end apart: 26, of which 6 were waited for; matrix products, arithmetic and copies ran while one was open for 5% of the time, Pallas kernels for 26%

profile of v2, /device:TPU:1, one launch (start us, length us, event | category | flops | bytes accessed | tf_op | source)
XLA Modules:
  0.0 140.5 jit_solution(7584443113308629554)
XLA Ops:
  0.6 0.0 copy-start
  0.6 4.7 %collective-permute-start = (bf16[64,64,256]{2,1,0:T(8,128)(2,1)}, bf16[64,64,256]{2,1,0:T(8,128)(2,1)}, u32[]{:S(2)}, u32[]{:S(2)}) collective-permute-start(bf16[64,64,256]{2,1,0:T(8,128)(2,1)} %bitcast.22), channel_id=1, source_target_pairs={{0,96},{8,104},{16,112},{24,120},{32,64},{40,72},{48,80},{56,88},{... | collective-permute-start | bytes 6291464 | tf_op jit(solution)/shard_map/ppermute | solution.py:469
  5.3 1.9 %fusion.9 = f16[512,256]{1,0:T(8,128)(2,1)S(1)} fusion(bf16[2048,256]{1,0:T(8,128)(2,1)} %param.9, bf16[1,512,2048]{2,1,0:T(8,128)(2,1)S(1)} %copy-done), kind=kOutput, calls=%fused_computation.8 | convolution fusion | flops 537133056 | bytes 3407872 | tf_op jit(solution)/shard_map/dot_general | solution.py:477
  7.3 4.5 %multiply_convert_fusion = f16[512,1024]{1,0:T(8,128)(2,1)S(1)} fusion(bf16[2048,1024]{1,0:T(8,128)(2,1)} %param.8, bf16[1,512,2048]{2,1,0:T(8,128)(2,1)S(1)} %copy-done), kind=kOutput, calls=%fused_computation.5 | convolution fusion | flops 2148532224 | bytes 7340032 | tf_op jit(solution)/shard_map/dot_general | solution.py:477
  11.8 0.3 pad_maximum_fusion
  12.1 0.0 copy-start.4
  12.1 21.1 %all_to_all.5 = f16[8,64,1280]{2,1,0:T(8,128)(2,1)S(1)} all-to-all(f16[8,64,1280]{2,1,0:T(8,128)(2,1)S(1)} %bitcast.29), channel_id=1, replica_groups=mesh['group'=2,'ctx'=8,'tp'=8] {'ctx'}, dimensions={0} | all-to-all | bytes 2621440 | tf_op jit(solution)/shard_map/all_to_all | solution.py:472
  33.3 0.2 convert_reduce_fusion
  33.5 1.0 collective-permute-start.7
  34.5 1.9 %collective-permute-start.6 = (bf16[64,1024]{1,0:T(8,128)(2,1)S(1)}, bf16[64,1024]{1,0:T(8,128)(2,1)S(1)}, u32[]{:S(2)}, u32[]{:S(2)}) collective-permute-start(bf16[64,1024]{1,0:T(8,128)(2,1)S(1)} %slice.4), channel_id=1, source_target_pairs={{0,48},{8,56},{16,32},{24,40},{32,16},{40,24},{48,0},{56,8},{1,49}... | collective-permute-start | bytes 393224 | tf_op jit(solution)/shard_map/ppermute | solution.py:462
  36.4 1.6 %collective-permute-start.5 = (bf16[64,1024]{1,0:T(8,128)(2,1)S(1)}, bf16[64,1024]{1,0:T(8,128)(2,1)S(1)}, u32[]{:S(2)}, u32[]{:S(2)}) collective-permute-start(bf16[64,1024]{1,0:T(8,128)(2,1)S(1)} %slice.4), channel_id=1, source_target_pairs={{0,40},{8,48},{16,56},{24,32},{32,8},{40,16},{48,24},{56,0},{1,41}... | collective-permute-start | bytes 393224 | tf_op jit(solution)/shard_map/ppermute | solution.py:462
  37.9 2.0 %collective-permute-start.4 = (bf16[64,1024]{1,0:T(8,128)(2,1)S(1)}, bf16[64,1024]{1,0:T(8,128)(2,1)S(1)}, u32[]{:S(2)}, u32[]{:S(2)}) collective-permute-start(bf16[64,1024]{1,0:T(8,128)(2,1)S(1)} %slice.4), channel_id=1, source_target_pairs={{0,56},{8,32},{16,40},{24,48},{32,24},{40,0},{48,8},{56,16},{1,57}... | collective-permute-start | bytes 393224 | tf_op jit(solution)/shard_map/ppermute | solution.py:462
  39.9 0.1 pad_add_fusion.meta
  40.0 1.2 plan.1.spots
  41.2 0.0 collective-permute-done.7.rest_1_
  41.2 0.1 collective-permute-start.3
  41.3 0.1 collective-permute-done.6.rest_0_
  41.4 2.7 %collective-permute-start.2 = (bf16[64,1024]{1,0:T(8,128)(2,1)S(1)}, bf16[64,1024]{1,0:T(8,128)(2,1)S(1)}, u32[]{:S(2)}, u32[]{:S(2)}) collective-permute-start(bf16[64,1024]{1,0:T(8,128)(2,1)S(1)} %slice.4), channel_id=1, source_target_pairs={{0,24},{8,0},{16,8},{24,16},{32,56},{40,32},{48,40},{56,48},{1,25}... | collective-permute-start | bytes 393224 | tf_op jit(solution)/shard_map/ppermute | solution.py:462
  44.0 1.6 %copy-done.2 = bf16[1,64,64,256]{3,2,1,0:T(8,128)(2,1)S(1)} copy-done((bf16[1,64,64,256]{3,2,1,0:T(8,128)(2,1)S(1)}, bf16[1,64,64,256]{3,2,1,0:T(8,128)(2,1)}, u32[]{:S(2)}) %copy-start.2) | copy-done | bytes 2097176
  45.6 7.7 %attend_7.1 = (bf16[64,2048]{1,0:T(8,128)(2,1)S(1)}, bf16[64,2048]{1,0:T(8,128)(2,1)S(1)}, bf16[4096,256]{1,0:T(8,128)(2,1)}) custom-call(s32[3]{0:T(128)S(1)} %pad_add_fusion.meta, bf16[4096,256]{1,0:T(8,128)(2,1)S(1)} %bitcast.23, bf16[64,1280]{1,0:T(8,128)(2,1)S(1)} %multiply_convert_fusion.1.mine, bf16[64,1024]{1,0:T(8,128)(2,1)S(1)} %collective-permute-done.6.rest_0_, ...), custom_call_target="tpu_custom_call" | custom-call | tf_op jit(solution)/shard_map/attend_7/pallas_call | solution.py:236
  53.4 0.0 collective-permute-done.crossed.rest_9_
  53.4 1.4 collective-permute-start.1
  54.8 0.7 fill_7.1
  55.5 0.0 collective-permute-done.5.rest_1_
  55.5 0.1 collective-permute-start.9
  55.6 0.0 collective-permute-done.4.rest_0_
  55.6 2.9 %collective-permute-start.8 = (bf16[64,2048]{1,0:T(8,128)(2,1)S(1)}, bf16[64,2048]{1,0:T(8,128)(2,1)S(1)}, u32[]{:S(2)}, u32[]{:S(2)}) collective-permute-start(bf16[64,2048]{1,0:T(8,128)(2,1)S(1)} %get-tuple-element.19.rest_2_), channel_id=1, source_target_pairs={{0,48},{8,56},{16,32},{24,40},{32,16},{40,24},{48,0},{56,8},{1,49}... | collective-permute-start | bytes 786440 | tf_op jit(solution)/shard_map/ppermute | solution.py:465
  58.5 8.0 %attend_5.1 = (bf16[64,2048]{1,0:T(8,128)(2,1)S(1)}, bf16[64,2048]{1,0:T(8,128)(2,1)S(1)}) custom-call(s32[3]{0:T(128)S(1)} %pad_add_fusion.meta, s32[128]{0:T(128)S(1)} %plan.1.spots, bf16[64,64,256]{2,1,0:T(8,128)(2,1)} %collective-permute-done.crossed.rest_9_, bf16[4096,256]{1,0:T(8,128)(2,1)S(1)} %bitcast.24, ...), custom_call_target="tpu_custom_call" | custom-call | flops 8589934592 | tf_op jit(solution)/shard_map/attend_5/pallas_call | solution.py:203
  66.5 0.0 collective-permute-done.3.rest_1_
  66.5 1.1 collective-permute-start.11
  67.6 0.0 collective-permute-done.2.rest_0_
  67.6 1.4 collective-permute-start.10
  68.9 8.0 %attend_3.1 = (bf16[64,2048]{1,0:T(8,128)(2,1)S(1)}, bf16[64,2048]{1,0:T(8,128)(2,1)S(1)}) custom-call(s32[3]{0:T(128)S(1)} %pad_add_fusion.meta, s32[128]{0:T(128)S(1)} %plan.1.spots, bf16[64,64,256]{2,1,0:T(8,128)(2,1)} %collective-permute-done.crossed.rest_9_, bf16[4096,256]{1,0:T(8,128)(2,1)S(1)} %bitcast.25, ...), custom_call_target="tpu_custom_call" | custom-call | flops 8589934592 | tf_op jit(solution)/shard_map/attend_3/pallas_call | solution.py:203
  76.9 0.2 collective-permute-start.14
  77.1 0.0 collective-permute-done.1.rest_0_
  77.1 0.0 collective-permute-done.11.rest_3_.rest_4_
  77.1 4.2 %attend_1.1.after = bf16[64,2048]{1,0:T(8,128)(2,1)S(1)} custom-call(s32[3]{0:T(128)S(1)} %pad_add_fusion.meta, s32[128]{0:T(128)S(1)} %plan.1.spots, bf16[64,64,256]{2,1,0:T(8,128)(2,1)} %collective-permute-done.crossed.rest_9_, bf16[4096,256]{1,0:T(8,128)(2,1)S(1)} %bitcast.26, bf16[64,1280]{1,0:T(8,128)(2,1)S(1)} %multiply_convert_fusion.1.mine, ...), custom_call_target="tpu_custom_call" | custom-call | flops 4294967296 | tf_op jit(solution)/shard_map/attend_1/pallas_call | solution.py:203
  81.3 1.5 %collective-permute-start.12 = (bf16[64,2048]{1,0:T(8,128)(2,1)S(1)}, bf16[64,2048]{1,0:T(8,128)(2,1)S(1)}, u32[]{:S(2)}, u32[]{:S(2)}) collective-permute-start(bf16[64,2048]{1,0:T(8,128)(2,1)S(1)} %attend_1.1.after), channel_id=1, source_target_pairs={{0,32},{8,40},{16,48},{24,56},{32,0},{40,8},{48,16},{56,24},{1,33}... | collective-permute-start | bytes 786440 | tf_op jit(solution)/shard_map/ppermute | solution.py:465
  82.8 2.6 %collective-permute-start.13 = (bf16[64,2048]{1,0:T(8,128)(2,1)S(1)}, bf16[64,2048]{1,0:T(8,128)(2,1)S(1)}, u32[]{:S(2)}, u32[]{:S(2)}) collective-permute-start(bf16[64,2048]{1,0:T(8,128)(2,1)S(1)} %get-tuple-element.24), channel_id=1, source_target_pairs={{0,24},{8,0},{16,8},{24,16},{32,56},{40,32},{48,40},{56,48},{1,25}... | collective-permute-start | bytes 786440 | tf_op jit(solution)/shard_map/ppermute | solution.py:465
  85.5 4.1 %attend_own.1.rest_0_ = f32[64,1152]{1,0:T(8,128)S(1)} custom-call(s32[3]{0:T(128)S(1)} %pad_add_fusion.meta, bf16[64,1280]{1,0:T(8,128)(2,1)S(1)} %multiply_convert_fusion.1.mine, bf16[4096,256]{1,0:T(8,128)(2,1)S(1)} %bitcast.27, bf16[64,2048]{1,0:T(8,128)(2,1)S(1)} %attend_1.1.after), custom_call_target="tpu_custom_call" | custom-call | flops 4294967296 | tf_op jit(solution)/shard_map/attend_own/pallas_call | solution.py:153
  89.5 0.0 collective-permute-done.12.rest_1_
  89.6 0.0 copy-start.1
  89.6 1.5 %finish.1 = (bf16[64,1024]{1,0:T(8,128)(2,1)S(1)}, bf16[64,64,256]{2,1,0:T(8,128)(2,1)}) custom-call(s32[3]{0:T(128)S(1)} %pad_add_fusion.meta, s32[128]{0:T(128)S(1)} %plan.1.spots, s32[64]{0:T(128)S(1)} %copy-done.5, bf16[64,1280]{1,0:T(8,128)(2,1)S(1)} %multiply_convert_fusion.1.mine, ...), custom_call_target="tpu_custom_call", output_to_operand_aliasing={{1}: (14, {})} | custom-call | flops 16777216 | bytes 6291456 | tf_op jit(solution)/shard_map/finish/pallas_call | solution.py:358
  91.0 1.0 collective-permute-start.21
  92.0 2.0 %collective-permute-start.20 = (bf16[64,1024]{1,0:T(8,128)(2,1)S(1)}, bf16[64,1024]{1,0:T(8,128)(2,1)S(1)}, u32[]{:S(2)}, u32[]{:S(2)}) collective-permute-start(bf16[64,1024]{1,0:T(8,128)(2,1)S(1)} %get-tuple-element.26.rest_0_), channel_id=1, source_target_pairs={{0,16},{8,24},{16,0},{24,8},{32,48},{40,56},{48,32},{56,40},{1,17}... | collective-permute-start | bytes 393224 | tf_op jit(solution)/shard_map/ppermute | solution.py:462
  94.0 3.3 %collective-permute-start.19 = (bf16[64,1024]{1,0:T(8,128)(2,1)S(1)}, bf16[64,1024]{1,0:T(8,128)(2,1)S(1)}, u32[]{:S(2)}, u32[]{:S(2)}) collective-permute-start(bf16[64,1024]{1,0:T(8,128)(2,1)S(1)} %get-tuple-element.26.rest_0_), channel_id=1, source_target_pairs={{0,56},{8,32},{16,40},{24,48},{32,24},{40,0},{48,8},{56,16},{1,57}... | collective-permute-start | bytes 393224 | tf_op jit(solution)/shard_map/ppermute | solution.py:462
  97.3 0.0 collective-permute-start.18
  97.3 2.6 %collective-permute-start.17 = (bf16[64,1024]{1,0:T(8,128)(2,1)S(1)}, bf16[64,1024]{1,0:T(8,128)(2,1)S(1)}, u32[]{:S(2)}, u32[]{:S(2)}) collective-permute-start(bf16[64,1024]{1,0:T(8,128)(2,1)S(1)} %get-tuple-element.26.rest_0_), channel_id=1, source_target_pairs={{0,24},{8,0},{16,8},{24,16},{32,56},{40,32},{48,40},{56,48},{1,25}... | collective-permute-start | bytes 393224 | tf_op jit(solution)/shard_map/ppermute | solution.py:462
  99.9 0.0 collective-permute-done.21.rest_7_
  99.9 0.0 collective-permute-start.16
  99.9 1.4 collective-permute-start.15
  101.3 2.1 %collective-permute-done.18.rest_4_ = bf16[64,1024]{1,0:T(8,128)(2,1)S(1)} collective-permute-done((bf16[64,1024]{1,0:T(8,128)(2,1)S(1)}, bf16[64,1024]{1,0:T(8,128)(2,1)S(1)}, u32[]{:S(2)}, u32[]{:S(2)}) %collective-permute-start.18) | collective-permute-done | bytes 131104 | tf_op jit(solution)/shard_map/ppermute | solution.py:462
  103.3 3.3 %collective-permute-done.16.rest_2_ = bf16[64,1024]{1,0:T(8,128)(2,1)S(1)} collective-permute-done((bf16[64,1024]{1,0:T(8,128)(2,1)S(1)}, bf16[64,1024]{1,0:T(8,128)(2,1)S(1)}, u32[]{:S(2)}, u32[]{:S(2)}) %collective-permute-start.16) | collective-permute-done | bytes 131104 | tf_op jit(solution)/shard_map/ppermute | solution.py:462
  106.6 2.1 %other_half.1 = f32[256,2048]{1,0:T(8,128)S(1)} custom-call(s32[3]{0:T(128)S(1)} %pad_add_fusion.meta, bf16[64,1024]{1,0:T(8,128)(2,1)S(1)} %get-tuple-element.26.rest_0_, bf16[64,1024]{1,0:T(8,128)(2,1)S(1)} %collective-permute-done.15.rest_1_, bf16[64,1024]{1,0:T(8,128)(2,1)S(1)} %collective-permute-done.16.rest_2_, ...), custom_call_target="tpu_custom_call" | custom-call | flops 1073741824 | bytes 4194304 | tf_op jit(solution)/shard_map/other_half/pallas_call | solution.py:426
  108.7 11.4 %collective-permute-start.22 = (f32[256,2048]{1,0:T(8,128)S(1)}, f32[256,2048]{1,0:T(8,128)S(1)}, u32[]{:S(2)}, u32[]{:S(2)}) collective-permute-start(f32[256,2048]{1,0:T(8,128)S(1)} %other_half.1), channel_id=1, source_target_pairs={{0,1},{1,0},{2,3},{3,2},{4,5},{5,4},{6,7},{7,6},{8,9},{9,8},{10,11... | collective-permute-start | bytes 6291464 | tf_op jit(solution)/shard_map/ppermute | solution.py:504
  120.1 2.1 %own_half.1.own = f32[256,2048]{1,0:T(8,128)S(1)} custom-call(s32[3]{0:T(128)S(1)} %pad_add_fusion.meta, bf16[64,1024]{1,0:T(8,128)(2,1)S(1)} %get-tuple-element.26.rest_0_, bf16[64,1024]{1,0:T(8,128)(2,1)S(1)} %collective-permute-done.15.rest_1_, bf16[64,1024]{1,0:T(8,128)(2,1)S(1)} %collective-permute-done.16.rest_2_, ...), custom_call_target="tpu_custom_call" | custom-call | flops 1073741824 | bytes 4194304 | tf_op jit(solution)/shard_map/own_half/pallas_call | solution.py:426
  122.1 1.7 %collective-permute-done.22.came = f32[256,2048]{1,0:T(8,128)S(1)} collective-permute-done((f32[256,2048]{1,0:T(8,128)S(1)}, f32[256,2048]{1,0:T(8,128)S(1)}, u32[]{:S(2)}, u32[]{:S(2)}) %collective-permute-start.22) | collective-permute-done | bytes 2097184 | tf_op jit(solution)/shard_map/ppermute | solution.py:504
  123.9 0.2 pair_sum.1
  124.0 1.4 collective-permute-start.23
  125.4 2.6 %collective-permute-start.24 = (bf16[64,2048]{1,0:T(8,128)(2,1)S(1)}, bf16[64,2048]{1,0:T(8,128)(2,1)S(1)}, u32[]{:S(2)}, u32[]{:S(2)}) collective-permute-start(bf16[64,2048]{1,0:T(8,128)(2,1)S(1)} %get-tuple-element.29), channel_id=1, source_target_pairs={{0,4},{1,5},{2,6},{3,7},{4,0},{5,1},{6,2},{7,3},{8,12},{9,13},{10,... | collective-permute-start | bytes 786440 | tf_op jit(solution)/shard_map/ppermute | solution.py:507
  128.0 1.1 collective-permute-start.25
  129.1 3.9 %collective-permute-done.23.b = bf16[64,2048]{1,0:T(8,128)(2,1)S(1)} collective-permute-done((bf16[64,2048]{1,0:T(8,128)(2,1)S(1)}, bf16[64,2048]{1,0:T(8,128)(2,1)S(1)}, u32[]{:S(2)}, u32[]{:S(2)}) %collective-permute-start.23) | collective-permute-done | bytes 262176 | tf_op jit(solution)/shard_map/ppermute | solution.py:507
  133.0 6.7 %collective-permute-done.24.c = bf16[64,2048]{1,0:T(8,128)(2,1)S(1)} collective-permute-done((bf16[64,2048]{1,0:T(8,128)(2,1)S(1)}, bf16[64,2048]{1,0:T(8,128)(2,1)S(1)}, u32[]{:S(2)}, u32[]{:S(2)}) %collective-permute-start.24) | collective-permute-done | bytes 262176 | tf_op jit(solution)/shard_map/ppermute | solution.py:507
  139.7 0.8 last_sum.1
  (20 shorter events, 0.1 us)
Async XLA Ops:
  0.6 4.7 %copy-start = (bf16[1,512,2048]{2,1,0:T(8,128)(2,1)S(1)}, bf16[1,512,2048]{2,1,0:T(8,128)(2,1)}, u32[]{:S(2)}) copy-start(bf16[1,512,2048]{2,1,0:T(8,128)(2,1)} %param.7) | copy-start | bytes 6291460
  0.6 52.7 %collective-permute-start = (bf16[64,64,256]{2,1,0:T(8,128)(2,1)}, bf16[64,64,256]{2,1,0:T(8,128)(2,1)}, u32[]{:S(2)}, u32[]{:S(2)}) collective-permute-start(bf16[64,64,256]{2,1,0:T(8,128)(2,1)} %bitcast.22), channel_id=1, source_target_pairs={{0,96},{8,104},{16,112},{24,120},{32,64},{40,72},{48,80},{56,88},{... | collective-permute-start | bytes 6291464 | tf_op jit(solution)/shard_map/ppermute | solution.py:469
  12.1 27.9 %copy-start.4 = (s32[512]{0:T(512)S(1)}, s32[512]{0:T(512)}, u32[]{:S(2)}) copy-start(s32[512]{0:T(512)} %slots.1) | copy-start | bytes 6148
  33.5 7.7 %collective-permute-start.7 = (bf16[64,1024]{1,0:T(8,128)(2,1)S(1)}, bf16[64,1024]{1,0:T(8,128)(2,1)S(1)}, u32[]{:S(2)}, u32[]{:S(2)}) collective-permute-start(bf16[64,1024]{1,0:T(8,128)(2,1)S(1)} %slice.4), channel_id=1, source_target_pairs={{0,16},{8,24},{16,0},{24,8},{32,48},{40,56},{48,32},{56,40},{1,17}... | collective-permute-start | bytes 393224 | tf_op jit(solution)/shard_map/ppermute | solution.py:462
  34.5 6.9 %collective-permute-start.6 = (bf16[64,1024]{1,0:T(8,128)(2,1)S(1)}, bf16[64,1024]{1,0:T(8,128)(2,1)S(1)}, u32[]{:S(2)}, u32[]{:S(2)}) collective-permute-start(bf16[64,1024]{1,0:T(8,128)(2,1)S(1)} %slice.4), channel_id=1, source_target_pairs={{0,48},{8,56},{16,32},{24,40},{32,16},{40,24},{48,0},{56,8},{1,49}... | collective-permute-start | bytes 393224 | tf_op jit(solution)/shard_map/ppermute | solution.py:462
  36.4 19.1 %collective-permute-start.5 = (bf16[64,1024]{1,0:T(8,128)(2,1)S(1)}, bf16[64,1024]{1,0:T(8,128)(2,1)S(1)}, u32[]{:S(2)}, u32[]{:S(2)}) collective-permute-start(bf16[64,1024]{1,0:T(8,128)(2,1)S(1)} %slice.4), channel_id=1, source_target_pairs={{0,40},{8,48},{16,56},{24,32},{32,8},{40,16},{48,24},{56,0},{1,41}... | collective-permute-start | bytes 393224 | tf_op jit(solution)/shard_map/ppermute | solution.py:462
  37.9 17.7 %collective-permute-start.4 = (bf16[64,1024]{1,0:T(8,128)(2,1)S(1)}, bf16[64,1024]{1,0:T(8,128)(2,1)S(1)}, u32[]{:S(2)}, u32[]{:S(2)}) collective-permute-start(bf16[64,1024]{1,0:T(8,128)(2,1)S(1)} %slice.4), channel_id=1, source_target_pairs={{0,56},{8,32},{16,40},{24,48},{32,24},{40,0},{48,8},{56,16},{1,57}... | collective-permute-start | bytes 393224 | tf_op jit(solution)/shard_map/ppermute | solution.py:462
  41.2 25.3 %collective-permute-start.3 = (bf16[64,1024]{1,0:T(8,128)(2,1)S(1)}, bf16[64,1024]{1,0:T(8,128)(2,1)S(1)}, u32[]{:S(2)}, u32[]{:S(2)}) collective-permute-start(bf16[64,1024]{1,0:T(8,128)(2,1)S(1)} %slice.4), channel_id=1, source_target_pairs={{0,8},{8,16},{16,24},{24,0},{32,40},{40,48},{48,56},{56,32},{1,9},... | collective-permute-start | bytes 393224 | tf_op jit(solution)/shard_map/ppermute | solution.py:462
  41.4 26.2 %collective-permute-start.2 = (bf16[64,1024]{1,0:T(8,128)(2,1)S(1)}, bf16[64,1024]{1,0:T(8,128)(2,1)S(1)}, u32[]{:S(2)}, u32[]{:S(2)}) collective-permute-start(bf16[64,1024]{1,0:T(8,128)(2,1)S(1)} %slice.4), channel_id=1, source_target_pairs={{0,24},{8,0},{16,8},{24,16},{32,56},{40,32},{48,40},{56,48},{1,25}... | collective-permute-start | bytes 393224 | tf_op jit(solution)/shard_map/ppermute | solution.py:462
  44.0 1.6 %copy-start.2 = (bf16[1,64,64,256]{3,2,1,0:T(8,128)(2,1)S(1)}, bf16[1,64,64,256]{3,2,1,0:T(8,128)(2,1)}, u32[]{:S(2)}) copy-start(bf16[1,64,64,256]{3,2,1,0:T(8,128)(2,1)} %param.11) | copy-start | bytes 6291460
  45.6 12.8 %copy-start.3 = (bf16[1,64,64,256]{3,2,1,0:T(8,128)(2,1)S(1)}, bf16[1,64,64,256]{3,2,1,0:T(8,128)(2,1)}, u32[]{:S(2)}) copy-start(bf16[1,64,64,256]{3,2,1,0:T(8,128)(2,1)} %param.11) | copy-start | bytes 6291460
  53.4 23.7 %collective-permute-start.1 = (bf16[64,1024]{1,0:T(8,128)(2,1)S(1)}, bf16[64,1024]{1,0:T(8,128)(2,1)S(1)}, u32[]{:S(2)}, u32[]{:S(2)}) collective-permute-start(bf16[64,1024]{1,0:T(8,128)(2,1)S(1)} %slice.4), channel_id=1, source_target_pairs={{0,32},{8,40},{16,48},{24,56},{32,0},{40,8},{48,16},{56,24},{1,33}... | collective-permute-start | bytes 393224 | tf_op jit(solution)/shard_map/ppermute | solution.py:462
  55.5 13.4 %collective-permute-start.9 = (bf16[64,2048]{1,0:T(8,128)(2,1)S(1)}, bf16[64,2048]{1,0:T(8,128)(2,1)S(1)}, u32[]{:S(2)}, u32[]{:S(2)}) collective-permute-start(bf16[64,2048]{1,0:T(8,128)(2,1)S(1)} %get-tuple-element.21), channel_id=1, source_target_pairs={{0,16},{8,24},{16,0},{24,8},{32,48},{40,56},{48,32},{56,40},{1,17}... | collective-permute-start | bytes 786440 | tf_op jit(solution)/shard_map/ppermute | solution.py:465
  55.6 13.3 %collective-permute-start.8 = (bf16[64,2048]{1,0:T(8,128)(2,1)S(1)}, bf16[64,2048]{1,0:T(8,128)(2,1)S(1)}, u32[]{:S(2)}, u32[]{:S(2)}) collective-permute-start(bf16[64,2048]{1,0:T(8,128)(2,1)S(1)} %get-tuple-element.19.rest_2_), channel_id=1, source_target_pairs={{0,48},{8,56},{16,32},{24,40},{32,16},{40,24},{48,0},{56,8},{1,49}... | collective-permute-start | bytes 786440 | tf_op jit(solution)/shard_map/ppermute | solution.py:465
  66.5 10.6 %collective-permute-start.11 = (bf16[64,2048]{1,0:T(8,128)(2,1)S(1)}, bf16[64,2048]{1,0:T(8,128)(2,1)S(1)}, u32[]{:S(2)}, u32[]{:S(2)}) collective-permute-start(bf16[64,2048]{1,0:T(8,128)(2,1)S(1)} %get-tuple-element.23), channel_id=1, source_target_pairs={{0,56},{8,32},{16,40},{24,48},{32,24},{40,0},{48,8},{56,16},{1,57}... | collective-permute-start | bytes 786440 | tf_op jit(solution)/shard_map/ppermute | solution.py:465
  67.6 9.6 %collective-permute-start.10 = (bf16[64,2048]{1,0:T(8,128)(2,1)S(1)}, bf16[64,2048]{1,0:T(8,128)(2,1)S(1)}, u32[]{:S(2)}, u32[]{:S(2)}) collective-permute-start(bf16[64,2048]{1,0:T(8,128)(2,1)S(1)} %get-tuple-element.20.rest_2_), channel_id=1, source_target_pairs={{0,40},{8,48},{16,56},{24,32},{32,8},{40,16},{48,24},{56,0},{1,41}... | collective-permute-start | bytes 786440 | tf_op jit(solution)/shard_map/ppermute | solution.py:465
  76.9 12.6 %collective-permute-start.14 = (bf16[64,2048]{1,0:T(8,128)(2,1)S(1)}, bf16[64,2048]{1,0:T(8,128)(2,1)S(1)}, u32[]{:S(2)}, u32[]{:S(2)}) collective-permute-start(bf16[64,2048]{1,0:T(8,128)(2,1)S(1)} %get-tuple-element.22.rest_1_), channel_id=1, source_target_pairs={{0,8},{8,16},{16,24},{24,0},{32,40},{40,48},{48,56},{56,32},{1,9},... | collective-permute-start | bytes 786440 | tf_op jit(solution)/shard_map/ppermute | solution.py:465
  81.3 8.2 %collective-permute-start.12 = (bf16[64,2048]{1,0:T(8,128)(2,1)S(1)}, bf16[64,2048]{1,0:T(8,128)(2,1)S(1)}, u32[]{:S(2)}, u32[]{:S(2)}) collective-permute-start(bf16[64,2048]{1,0:T(8,128)(2,1)S(1)} %attend_1.1.after), channel_id=1, source_target_pairs={{0,32},{8,40},{16,48},{24,56},{32,0},{40,8},{48,16},{56,24},{1,33}... | collective-permute-start | bytes 786440 | tf_op jit(solution)/shard_map/ppermute | solution.py:465
  82.8 6.7 %copy-start.5 = (s32[64]{0:T(128)S(1)}, s32[64]{0:T(128)}, u32[]{:S(2)}) copy-start(s32[64]{0:T(128)} %lengths.1) | copy-start | bytes 772
  82.8 6.7 %collective-permute-start.13 = (bf16[64,2048]{1,0:T(8,128)(2,1)S(1)}, bf16[64,2048]{1,0:T(8,128)(2,1)S(1)}, u32[]{:S(2)}, u32[]{:S(2)}) collective-permute-start(bf16[64,2048]{1,0:T(8,128)(2,1)S(1)} %get-tuple-element.24), channel_id=1, source_target_pairs={{0,24},{8,0},{16,8},{24,16},{32,56},{40,32},{48,40},{56,48},{1,25}... | collective-permute-start | bytes 786440 | tf_op jit(solution)/shard_map/ppermute | solution.py:465
  89.6 17.1 %copy-start.1 = (bf16[1024,2048]{1,0:T(8,128)(2,1)S(1)}, bf16[1024,2048]{1,0:T(8,128)(2,1)}, u32[]{:S(2)}) copy-start(bf16[1024,2048]{1,0:T(8,128)(2,1)} %rest_8_.3) | copy-start | bytes 12582916
  91.0 8.9 %collective-permute-start.21 = (bf16[64,1024]{1,0:T(8,128)(2,1)S(1)}, bf16[64,1024]{1,0:T(8,128)(2,1)S(1)}, u32[]{:S(2)}, u32[]{:S(2)}) collective-permute-start(bf16[64,1024]{1,0:T(8,128)(2,1)S(1)} %get-tuple-element.26.rest_0_), channel_id=1, source_target_pairs={{0,48},{8,56},{16,32},{24,40},{32,16},{40,24},{48,0},{56,8},{1,49}... | collective-permute-start | bytes 393224 | tf_op jit(solution)/shard_map/ppermute | solution.py:462
  92.0 7.9 %collective-permute-start.20 = (bf16[64,1024]{1,0:T(8,128)(2,1)S(1)}, bf16[64,1024]{1,0:T(8,128)(2,1)S(1)}, u32[]{:S(2)}, u32[]{:S(2)}) collective-permute-start(bf16[64,1024]{1,0:T(8,128)(2,1)S(1)} %get-tuple-element.26.rest_0_), channel_id=1, source_target_pairs={{0,16},{8,24},{16,0},{24,8},{32,48},{40,56},{48,32},{56,40},{1,17}... | collective-permute-start | bytes 393224 | tf_op jit(solution)/shard_map/ppermute | solution.py:462
  94.0 7.3 %collective-permute-start.19 = (bf16[64,1024]{1,0:T(8,128)(2,1)S(1)}, bf16[64,1024]{1,0:T(8,128)(2,1)S(1)}, u32[]{:S(2)}, u32[]{:S(2)}) collective-permute-start(bf16[64,1024]{1,0:T(8,128)(2,1)S(1)} %get-tuple-element.26.rest_0_), channel_id=1, source_target_pairs={{0,56},{8,32},{16,40},{24,48},{32,24},{40,0},{48,8},{56,16},{1,57}... | collective-permute-start | bytes 393224 | tf_op jit(solution)/shard_map/ppermute | solution.py:462
  97.3 6.0 %collective-permute-start.18 = (bf16[64,1024]{1,0:T(8,128)(2,1)S(1)}, bf16[64,1024]{1,0:T(8,128)(2,1)S(1)}, u32[]{:S(2)}, u32[]{:S(2)}) collective-permute-start(bf16[64,1024]{1,0:T(8,128)(2,1)S(1)} %get-tuple-element.26.rest_0_), channel_id=1, source_target_pairs={{0,40},{8,48},{16,56},{24,32},{32,8},{40,16},{48,24},{56,0},{1,41}... | collective-permute-start | bytes 393224 | tf_op jit(solution)/shard_map/ppermute | solution.py:462
  97.3 6.0 %collective-permute-start.17 = (bf16[64,1024]{1,0:T(8,128)(2,1)S(1)}, bf16[64,1024]{1,0:T(8,128)(2,1)S(1)}, u32[]{:S(2)}, u32[]{:S(2)}) collective-permute-start(bf16[64,1024]{1,0:T(8,128)(2,1)S(1)} %get-tuple-element.26.rest_0_), channel_id=1, source_target_pairs={{0,24},{8,0},{16,8},{24,16},{32,56},{40,32},{48,40},{56,48},{1,25}... | collective-permute-start | bytes 393224 | tf_op jit(solution)/shard_map/ppermute | solution.py:462
  99.9 6.7 %collective-permute-start.16 = (bf16[64,1024]{1,0:T(8,128)(2,1)S(1)}, bf16[64,1024]{1,0:T(8,128)(2,1)S(1)}, u32[]{:S(2)}, u32[]{:S(2)}) collective-permute-start(bf16[64,1024]{1,0:T(8,128)(2,1)S(1)} %get-tuple-element.26.rest_0_), channel_id=1, source_target_pairs={{0,8},{8,16},{16,24},{24,0},{32,40},{40,48},{48,56},{56,32},{1,9},... | collective-permute-start | bytes 393224 | tf_op jit(solution)/shard_map/ppermute | solution.py:462
  99.9 6.7 %collective-permute-start.15 = (bf16[64,1024]{1,0:T(8,128)(2,1)S(1)}, bf16[64,1024]{1,0:T(8,128)(2,1)S(1)}, u32[]{:S(2)}, u32[]{:S(2)}) collective-permute-start(bf16[64,1024]{1,0:T(8,128)(2,1)S(1)} %get-tuple-element.26.rest_0_), channel_id=1, source_target_pairs={{0,32},{8,40},{16,48},{24,56},{32,0},{40,8},{48,16},{56,24},{1,33}... | collective-permute-start | bytes 393224 | tf_op jit(solution)/shard_map/ppermute | solution.py:462
  108.7 15.1 %collective-permute-start.22 = (f32[256,2048]{1,0:T(8,128)S(1)}, f32[256,2048]{1,0:T(8,128)S(1)}, u32[]{:S(2)}, u32[]{:S(2)}) collective-permute-start(f32[256,2048]{1,0:T(8,128)S(1)} %other_half.1), channel_id=1, source_target_pairs={{0,1},{1,0},{2,3},{3,2},{4,5},{5,4},{6,7},{7,6},{8,9},{9,8},{10,11... | collective-permute-start | bytes 6291464 | tf_op jit(solution)/shard_map/ppermute | solution.py:504
  124.0 8.9 %collective-permute-start.23 = (bf16[64,2048]{1,0:T(8,128)(2,1)S(1)}, bf16[64,2048]{1,0:T(8,128)(2,1)S(1)}, u32[]{:S(2)}, u32[]{:S(2)}) collective-permute-start(bf16[64,2048]{1,0:T(8,128)(2,1)S(1)} %get-tuple-element.28), channel_id=1, source_target_pairs={{0,2},{1,3},{2,4},{3,5},{4,6},{5,7},{6,0},{7,1},{8,10},{9,11},{10,... | collective-permute-start | bytes 786440 | tf_op jit(solution)/shard_map/ppermute | solution.py:507
  125.4 14.3 %collective-permute-start.24 = (bf16[64,2048]{1,0:T(8,128)(2,1)S(1)}, bf16[64,2048]{1,0:T(8,128)(2,1)S(1)}, u32[]{:S(2)}, u32[]{:S(2)}) collective-permute-start(bf16[64,2048]{1,0:T(8,128)(2,1)S(1)} %get-tuple-element.29), channel_id=1, source_target_pairs={{0,4},{1,5},{2,6},{3,7},{4,0},{5,1},{6,2},{7,3},{8,12},{9,13},{10,... | collective-permute-start | bytes 786440 | tf_op jit(solution)/shard_map/ppermute | solution.py:507
  128.0 11.7 %collective-permute-start.25 = (bf16[64,2048]{1,0:T(8,128)(2,1)S(1)}, bf16[64,2048]{1,0:T(8,128)(2,1)S(1)}, u32[]{:S(2)}, u32[]{:S(2)}) collective-permute-start(bf16[64,2048]{1,0:T(8,128)(2,1)S(1)} %get-tuple-element.30), channel_id=1, source_target_pairs={{0,6},{1,7},{2,0},{3,1},{4,2},{5,3},{6,4},{7,5},{8,14},{9,15},{10,... | collective-permute-start | bytes 786440 | tf_op jit(solution)/shard_map/ppermute | solution.py:507

commit v3 on v2

--- a/solution.py
+++ b/solution.py
@@ -71,20 +71,26 @@
         pages_for(slots, me, peer(me, STEPS[step], -1), leaving)
 
 
-def weigh(scores, values, state):
-    m, l, acc = state
-    new = jnp.maximum(m, jnp.max(scores, axis=1, keepdims=True))
-    fade = jnp.exp2((m - new) * COEF)
-    weights = jnp.exp2((scores - new) * COEF)
-    lanes = [weights[:, x : x + HD] for x in range(0, weights.shape[1], HD)]
-    l = l * fade + functools.reduce(jnp.add, lanes)
-    acc = acc * fade + jnp.dot(weights.astype(BF), values, preferred_element_type=F32)
+def weigh(pieces, state=None):
+    new = functools.reduce(jnp.maximum, [jnp.max(scores, axis=1, keepdims=True) for scores, _ in pieces])
+    l = acc = None
+    if state is not None:
+        m, l, acc = state
+        new = jnp.maximum(m, new)
+        fade = jnp.exp2((m - new) * COEF)
+        l, acc = l * fade, acc * fade
+    for scores, values in pieces:
+        weights = jnp.exp2((scores - new) * COEF)
+        lanes = [weights[:, x : x + HD] for x in range(0, weights.shape[1], HD)]
+        lanes = functools.reduce(jnp.add, lanes)
+        mixed = jnp.dot(weights.astype(BF), values, preferred_element_type=F32)
+        l = lanes if l is None else l + lanes
+        acc = mixed if acc is None else acc + mixed
     return (new, l, acc)
 
 
 def attend_rows(meta, owner, block, q, kv, mine, out, q2, pair):
     contract = (((1,), (1,)), ((), ()))
-    big = HEADS * ROW
     if q is not None:
         for h in range(HEADS):
             q2[h * ROW : (h + 1) * ROW, :] = q[:, h * HD : (h + 1) * HD]
@@ -95,16 +101,13 @@
     token = lax.bitwise_and(lax.broadcasted_iota(jnp.int32, scores.shape, 0), ROW - 1)
     key = lax.broadcasted_iota(jnp.int32, scores.shape, 1)
     scores = jnp.where((key <= token + ahead) & (key < ROW), scores, -1e30)
-    state = (
-        jnp.full((big, 1), -1e30, F32),
-        jnp.zeros((big, HD), F32),
-        jnp.zeros((big, HD), F32),
-    )
-    state = weigh(scores, pair[:, HD:], state)
+    recent = (scores, pair[:, HD:])
+    state = None
     for first in range(0, kv.shape[0], block):
         some = slice(first, first + block)
         scores = lax.dot_general(q2[...], kv[some, :HD], contract, preferred_element_type=F32)
-        state = weigh(scores, kv[some, HD:], state)
+        pieces = [(scores, kv[some, HD:])]
+        state = weigh(pieces if state is not None else [recent] + pieces, state)
     m, l, acc = state
     l = jnp.sum(l, axis=1, keepdims=True)
     mixed = acc * (1.0 / l)
@@ -124,25 +127,8 @@
     out[:, HEADS * HD :] = stats.astype(out.dtype)
 
 
-def plan_kernel(meta, slots, spots):
-    @pl.when(meta[PREFILL] == 0)
-    def _():
-        places(meta, slots, spots)
-
-
-def plan(meta, slots):
-    return pl.pallas_call(
-        plan_kernel,
-        in_specs=[SMEM] * 2,
-        out_specs=SMEM,
-        out_shape=jax.ShapeDtypeStruct((128,), jnp.int32),
-        compiler_params=params(),
-        cost_estimate=pl.CostEstimate(flops=0, bytes_accessed=0, transcendentals=0),
-        name="plan",
-    )(meta, slots)
-
-
-def own_kernel(block, meta, mine, kv, after, out, q2, pair):
+def own_kernel(block, meta, mine, kv, *rest):
+    out, q2, pair = rest[-3:]
     @pl.when(meta[PREFILL] == 1)
     def _():
         attend_rows(meta, meta[ME], block, mine, kv, mine, out, q2, pair)
@@ -152,14 +138,14 @@
     big = HEADS * ROW
     return pl.pallas_call(
         functools.partial(own_kernel, block),
-        in_specs=[SMEM] + [VMEM] * 2 + [ANY],
+        in_specs=[SMEM] + [VMEM] * 2 + [ANY] * len(after),
         out_specs=VMEM,
         out_shape=jax.ShapeDtypeStruct((ROW, STATE), F32),
         scratch_shapes=[pltpu.VMEM((big, HD), BF), pltpu.VMEM((HD, 2 * HD), BF)],
         compiler_params=params(),
         cost_estimate=pl.CostEstimate(flops=1 << 32, bytes_accessed=0, transcendentals=0),
         name="attend_own",
-    )(meta, mine, pages, after)
+    )(meta, mine, pages, *after)
 
 
 def attend_kernel(steps, block, meta, spots, crossed, kv, mine, *rest):
@@ -213,8 +199,8 @@
     )(meta, spots, crossed, pages, mine, *queries, *after)
 
 
-def start_kernel(steps, block, meta, kv, mine, *rest):
-    queries, outs, (pool, state, q2, pair, sem) = rest[: len(steps)], rest[-len(steps) - 5 : -5], rest[-5:]
+def start_kernel(steps, block, meta, slots, kv, mine, *rest):
+    queries, outs, (pool, spots, state, q2, pair, sem) = rest[: len(steps)], rest[-len(steps) - 6 : -6], rest[-6:]
     i = pl.program_id(0)
 
     @pl.when(meta[PREFILL] == 1)
@@ -231,20 +217,24 @@
         def _():
             keep.wait()
 
-
-def attend_first(steps, meta, pages, mine, queries, block=2048):
+    @pl.when((meta[PREFILL] == 0) & (i == 0))
+    def _():
+        places(meta, slots, spots)
+
+
+def attend_first(steps, meta, slots, pages, mine, queries, block=2048):
     return pl.pallas_call(
         functools.partial(start_kernel, steps, block),
         grid=(len(steps),),
-        in_specs=[SMEM] + [VMEM] * (2 + len(queries)),
-        out_specs=[VMEM] * len(steps) + [ANY],
+        in_specs=[SMEM] * 2 + [VMEM] * (2 + len(queries)),
+        out_specs=[VMEM] * len(steps) + [ANY, SMEM],
         out_shape=[jax.ShapeDtypeStruct((ROW, 16 * HD), BF)] * len(steps)
-        + [jax.ShapeDtypeStruct(pages.shape, BF)],
+        + [jax.ShapeDtypeStruct(pages.shape, BF), jax.ShapeDtypeStruct((128,), jnp.int32)],
         scratch_shapes=attend_scratch() + [pltpu.SemaphoreType.DMA],
         compiler_params=params(),
         cost_estimate=pl.CostEstimate(flops=0, bytes_accessed=0, transcendentals=0),
         name=f"attend_{steps[0]}",
-    )(meta, pages, mine, *queries)
+    )(meta, slots, pages, mine, *queries)
 
 
 def fill_pages(steps, spots, crossed, outs, sem):
@@ -284,7 +274,7 @@
 
 
 def finish_kernel(meta, spots, lengths, mine, *rest):
-    came, (pages, crossed, _, heads, pool, held, relaid, q3, o3, sems) = rest[:CTX], rest[CTX:]
+    came, (pages, crossed, _, heads, pool, held, relaid, q3, o3, own3, sems) = rest[:CTX], rest[CTX:]
     contract = (((1,), (1,)), ((), ()))
 
     @pl.when(meta[PREFILL] == 1)
@@ -314,6 +304,7 @@
                 relaid[spots[step * 8 + n]] = came[step][:, n * 2 * HD : (n + 1) * 2 * HD]
         for h in range(HEADS):
             q3[:, h, :] = mine[:, h * HD : (h + 1) * HD].astype(F32)
+        own3[...] = mine[:, HEADS * HD :].astype(F32)
         load.wait()
         pltpu.make_async_copy(pages.at[pl.ds(0, 8)], relaid.at[pl.ds(0, 8)], sems.at[1]).wait()
         keep = pltpu.make_async_copy(relaid, pool, sems.at[2])
@@ -323,7 +314,7 @@
 
         def some(i, _):
             first = i * at_once
-            own = mine[pl.ds(pl.multiple_of(first, at_once), at_once), HEADS * HD :].astype(F32)
+            own = own3[pl.ds(pl.multiple_of(first, at_once), at_once), :]
             scores, own_scores, values = [], [], []
             for r in range(at_once):
                 both = jnp.concatenate([held[first + r], relaid[first + r]], axis=0)
@@ -339,11 +330,10 @@
             weights = jnp.exp2((scores - top) * COEF)
             own_weights = jnp.exp2((own_scores - top) * COEF)
             total = jnp.sum(weights, axis=1, keepdims=True) + own_weights
-            weights = weights.astype(BF)
             own_weights = own_weights.astype(BF).astype(F32)
             for r in range(at_once):
                 rows = slice(r * HEADS, (r + 1) * HEADS)
-                mixed = jnp.dot(weights[rows], values[r], preferred_element_type=F32)
+                mixed = jnp.dot(weights[rows].astype(BF), values[r], preferred_element_type=F32)
                 mixed = mixed + own_weights[rows] * own[r : r + 1, HD:]
                 o3[first + r] = mixed / total[rows]
             return 0
@@ -368,6 +358,7 @@
             pltpu.VMEM(pool.shape, BF),
             pltpu.VMEM((ROW, HEADS, HD), F32),
             pltpu.VMEM((ROW, HEADS, HD), F32),
+            pltpu.VMEM((ROW, 2 * HD), F32),
             pltpu.SemaphoreType.DMA((3,)),
         ],
         input_output_aliases={6 + CTX: 1},
@@ -482,10 +473,9 @@
     came = swap(part.reshape(CTX, ROW, -1))
     mine = (jnp.sum(came.astype(F32), axis=0) * (1.0 / LIFT)).astype(BF)
     queries = mine[:, : HEADS * HD]
-    spots = plan(meta, page_slot)
     groups = ((7, 6), (5, 4), (3, 2), (1,))
     asked = {s: both_rings(queries, s) for steps in groups for s in steps}
-    *outs, pool = attend_first(groups[0], meta, flat_pages, mine, [asked[s] for s in groups[0]])
+    *outs, pool, spots = attend_first(groups[0], meta, page_slot, flat_pages, mine, [asked[s] for s in groups[0]])
     outs = fill(groups[0], meta, spots, crossed, outs)
     came = {}
     before = []
@@ -496,7 +486,7 @@
             before = [came[s] for s in groups[n - 1]]
         for s, value in zip(steps, outs):
             came[s] = back(value, s)
-    state = attend_own(meta, mine, flat_pages, outs[0])
+    state = attend_own(meta, mine, flat_pages, [outs[0]] + before)
     states = [state] + [came[s] for s in range(1, CTX)]
     heads, pool = finish(meta, spots, lengths, mine, states, pages, crossed, pool.reshape(pages.shape))
     gathered = [heads] + [both_rings(heads, s) for s in range(1, CTX)]

time: 141 us -> 142 us (level)
  waiting for transfers between devices: 17.8 us -> 22.1 us
  Pallas kernels: 40.5 us -> 39 us
  starting transfers between devices: 51.5 us -> 50 us
    ppermute x14, waiting for transfers between devices: 5.47 us -> 7.97 us  [both_rings(): lax.ppermute(value, 'ctx', [(c, peer(c, STEPS[s], 1)) for c in range(CTX)])]
    ppermute x7, waiting for transfers between devices: 0.02 us -> 1.83 us  [back(): lax.ppermute(value, 'ctx', [(c, peer(c, STEPS[s], -1)) for c in range(CTX)])]
    ppermute x14, starting transfers between devices: 20.8 us -> 19.3 us  [both_rings(): lax.ppermute(value, 'ctx', [(c, peer(c, STEPS[s], 1)) for c in range(CTX)])]
  transfers between devices with their start and end apart: 26 -> 26, of which waited for: 6 -> 7; matrix products, arithmetic and copies ran while one was open for 5% -> 5% of each run, Pallas kernels for 26% -> 24%
where the time goes in v3:
time: 142 us
  starting transfers between devices  50 us (35%)
  Pallas kernels  39 us (27%)
  waiting for transfers between devices  22.1 us (16%)
  blocking collectives  21.1 us (15%)
  matrix products  6.45 us (5%)
  local copies, waits for them, and re-layouts  1.63 us (1%)
    all_to_all x1, blocking collectives, swap(): return lax.all_to_all(value, 'ctx', 0, 0, tiled=True)  21.1 us
    pallas_call x3, Pallas kernels, attend(): pl.pallas_call(functools.partial(attend_kernel, steps, block), grid=(len(...  19.5 us
    ppermute x14, starting transfers between devices, both_rings(): lax.ppermute(value, 'ctx', [(c, peer(c, STEPS[s], 1)) for c in range(CTX)])  19.3 us
    ppermute x1, starting transfers between devices, shards(): came = lax.ppermute(sent, 'tp', [(t, t ^ 1) for t in range(8)])  12.3 us
    ppermute x3, waiting for transfers between devices, shards(): lax.ppermute(mine[p], 'tp', [(t, (t + 2 * p) % 8) for t in range(8)])  10.6 us
    ppermute x7, starting transfers between devices, back(): lax.ppermute(value, 'ctx', [(c, peer(c, STEPS[s], -1)) for c in range(CTX)])  8.6 us
    pallas_call x1, Pallas kernels, attend_first(): pl.pallas_call(functools.partial(start_kernel, steps, block), grid=(len(s...  8.25 us
    ppermute x14, waiting for transfers between devices, both_rings(): lax.ppermute(value, 'ctx', [(c, peer(c, STEPS[s], 1)) for c in range(CTX)])  7.97 us
  transfers between devices with their start and end apart: 26, of which 7 were waited for; matrix products, arithmetic and copies ran while one was open for 5% of the time, Pallas kernels for 24%

profile of v3, /device:TPU:1, one launch (start us, length us, event | category | flops | bytes accessed | tf_op | source)
XLA Modules:
  0.0 141.8 jit_solution(3129067059591184179)
XLA Ops:
  0.6 0.0 copy-start
  0.6 4.7 %collective-permute-start.2 = (bf16[64,64,256]{2,1,0:T(8,128)(2,1)}, bf16[64,64,256]{2,1,0:T(8,128)(2,1)}, u32[]{:S(2)}, u32[]{:S(2)}) collective-permute-start(bf16[64,64,256]{2,1,0:T(8,128)(2,1)} %bitcast.22), channel_id=1, source_target_pairs={{0,96},{8,104},{16,112},{24,120},{32,64},{40,72},{48,80},{56,88},{... | collective-permute-start | bytes 6291464 | tf_op jit(solution)/shard_map/ppermute | solution.py:460
  5.3 1.9 %fusion.9 = f16[512,256]{1,0:T(8,128)(2,1)S(1)} fusion(bf16[2048,256]{1,0:T(8,128)(2,1)} %param.9, bf16[1,512,2048]{2,1,0:T(8,128)(2,1)S(1)} %copy-done), kind=kOutput, calls=%fused_computation.8 | convolution fusion | flops 537133056 | bytes 3407872 | tf_op jit(solution)/shard_map/dot_general | solution.py:468
  7.3 4.5 %multiply_convert_fusion = f16[512,1024]{1,0:T(8,128)(2,1)S(1)} fusion(bf16[2048,1024]{1,0:T(8,128)(2,1)} %param.8, bf16[1,512,2048]{2,1,0:T(8,128)(2,1)S(1)} %copy-done), kind=kOutput, calls=%fused_computation.5 | convolution fusion | flops 2148532224 | bytes 7340032 | tf_op jit(solution)/shard_map/dot_general | solution.py:468
  11.8 0.3 pad_maximum_fusion
  12.1 0.0 copy-start.4
  12.1 21.1 %all_to_all.5 = f16[8,64,1280]{2,1,0:T(8,128)(2,1)S(1)} all-to-all(f16[8,64,1280]{2,1,0:T(8,128)(2,1)S(1)} %bitcast.29), channel_id=1, replica_groups=mesh['group'=2,'ctx'=8,'tp'=8] {'ctx'}, dimensions={0} | all-to-all | bytes 2621440 | tf_op jit(solution)/shard_map/all_to_all | solution.py:463
  33.3 0.2 convert_reduce_fusion
  33.5 1.0 collective-permute-start.1
  34.5 1.9 %collective-permute-start = (bf16[64,1024]{1,0:T(8,128)(2,1)S(1)}, bf16[64,1024]{1,0:T(8,128)(2,1)S(1)}, u32[]{:S(2)}, u32[]{:S(2)}) collective-permute-start(bf16[64,1024]{1,0:T(8,128)(2,1)S(1)} %slice.4), channel_id=1, source_target_pairs={{0,48},{8,56},{16,32},{24,40},{32,16},{40,24},{48,0},{56,8},{1,49}... | collective-permute-start | bytes 393224 | tf_op jit(solution)/shard_map/ppermute | solution.py:453
  36.4 1.6 %collective-permute-start.7 = (bf16[64,1024]{1,0:T(8,128)(2,1)S(1)}, bf16[64,1024]{1,0:T(8,128)(2,1)S(1)}, u32[]{:S(2)}, u32[]{:S(2)}) collective-permute-start(bf16[64,1024]{1,0:T(8,128)(2,1)S(1)} %slice.4), channel_id=1, source_target_pairs={{0,40},{8,48},{16,56},{24,32},{32,8},{40,16},{48,24},{56,0},{1,41}... | collective-permute-start | bytes 393224 | tf_op jit(solution)/shard_map/ppermute | solution.py:453
  37.9 2.0 %collective-permute-start.6 = (bf16[64,1024]{1,0:T(8,128)(2,1)S(1)}, bf16[64,1024]{1,0:T(8,128)(2,1)S(1)}, u32[]{:S(2)}, u32[]{:S(2)}) collective-permute-start(bf16[64,1024]{1,0:T(8,128)(2,1)S(1)} %slice.4), channel_id=1, source_target_pairs={{0,56},{8,32},{16,40},{24,48},{32,24},{40,0},{48,8},{56,16},{1,57}... | collective-permute-start | bytes 393224 | tf_op jit(solution)/shard_map/ppermute | solution.py:453
  39.9 0.1 pad_add_fusion.meta
  40.0 0.0 collective-permute-done.1.rest_1_
  40.0 0.0 collective-permute-start.5
  40.0 1.3 collective-permute-done.rest_0_
  41.4 2.7 %collective-permute-start.4 = (bf16[64,1024]{1,0:T(8,128)(2,1)S(1)}, bf16[64,1024]{1,0:T(8,128)(2,1)S(1)}, u32[]{:S(2)}, u32[]{:S(2)}) collective-permute-start(bf16[64,1024]{1,0:T(8,128)(2,1)S(1)} %slice.4), channel_id=1, source_target_pairs={{0,24},{8,0},{16,8},{24,16},{32,56},{40,32},{48,40},{56,48},{1,25}... | collective-permute-start | bytes 393224 | tf_op jit(solution)/shard_map/ppermute | solution.py:453
  44.0 1.6 %copy-done.2 = bf16[1,64,64,256]{3,2,1,0:T(8,128)(2,1)S(1)} copy-done((bf16[1,64,64,256]{3,2,1,0:T(8,128)(2,1)S(1)}, bf16[1,64,64,256]{3,2,1,0:T(8,128)(2,1)}, u32[]{:S(2)}) %copy-start.2) | copy-done | bytes 2097176
  45.6 8.2 %attend_7.1 = (bf16[64,2048]{1,0:T(8,128)(2,1)S(1)}, bf16[64,2048]{1,0:T(8,128)(2,1)S(1)}, bf16[4096,256]{1,0:T(8,128)(2,1)}, s32[128]{0:T(128)S(1)}) custom-call(s32[3]{0:T(128)S(1)} %pad_add_fusion.meta, s32[512]{0:T(512)S(1)} %copy-done.4, bf16[4096,256]{1,0:T(8,128)(2,1)S(1)} %bitcast.23, bf16[64,1280]{1,0:T(8,128)(2,1)S(1)} %multiply_convert_fusion.1.mine, ...), custom_call_target="tpu_custom_call" | custom-call | tf_op jit(solution)/shard_map/attend_7/pallas_call | solution.py:226
  53.9 0.0 collective-permute-done.2.crossed.rest_9_
  53.9 0.1 collective-permute-start.3
  54.0 0.7 fill_7.1
  54.8 0.0 collective-permute-done.7.rest_1_
  54.8 0.1 collective-permute-start.9
  54.9 4.1 %collective-permute-start.8 = (bf16[64,2048]{1,0:T(8,128)(2,1)S(1)}, bf16[64,2048]{1,0:T(8,128)(2,1)S(1)}, u32[]{:S(2)}, u32[]{:S(2)}) collective-permute-start(bf16[64,2048]{1,0:T(8,128)(2,1)S(1)} %get-tuple-element.21.rest_2_), channel_id=1, source_target_pairs={{0,48},{8,56},{16,32},{24,40},{32,16},{40,24},{48,0},{56,8},{1,49}... | collective-permute-start | bytes 786440 | tf_op jit(solution)/shard_map/ppermute | solution.py:456
  59.0 7.7 %attend_5.1 = (bf16[64,2048]{1,0:T(8,128)(2,1)S(1)}, bf16[64,2048]{1,0:T(8,128)(2,1)S(1)}) custom-call(s32[3]{0:T(128)S(1)} %pad_add_fusion.meta, s32[128]{0:T(128)S(1)} %get-tuple-element.18.spots, bf16[64,64,256]{2,1,0:T(8,128)(2,1)} %collective-permute-done.2.crossed.rest_9_, bf16[4096,256]{1,0:T(8,128)(2,1)S(1)} %bitcast.24, ...), custom_call_target="tpu_custom_call" | custom-call | flops 8589934592 | tf_op jit(solution)/shard_map/attend_5/pallas_call | solution.py:189
  66.7 0.1 collective-permute-start.11
  66.8 2.3 %collective-permute-start.10 = (bf16[64,2048]{1,0:T(8,128)(2,1)S(1)}, bf16[64,2048]{1,0:T(8,128)(2,1)S(1)}, u32[]{:S(2)}, u32[]{:S(2)}) collective-permute-start(bf16[64,2048]{1,0:T(8,128)(2,1)S(1)} %get-tuple-element.22.rest_2_), channel_id=1, source_target_pairs={{0,40},{8,48},{16,56},{24,32},{32,8},{40,16},{48,24},{56,0},{1,41}... | collective-permute-start | bytes 786440 | tf_op jit(solution)/shard_map/ppermute | solution.py:456
  69.2 0.0 collective-permute-done.9.rest_4_.rest_6_
  69.2 0.0 collective-permute-done.8.rest_3_.rest_7_
  69.2 7.7 %attend_3.1 = (bf16[64,2048]{1,0:T(8,128)(2,1)S(1)}, bf16[64,2048]{1,0:T(8,128)(2,1)S(1)}) custom-call(s32[3]{0:T(128)S(1)} %pad_add_fusion.meta, s32[128]{0:T(128)S(1)} %get-tuple-element.18.spots, bf16[64,64,256]{2,1,0:T(8,128)(2,1)} %collective-permute-done.2.crossed.rest_9_, bf16[4096,256]{1,0:T(8,128)(2,1)S(1)} %bitcast.25, ...), custom_call_target="tpu_custom_call" | custom-call | flops 8589934592 | tf_op jit(solution)/shard_map/attend_3/pallas_call | solution.py:189
  76.9 1.5 %collective-permute-start.13 = (bf16[64,2048]{1,0:T(8,128)(2,1)S(1)}, bf16[64,2048]{1,0:T(8,128)(2,1)S(1)}, u32[]{:S(2)}, u32[]{:S(2)}) collective-permute-start(bf16[64,2048]{1,0:T(8,128)(2,1)S(1)} %get-tuple-element.26), channel_id=1, source_target_pairs={{0,24},{8,0},{16,8},{24,16},{32,56},{40,32},{48,40},{56,48},{1,25}... | collective-permute-start | bytes 786440 | tf_op jit(solution)/shard_map/ppermute | solution.py:456
  78.4 0.1 collective-permute-start.12
  78.4 0.0 collective-permute-done.3.rest_0_
  78.4 0.0 collective-permute-done.11.rest_3_.rest_4_
  78.4 0.0 collective-permute-done.10.rest_2_.rest_5_
  78.4 4.1 %attend_1.1.rest_0_ = bf16[64,2048]{1,0:T(8,128)(2,1)S(1)} custom-call(s32[3]{0:T(128)S(1)} %pad_add_fusion.meta, s32[128]{0:T(128)S(1)} %get-tuple-element.18.spots, bf16[64,64,256]{2,1,0:T(8,128)(2,1)} %collective-permute-done.2.crossed.rest_9_, bf16[4096,256]{1,0:T(8,128)(2,1)S(1)} %bitcast.26, bf16[64,1280]{1,0:T(8,128)(2,1)S(1)} %multiply_convert_fusion.1.mine, ...), custom_call_target="tpu_custom_call" | custom-call | flops 4294967296 | tf_op jit(solution)/shard_map/attend_1/pallas_call | solution.py:189
  82.5 0.0 copy-start.5
  82.5 0.4 collective-permute-start.14
  83.0 0.0 collective-permute-done.13.rest_2_
  83.0 1.8 %collective-permute-done.12.rest_1_.rest_3_ = bf16[64,2048]{1,0:T(8,128)(2,1)S(1)} collective-permute-done((bf16[64,2048]{1,0:T(8,128)(2,1)S(1)}, bf16[64,2048]{1,0:T(8,128)(2,1)S(1)}, u32[]{:S(2)}, u32[]{:S(2)}) %collective-permute-start.12) | collective-permute-done | bytes 262176 | tf_op jit(solution)/shard_map/ppermute | solution.py:456
  84.8 3.9 %attend_own.1.rest_0_ = f32[64,1152]{1,0:T(8,128)S(1)} custom-call(s32[3]{0:T(128)S(1)} %pad_add_fusion.meta, bf16[64,1280]{1,0:T(8,128)(2,1)S(1)} %multiply_convert_fusion.1.mine, bf16[4096,256]{1,0:T(8,128)(2,1)S(1)} %bitcast.27, bf16[64,2048]{1,0:T(8,128)(2,1)S(1)} %attend_1.1.rest_0_, bf16[64,2048]{1,0:T(8,128)(2,1)S(1)} %collective-permute-done.12.rest_1_.rest_3_, ...), custom_call_target="tpu_custom_call" | custom-call | flops 4294967296 | tf_op jit(solution)/shard_map/attend_own/pallas_call | solution.py:139
  88.8 0.0 copy-start.1
  88.8 1.5 %finish.1 = (bf16[64,1024]{1,0:T(8,128)(2,1)S(1)}, bf16[64,64,256]{2,1,0:T(8,128)(2,1)}) custom-call(s32[3]{0:T(128)S(1)} %pad_add_fusion.meta, s32[128]{0:T(128)S(1)} %get-tuple-element.18.spots, s32[64]{0:T(128)S(1)} %copy-done.5, bf16[64,1280]{1,0:T(8,128)(2,1)S(1)} %multiply_convert_fusion.1.mine, ...), custom_call_target="tpu_custom_call", output_to_operand_aliasing={{1}: (14, {})} | custom-call | flops 16777216 | bytes 6291456 | tf_op jit(solution)/shard_map/finish/pallas_call | solution.py:348
  90.2 0.8 collective-permute-start.21
  91.0 2.3 %collective-permute-start.20 = (bf16[64,1024]{1,0:T(8,128)(2,1)S(1)}, bf16[64,1024]{1,0:T(8,128)(2,1)S(1)}, u32[]{:S(2)}, u32[]{:S(2)}) collective-permute-start(bf16[64,1024]{1,0:T(8,128)(2,1)S(1)} %get-tuple-element.28.rest_0_), channel_id=1, source_target_pairs={{0,16},{8,24},{16,0},{24,8},{32,48},{40,56},{48,32},{56,40},{1,17}... | collective-permute-start | bytes 393224 | tf_op jit(solution)/shard_map/ppermute | solution.py:453
  93.3 3.0 %collective-permute-start.19 = (bf16[64,1024]{1,0:T(8,128)(2,1)S(1)}, bf16[64,1024]{1,0:T(8,128)(2,1)S(1)}, u32[]{:S(2)}, u32[]{:S(2)}) collective-permute-start(bf16[64,1024]{1,0:T(8,128)(2,1)S(1)} %get-tuple-element.28.rest_0_), channel_id=1, source_target_pairs={{0,56},{8,32},{16,40},{24,48},{32,24},{40,0},{48,8},{56,16},{1,57}... | collective-permute-start | bytes 393224 | tf_op jit(solution)/shard_map/ppermute | solution.py:453
  96.4 2.6 %collective-permute-start.17 = (bf16[64,1024]{1,0:T(8,128)(2,1)S(1)}, bf16[64,1024]{1,0:T(8,128)(2,1)S(1)}, u32[]{:S(2)}, u32[]{:S(2)}) collective-permute-start(bf16[64,1024]{1,0:T(8,128)(2,1)S(1)} %get-tuple-element.28.rest_0_), channel_id=1, source_target_pairs={{0,24},{8,0},{16,8},{24,16},{32,56},{40,32},{48,40},{56,48},{1,25}... | collective-permute-start | bytes 393224 | tf_op jit(solution)/shard_map/ppermute | solution.py:453
  98.9 0.0 collective-permute-done.21.rest_7_
  98.9 0.0 collective-permute-start.16
  99.0 1.4 collective-permute-start.15
  100.3 2.1 %collective-permute-done.18.rest_4_ = bf16[64,1024]{1,0:T(8,128)(2,1)S(1)} collective-permute-done((bf16[64,1024]{1,0:T(8,128)(2,1)S(1)}, bf16[64,1024]{1,0:T(8,128)(2,1)S(1)}, u32[]{:S(2)}, u32[]{:S(2)}) %collective-permute-start.18) | collective-permute-done | bytes 131104 | tf_op jit(solution)/shard_map/ppermute | solution.py:453
  102.4 4.5 %collective-permute-done.16.rest_2_ = bf16[64,1024]{1,0:T(8,128)(2,1)S(1)} collective-permute-done((bf16[64,1024]{1,0:T(8,128)(2,1)S(1)}, bf16[64,1024]{1,0:T(8,128)(2,1)S(1)}, u32[]{:S(2)}, u32[]{:S(2)}) %collective-permute-start.16) | collective-permute-done | bytes 131104 | tf_op jit(solution)/shard_map/ppermute | solution.py:453
  106.9 2.1 %other_half.1 = f32[256,2048]{1,0:T(8,128)S(1)} custom-call(s32[3]{0:T(128)S(1)} %pad_add_fusion.meta, bf16[64,1024]{1,0:T(8,128)(2,1)S(1)} %get-tuple-element.28.rest_0_, bf16[64,1024]{1,0:T(8,128)(2,1)S(1)} %collective-permute-done.15.rest_1_, bf16[64,1024]{1,0:T(8,128)(2,1)S(1)} %collective-permute-done.16.rest_2_, ...), custom_call_target="tpu_custom_call" | custom-call | flops 1073741824 | bytes 4194304 | tf_op jit(solution)/shard_map/other_half/pallas_call | solution.py:417
  109.0 12.3 %collective-permute-start.22 = (f32[256,2048]{1,0:T(8,128)S(1)}, f32[256,2048]{1,0:T(8,128)S(1)}, u32[]{:S(2)}, u32[]{:S(2)}) collective-permute-start(f32[256,2048]{1,0:T(8,128)S(1)} %other_half.1), channel_id=1, source_target_pairs={{0,1},{1,0},{2,3},{3,2},{4,5},{5,4},{6,7},{7,6},{8,9},{9,8},{10,11... | collective-permute-start | bytes 6291464 | tf_op jit(solution)/shard_map/ppermute | solution.py:494
  121.3 2.1 %own_half.1.own = f32[256,2048]{1,0:T(8,128)S(1)} custom-call(s32[3]{0:T(128)S(1)} %pad_add_fusion.meta, bf16[64,1024]{1,0:T(8,128)(2,1)S(1)} %get-tuple-element.28.rest_0_, bf16[64,1024]{1,0:T(8,128)(2,1)S(1)} %collective-permute-done.15.rest_1_, bf16[64,1024]{1,0:T(8,128)(2,1)S(1)} %collective-permute-done.16.rest_2_, ...), custom_call_target="tpu_custom_call" | custom-call | flops 1073741824 | bytes 4194304 | tf_op jit(solution)/shard_map/own_half/pallas_call | solution.py:417
  123.4 1.7 %collective-permute-done.22.came = f32[256,2048]{1,0:T(8,128)S(1)} collective-permute-done((f32[256,2048]{1,0:T(8,128)S(1)}, f32[256,2048]{1,0:T(8,128)S(1)}, u32[]{:S(2)}, u32[]{:S(2)}) %collective-permute-start.22) | collective-permute-done | bytes 2097184 | tf_op jit(solution)/shard_map/ppermute | solution.py:494
  125.1 0.2 pair_sum.1
  125.3 1.4 collective-permute-start.23
  126.7 2.6 %collective-permute-start.24 = (bf16[64,2048]{1,0:T(8,128)(2,1)S(1)}, bf16[64,2048]{1,0:T(8,128)(2,1)S(1)}, u32[]{:S(2)}, u32[]{:S(2)}) collective-permute-start(bf16[64,2048]{1,0:T(8,128)(2,1)S(1)} %get-tuple-element.31), channel_id=1, source_target_pairs={{0,4},{1,5},{2,6},{3,7},{4,0},{5,1},{6,2},{7,3},{8,12},{9,13},{10,... | collective-permute-start | bytes 786440 | tf_op jit(solution)/shard_map/ppermute | solution.py:497
  129.3 1.1 collective-permute-start.25
  130.4 3.9 %collective-permute-done.23.b = bf16[64,2048]{1,0:T(8,128)(2,1)S(1)} collective-permute-done((bf16[64,2048]{1,0:T(8,128)(2,1)S(1)}, bf16[64,2048]{1,0:T(8,128)(2,1)S(1)}, u32[]{:S(2)}, u32[]{:S(2)}) %collective-permute-start.23) | collective-permute-done | bytes 262176 | tf_op jit(solution)/shard_map/ppermute | solution.py:497
  134.3 6.7 %collective-permute-done.24.c = bf16[64,2048]{1,0:T(8,128)(2,1)S(1)} collective-permute-done((bf16[64,2048]{1,0:T(8,128)(2,1)S(1)}, bf16[64,2048]{1,0:T(8,128)(2,1)S(1)}, u32[]{:S(2)}, u32[]{:S(2)}) %collective-permute-start.24) | collective-permute-done | bytes 262176 | tf_op jit(solution)/shard_map/ppermute | solution.py:497
  141.0 0.8 last_sum.1
  (19 shorter events, 0.1 us)
Async XLA Ops:
  0.6 4.7 %copy-start = (bf16[1,512,2048]{2,1,0:T(8,128)(2,1)S(1)}, bf16[1,512,2048]{2,1,0:T(8,128)(2,1)}, u32[]{:S(2)}) copy-start(bf16[1,512,2048]{2,1,0:T(8,128)(2,1)} %param.7) | copy-start | bytes 6291460
  0.6 53.3 %collective-permute-start.2 = (bf16[64,64,256]{2,1,0:T(8,128)(2,1)}, bf16[64,64,256]{2,1,0:T(8,128)(2,1)}, u32[]{:S(2)}, u32[]{:S(2)}) collective-permute-start(bf16[64,64,256]{2,1,0:T(8,128)(2,1)} %bitcast.22), channel_id=1, source_target_pairs={{0,96},{8,104},{16,112},{24,120},{32,64},{40,72},{48,80},{56,88},{... | collective-permute-start | bytes 6291464 | tf_op jit(solution)/shard_map/ppermute | solution.py:460
  12.1 31.9 %copy-start.4 = (s32[512]{0:T(512)S(1)}, s32[512]{0:T(512)}, u32[]{:S(2)}) copy-start(s32[512]{0:T(512)} %slots.1) | copy-start | bytes 6148
  33.5 6.5 %collective-permute-start.1 = (bf16[64,1024]{1,0:T(8,128)(2,1)S(1)}, bf16[64,1024]{1,0:T(8,128)(2,1)S(1)}, u32[]{:S(2)}, u32[]{:S(2)}) collective-permute-start(bf16[64,1024]{1,0:T(8,128)(2,1)S(1)} %slice.4), channel_id=1, source_target_pairs={{0,16},{8,24},{16,0},{24,8},{32,48},{40,56},{48,32},{56,40},{1,17}... | collective-permute-start | bytes 393224 | tf_op jit(solution)/shard_map/ppermute | solution.py:453
  34.5 6.9 %collective-permute-start = (bf16[64,1024]{1,0:T(8,128)(2,1)S(1)}, bf16[64,1024]{1,0:T(8,128)(2,1)S(1)}, u32[]{:S(2)}, u32[]{:S(2)}) collective-permute-start(bf16[64,1024]{1,0:T(8,128)(2,1)S(1)} %slice.4), channel_id=1, source_target_pairs={{0,48},{8,56},{16,32},{24,40},{32,16},{40,24},{48,0},{56,8},{1,49}... | collective-permute-start | bytes 393224 | tf_op jit(solution)/shard_map/ppermute | solution.py:453
  36.4 18.4 %collective-permute-start.7 = (bf16[64,1024]{1,0:T(8,128)(2,1)S(1)}, bf16[64,1024]{1,0:T(8,128)(2,1)S(1)}, u32[]{:S(2)}, u32[]{:S(2)}) collective-permute-start(bf16[64,1024]{1,0:T(8,128)(2,1)S(1)} %slice.4), channel_id=1, source_target_pairs={{0,40},{8,48},{16,56},{24,32},{32,8},{40,16},{48,24},{56,0},{1,41}... | collective-permute-start | bytes 393224 | tf_op jit(solution)/shard_map/ppermute | solution.py:453
  37.9 16.9 %collective-permute-start.6 = (bf16[64,1024]{1,0:T(8,128)(2,1)S(1)}, bf16[64,1024]{1,0:T(8,128)(2,1)S(1)}, u32[]{:S(2)}, u32[]{:S(2)}) collective-permute-start(bf16[64,1024]{1,0:T(8,128)(2,1)S(1)} %slice.4), channel_id=1, source_target_pairs={{0,56},{8,32},{16,40},{24,48},{32,24},{40,0},{48,8},{56,16},{1,57}... | collective-permute-start | bytes 393224 | tf_op jit(solution)/shard_map/ppermute | solution.py:453
  40.0 26.7 %collective-permute-start.5 = (bf16[64,1024]{1,0:T(8,128)(2,1)S(1)}, bf16[64,1024]{1,0:T(8,128)(2,1)S(1)}, u32[]{:S(2)}, u32[]{:S(2)}) collective-permute-start(bf16[64,1024]{1,0:T(8,128)(2,1)S(1)} %slice.4), channel_id=1, source_target_pairs={{0,8},{8,16},{16,24},{24,0},{32,40},{40,48},{48,56},{56,32},{1,9},... | collective-permute-start | bytes 393224 | tf_op jit(solution)/shard_map/ppermute | solution.py:453
  41.4 25.4 %collective-permute-start.4 = (bf16[64,1024]{1,0:T(8,128)(2,1)S(1)}, bf16[64,1024]{1,0:T(8,128)(2,1)S(1)}, u32[]{:S(2)}, u32[]{:S(2)}) collective-permute-start(bf16[64,1024]{1,0:T(8,128)(2,1)S(1)} %slice.4), channel_id=1, source_target_pairs={{0,24},{8,0},{16,8},{24,16},{32,56},{40,32},{48,40},{56,48},{1,25}... | collective-permute-start | bytes 393224 | tf_op jit(solution)/shard_map/ppermute | solution.py:453
  44.0 1.6 %copy-start.2 = (bf16[1,64,64,256]{3,2,1,0:T(8,128)(2,1)S(1)}, bf16[1,64,64,256]{3,2,1,0:T(8,128)(2,1)}, u32[]{:S(2)}) copy-start(bf16[1,64,64,256]{3,2,1,0:T(8,128)(2,1)} %param.11) | copy-start | bytes 6291460
  45.6 13.3 %copy-start.3 = (bf16[1,64,64,256]{3,2,1,0:T(8,128)(2,1)S(1)}, bf16[1,64,64,256]{3,2,1,0:T(8,128)(2,1)}, u32[]{:S(2)}) copy-start(bf16[1,64,64,256]{3,2,1,0:T(8,128)(2,1)} %param.11) | copy-start | bytes 6291460
  53.9 24.5 %collective-permute-start.3 = (bf16[64,1024]{1,0:T(8,128)(2,1)S(1)}, bf16[64,1024]{1,0:T(8,128)(2,1)S(1)}, u32[]{:S(2)}, u32[]{:S(2)}) collective-permute-start(bf16[64,1024]{1,0:T(8,128)(2,1)S(1)} %slice.4), channel_id=1, source_target_pairs={{0,32},{8,40},{16,48},{24,56},{32,0},{40,8},{48,16},{56,24},{1,33}... | collective-permute-start | bytes 393224 | tf_op jit(solution)/shard_map/ppermute | solution.py:453
  54.8 14.4 %collective-permute-start.9 = (bf16[64,2048]{1,0:T(8,128)(2,1)S(1)}, bf16[64,2048]{1,0:T(8,128)(2,1)S(1)}, u32[]{:S(2)}, u32[]{:S(2)}) collective-permute-start(bf16[64,2048]{1,0:T(8,128)(2,1)S(1)} %get-tuple-element.23), channel_id=1, source_target_pairs={{0,16},{8,24},{16,0},{24,8},{32,48},{40,56},{48,32},{56,40},{1,17}... | collective-permute-start | bytes 786440 | tf_op jit(solution)/shard_map/ppermute | solution.py:456
  54.9 14.3 %collective-permute-start.8 = (bf16[64,2048]{1,0:T(8,128)(2,1)S(1)}, bf16[64,2048]{1,0:T(8,128)(2,1)S(1)}, u32[]{:S(2)}, u32[]{:S(2)}) collective-permute-start(bf16[64,2048]{1,0:T(8,128)(2,1)S(1)} %get-tuple-element.21.rest_2_), channel_id=1, source_target_pairs={{0,48},{8,56},{16,32},{24,40},{32,16},{40,24},{48,0},{56,8},{1,49}... | collective-permute-start | bytes 786440 | tf_op jit(solution)/shard_map/ppermute | solution.py:456
  66.7 11.7 %collective-permute-start.11 = (bf16[64,2048]{1,0:T(8,128)(2,1)S(1)}, bf16[64,2048]{1,0:T(8,128)(2,1)S(1)}, u32[]{:S(2)}, u32[]{:S(2)}) collective-permute-start(bf16[64,2048]{1,0:T(8,128)(2,1)S(1)} %get-tuple-element.25), channel_id=1, source_target_pairs={{0,56},{8,32},{16,40},{24,48},{32,24},{40,0},{48,8},{56,16},{1,57}... | collective-permute-start | bytes 786440 | tf_op jit(solution)/shard_map/ppermute | solution.py:456
  66.8 11.6 %collective-permute-start.10 = (bf16[64,2048]{1,0:T(8,128)(2,1)S(1)}, bf16[64,2048]{1,0:T(8,128)(2,1)S(1)}, u32[]{:S(2)}, u32[]{:S(2)}) collective-permute-start(bf16[64,2048]{1,0:T(8,128)(2,1)S(1)} %get-tuple-element.22.rest_2_), channel_id=1, source_target_pairs={{0,40},{8,48},{16,56},{24,32},{32,8},{40,16},{48,24},{56,0},{1,41}... | collective-permute-start | bytes 786440 | tf_op jit(solution)/shard_map/ppermute | solution.py:456
  76.9 6.1 %collective-permute-start.13 = (bf16[64,2048]{1,0:T(8,128)(2,1)S(1)}, bf16[64,2048]{1,0:T(8,128)(2,1)S(1)}, u32[]{:S(2)}, u32[]{:S(2)}) collective-permute-start(bf16[64,2048]{1,0:T(8,128)(2,1)S(1)} %get-tuple-element.26), channel_id=1, source_target_pairs={{0,24},{8,0},{16,8},{24,16},{32,56},{40,32},{48,40},{56,48},{1,25}... | collective-permute-start | bytes 786440 | tf_op jit(solution)/shard_map/ppermute | solution.py:456
  78.4 6.4 %collective-permute-start.12 = (bf16[64,2048]{1,0:T(8,128)(2,1)S(1)}, bf16[64,2048]{1,0:T(8,128)(2,1)S(1)}, u32[]{:S(2)}, u32[]{:S(2)}) collective-permute-start(bf16[64,2048]{1,0:T(8,128)(2,1)S(1)} %get-tuple-element.24.rest_1_), channel_id=1, source_target_pairs={{0,8},{8,16},{16,24},{24,0},{32,40},{40,48},{48,56},{56,32},{1,9},... | collective-permute-start | bytes 786440 | tf_op jit(solution)/shard_map/ppermute | solution.py:456
  82.5 6.2 %copy-start.5 = (s32[64]{0:T(128)S(1)}, s32[64]{0:T(128)}, u32[]{:S(2)}) copy-start(s32[64]{0:T(128)} %lengths.1) | copy-start | bytes 772
  82.5 6.2 %collective-permute-start.14 = (bf16[64,2048]{1,0:T(8,128)(2,1)S(1)}, bf16[64,2048]{1,0:T(8,128)(2,1)S(1)}, u32[]{:S(2)}, u32[]{:S(2)}) collective-permute-start(bf16[64,2048]{1,0:T(8,128)(2,1)S(1)} %attend_1.1.rest_0_), channel_id=1, source_target_pairs={{0,32},{8,40},{16,48},{24,56},{32,0},{40,8},{48,16},{56,24},{1,33}... | collective-permute-start | bytes 786440 | tf_op jit(solution)/shard_map/ppermute | solution.py:456
  88.8 18.2 %copy-start.1 = (bf16[1024,2048]{1,0:T(8,128)(2,1)S(1)}, bf16[1024,2048]{1,0:T(8,128)(2,1)}, u32[]{:S(2)}) copy-start(bf16[1024,2048]{1,0:T(8,128)(2,1)} %rest_8_.3) | copy-start | bytes 12582916
  90.2 8.7 %collective-permute-start.21 = (bf16[64,1024]{1,0:T(8,128)(2,1)S(1)}, bf16[64,1024]{1,0:T(8,128)(2,1)S(1)}, u32[]{:S(2)}, u32[]{:S(2)}) collective-permute-start(bf16[64,1024]{1,0:T(8,128)(2,1)S(1)} %get-tuple-element.28.rest_0_), channel_id=1, source_target_pairs={{0,48},{8,56},{16,32},{24,40},{32,16},{40,24},{48,0},{56,8},{1,49}... | collective-permute-start | bytes 393224 | tf_op jit(solution)/shard_map/ppermute | solution.py:453
  91.0 8.0 %collective-permute-start.20 = (bf16[64,1024]{1,0:T(8,128)(2,1)S(1)}, bf16[64,1024]{1,0:T(8,128)(2,1)S(1)}, u32[]{:S(2)}, u32[]{:S(2)}) collective-permute-start(bf16[64,1024]{1,0:T(8,128)(2,1)S(1)} %get-tuple-element.28.rest_0_), channel_id=1, source_target_pairs={{0,16},{8,24},{16,0},{24,8},{32,48},{40,56},{48,32},{56,40},{1,17}... | collective-permute-start | bytes 393224 | tf_op jit(solution)/shard_map/ppermute | solution.py:453
  93.3 7.0 %collective-permute-start.19 = (bf16[64,1024]{1,0:T(8,128)(2,1)S(1)}, bf16[64,1024]{1,0:T(8,128)(2,1)S(1)}, u32[]{:S(2)}, u32[]{:S(2)}) collective-permute-start(bf16[64,1024]{1,0:T(8,128)(2,1)S(1)} %get-tuple-element.28.rest_0_), channel_id=1, source_target_pairs={{0,56},{8,32},{16,40},{24,48},{32,24},{40,0},{48,8},{56,16},{1,57}... | collective-permute-start | bytes 393224 | tf_op jit(solution)/shard_map/ppermute | solution.py:453
  96.4 6.0 %collective-permute-start.18 = (bf16[64,1024]{1,0:T(8,128)(2,1)S(1)}, bf16[64,1024]{1,0:T(8,128)(2,1)S(1)}, u32[]{:S(2)}, u32[]{:S(2)}) collective-permute-start(bf16[64,1024]{1,0:T(8,128)(2,1)S(1)} %get-tuple-element.28.rest_0_), channel_id=1, source_target_pairs={{0,40},{8,48},{16,56},{24,32},{32,8},{40,16},{48,24},{56,0},{1,41}... | collective-permute-start | bytes 393224 | tf_op jit(solution)/shard_map/ppermute | solution.py:453
  96.4 6.0 %collective-permute-start.17 = (bf16[64,1024]{1,0:T(8,128)(2,1)S(1)}, bf16[64,1024]{1,0:T(8,128)(2,1)S(1)}, u32[]{:S(2)}, u32[]{:S(2)}) collective-permute-start(bf16[64,1024]{1,0:T(8,128)(2,1)S(1)} %get-tuple-element.28.rest_0_), channel_id=1, source_target_pairs={{0,24},{8,0},{16,8},{24,16},{32,56},{40,32},{48,40},{56,48},{1,25}... | collective-permute-start | bytes 393224 | tf_op jit(solution)/shard_map/ppermute | solution.py:453
  98.9 8.0 %collective-permute-start.16 = (bf16[64,1024]{1,0:T(8,128)(2,1)S(1)}, bf16[64,1024]{1,0:T(8,128)(2,1)S(1)}, u32[]{:S(2)}, u32[]{:S(2)}) collective-permute-start(bf16[64,1024]{1,0:T(8,128)(2,1)S(1)} %get-tuple-element.28.rest_0_), channel_id=1, source_target_pairs={{0,8},{8,16},{16,24},{24,0},{32,40},{40,48},{48,56},{56,32},{1,9},... | collective-permute-start | bytes 393224 | tf_op jit(solution)/shard_map/ppermute | solution.py:453
  99.0 8.0 %collective-permute-start.15 = (bf16[64,1024]{1,0:T(8,128)(2,1)S(1)}, bf16[64,1024]{1,0:T(8,128)(2,1)S(1)}, u32[]{:S(2)}, u32[]{:S(2)}) collective-permute-start(bf16[64,1024]{1,0:T(8,128)(2,1)S(1)} %get-tuple-element.28.rest_0_), channel_id=1, source_target_pairs={{0,32},{8,40},{16,48},{24,56},{32,0},{40,8},{48,16},{56,24},{1,33}... | collective-permute-start | bytes 393224 | tf_op jit(solution)/shard_map/ppermute | solution.py:453
  109.0 16.1 %collective-permute-start.22 = (f32[256,2048]{1,0:T(8,128)S(1)}, f32[256,2048]{1,0:T(8,128)S(1)}, u32[]{:S(2)}, u32[]{:S(2)}) collective-permute-start(f32[256,2048]{1,0:T(8,128)S(1)} %other_half.1), channel_id=1, source_target_pairs={{0,1},{1,0},{2,3},{3,2},{4,5},{5,4},{6,7},{7,6},{8,9},{9,8},{10,11... | collective-permute-start | bytes 6291464 | tf_op jit(solution)/shard_map/ppermute | solution.py:494
  125.3 9.0 %collective-permute-start.23 = (bf16[64,2048]{1,0:T(8,128)(2,1)S(1)}, bf16[64,2048]{1,0:T(8,128)(2,1)S(1)}, u32[]{:S(2)}, u32[]{:S(2)}) collective-permute-start(bf16[64,2048]{1,0:T(8,128)(2,1)S(1)} %get-tuple-element.30), channel_id=1, source_target_pairs={{0,2},{1,3},{2,4},{3,5},{4,6},{5,7},{6,0},{7,1},{8,10},{9,11},{10,... | collective-permute-start | bytes 786440 | tf_op jit(solution)/shard_map/ppermute | solution.py:497
  126.7 14.3 %collective-permute-start.24 = (bf16[64,2048]{1,0:T(8,128)(2,1)S(1)}, bf16[64,2048]{1,0:T(8,128)(2,1)S(1)}, u32[]{:S(2)}, u32[]{:S(2)}) collective-permute-start(bf16[64,2048]{1,0:T(8,128)(2,1)S(1)} %get-tuple-element.31), channel_id=1, source_target_pairs={{0,4},{1,5},{2,6},{3,7},{4,0},{5,1},{6,2},{7,3},{8,12},{9,13},{10,... | collective-permute-start | bytes 786440 | tf_op jit(solution)/shard_map/ppermute | solution.py:497
  129.3 11.7 %collective-permute-start.25 = (bf16[64,2048]{1,0:T(8,128)(2,1)S(1)}, bf16[64,2048]{1,0:T(8,128)(2,1)S(1)}, u32[]{:S(2)}, u32[]{:S(2)}) collective-permute-start(bf16[64,2048]{1,0:T(8,128)(2,1)S(1)} %get-tuple-element.32), channel_id=1, source_target_pairs={{0,6},{1,7},{2,0},{3,1},{4,2},{5,3},{6,4},{7,5},{8,14},{9,15},{10,... | collective-permute-start | bytes 786440 | tf_op jit(solution)/shard_map/ppermute | solution.py:497
